TPU v7x, 32 devices: a whole 2x2x4 slice. The times are simulated.
32 devices in a mesh: sx: 4 (over z), sy: 4 (over y, x), rep: 2 (over core).
Axes of the slice: x: 2, y: 2, z: 4, core: 2. Of those that a mesh axis runs over, the one named last changes fastest.
Arguments:
- volume: bfloat16 [2, 32, 8, 64, 256], P('rep', None, 'sx', 'sy'), may hold values from -6 to 6
- first_kernel: bfloat16 [64, 32, 3, 3, 3], replicated, may hold values from -0.21875 to 0.21875
- first_bias: float32 [64], replicated, may hold values from -3 to 3
- second_kernel: bfloat16 [128, 64, 3, 3, 3], P('sy'), may hold values from -0.15625 to 0.15625
- second_bias: float32 [128], P('sy'), may hold values from -3 to 3
- cotangent: bfloat16 [2, 128, 4, 32, 128], P('rep', 'sy', 'sx'), may hold values from -6 to 6
Outputs:
- second_out: float32 [2, 128, 4, 32, 128], P('rep', 'sy', 'sx')
- grad_first_kernel: float32 [64, 32, 3, 3, 3], replicated
- grad_first_bias: float32 [64], replicated
- grad_second_kernel: float32 [128, 64, 3, 3, 3], P('sy')
- grad_second_bias: float32 [128], P('sy')
All inputs are finite; a program needn't handle non-finite values.
Results may differ from a plain program's by a relative error of at most 0.0045.
Values may be sent and summed in bfloat16 or wider, within the bound.
No kernel may reach another device: no remote copies, remote signals or barrier semaphores. Data moves between devices by JAX's collectives and lax.ppermute only.
A program may use at most 128 MiB of HBM per device.

v0:
```python
import math

import jax
import jax.numpy as jnp
from jax import lax
from jax.sharding import PartitionSpec as P


def padded_2(cells, sides, width):
    for axis, dim in sides:
        count = lax.axis_size(axis)
        ends = count - 1
        head = lax.slice_in_dim(cells, 0, width, axis=dim)
        tail = lax.slice_in_dim(cells, cells.shape[dim] - width, cells.shape[dim], axis=dim)
        cells = jnp.concatenate(
            [
                lax.ppermute(tail, axis, [(i, (i + 1) % count) for i in range(ends)]),
                cells,
                lax.ppermute(head, axis, [((i + 1) % count, i) for i in range(ends)]),
            ],
            axis=dim,
        )
    return cells


def convolve(padded, kernel, z_pad):
    return lax.conv_general_dilated(
        padded[None],
        kernel,
        (1, 1, 1),
        ((0, 0), (0, 0), (z_pad, z_pad)),
        dimension_numbers=("NCDHW", "OIDHW", "NCDHW"),
        preferred_element_type=jnp.float32,
    )[0]


def weight_terms(cotan, padded):
    cells_x, cells_y, cells_z = (cotan.shape[1], cotan.shape[2], cotan.shape[3])
    terms = []
    for i in range(3):
        for j in range(3):
            for k in range(3):
                piece = padded[:, i : i + cells_x, j : j + cells_y, k : k + cells_z]
                terms.append(
                    jnp.einsum("oxyz,cxyz->oc", cotan, piece, preferred_element_type=jnp.float32)
                )
    stacked = jnp.stack(terms).reshape(3, 3, 3, cotan.shape[0], padded.shape[0])
    return stacked.transpose(3, 4, 0, 1, 2)


def pool_mean(field):
    chans, cells_x, cells_y, cells_z = field.shape
    blocks = field.astype(jnp.float32).reshape(
        chans, cells_x // 2, 2, cells_y // 2, 2, cells_z // 2, 2
    )
    return jnp.mean(blocks, axis=(2, 4, 6))


def per_device(volume, first_kernel, first_bias, second_kernel, second_bias, cotangent):
    source = volume[0]
    cotan = cotangent[0]
    half_x, half_y, half_z = (source.shape[1] // 2, source.shape[2] // 2, source.shape[3] // 2)
    count = (
        lax.axis_size("rep") * lax.axis_size("sx") * lax.axis_size("sy") * half_x * half_y * half_z
    )
    scale = 1.0 / math.sqrt(count)
    rimmed = padded_2(source, (("sx", 1), ("sy", 2)), 1)
    input_pad = jnp.pad(rimmed, ((0, 0), (0, 0), (0, 0), (1, 1)))
    pre = convolve(input_pad, first_kernel, 0) + first_bias[:, None, None, None]
    act = jnp.where(pre > 0, pre, 0.3 * pre)
    pooled = pool_mean(act).astype(jnp.bfloat16)
    pooled_x = padded_2(pooled, (("sx", 1),), 1)
    gathered = lax.all_gather(pooled_x, "sy", axis=2, tiled=True)
    pooled_pad = jnp.pad(gathered, ((0, 0), (0, 0), (1, 1), (1, 1)))
    second = convolve(pooled_pad, second_kernel, 0) + second_bias[:, None, None, None]
    second_out = second.astype(jnp.float32)
    local_w2 = weight_terms(cotan, pooled_pad)
    local_b2 = jnp.sum(cotan.astype(jnp.float32), axis=(1, 2, 3))
    cot_x = padded_2(cotan, (("sx", 1),), 1)
    cot_pad = jnp.pad(cot_x, ((0, 0), (0, 0), (1, 1), (1, 1)))
    flipped = second_kernel.transpose(1, 0, 2, 3, 4)[:, :, ::-1, ::-1, ::-1]
    partial_back = convolve(cot_pad, flipped, 0)
    back = lax.psum_scatter(partial_back, "sy", scatter_dimension=2, tiled=True)
    summed_w2, summed_b2 = lax.psum((local_w2, local_b2), ("sx", "rep"))
    spread = jnp.repeat(jnp.repeat(jnp.repeat(back, 2, axis=1), 2, axis=2), 2, axis=3)
    grad_pre = (spread * 0.125 * jnp.where(pre > 0, 1.0, 0.3)).astype(jnp.bfloat16)
    local_w1 = weight_terms(grad_pre, input_pad)
    local_b1 = jnp.sum(grad_pre.astype(jnp.float32), axis=(1, 2, 3))
    summed_w1, summed_b1 = lax.psum((local_w1, local_b1), ("sx", "sy", "rep"))
    return (
        second_out[None],
        scale * summed_w1,
        scale * summed_b1,
        scale * summed_w2,
        scale * summed_b2,
    )


def solution(mesh):
    placed = (
        P("rep", None, "sx", "sy", None),
        P(),
        P(),
        P("sy", None, None, None, None),
        P("sy"),
        P("rep", "sy", "sx", None, None),
    )
    return jax.shard_map(
        per_device,
        mesh=mesh,
        in_specs=placed,
        out_specs=(
            P("rep", "sy", "sx", None, None),
            P(),
            P(),
            P("sy", None, None, None, None),
            P("sy"),
        ),
        check_vma=False,
    )
```

profile of v0, /device:TPU:0, one launch (start us, length us, event | category | flops | bytes accessed | tf_op | source)
XLA Modules:
  0.0 405.9 jit_solution(17643233514923021415)
XLA Ops:
  7.2 1.4 copy.462
  8.7 4.9 %collective-permute-start = (bf16[32,1,16,256]{3,0,2,1:T(8,128)(2,1)S(1)}, bf16[32,1,16,256]{3,0,2,1:T(8,128)(2,1)S(1)}, u32[]{:S(2)}, u32[]{:S(2)}) collective-permute-start(bf16[32,1,16,256]{3,0,2,1:T(8,128)(2,1)S(1)} %get-tuple-element.33), channel_id=1, source_target_pairs={{0,8},{8,16},{16,24},{1,9},{9,17},{17,25},{2,10},{10,18},{18,26},{... | collective-permute-start | bytes 786440 | tf_op jit(solution)/shard_map/ppermute | solution.py:17
  13.6 1.3 collective-permute-start.1
  14.9 4.6 %collective-permute-start.6 = (bf16[32,1,32,128]{3,2,1,0:T(8,128)(2,1)S(1)}, bf16[32,1,32,128]{3,2,1,0:T(8,128)(2,1)S(1)}, u32[]{:S(2)}, u32[]{:S(2)}) collective-permute-start(bf16[32,1,32,128]{3,2,1,0:T(8,128)(2,1)S(1)} %bitcast.598), channel_id=1, source_target_pairs={{0,8},{8,16},{16,24},{1,9},{9,17},{17,25},{2,10},{10,18},{18,26},{... | collective-permute-start | bytes 786440 | tf_op jit(solution)/shard_map/ppermute | solution.py:17
  19.5 1.3 collective-permute-start.7
  20.8 2.7 collective-permute-done.1
  23.5 3.4 collective-permute-start.2
  27.0 1.3 collective-permute-start.3
  29.0 5.0 %copy.256 = bf16[32,3,32,128]{2,0,3,1:T(8,128)(2,1)} copy(bf16[32,3,32,128]{3,2,1,0:T(8,128)(2,1)S(1)} %pad_maximum_fusion.1) | data formatting | bytes 1572864 | tf_op jit(solution)/shard_map/concatenate | solution.py:15
  34.0 2.9 pad_bitcast_fusion.1
  36.9 2.4 pad.19
  39.3 6.9 %copy.258 = bf16[32,3,34,1,8,17]{0,4,5,2,1,3:T(8,128)(2,1)} copy(bf16[32,3,34,1,8,17]{2,0,5,4,1,3:T(8,128)(2,1)} %bitcast.643) | data formatting | bytes 1775616 | tf_op jit(solution)/shard_map/conv_general_dilated | solution.py:27
  47.3 6.0 %fusion.40 = f32[1,32,8,17,64]{4,2,3,1,0:T(8,128)S(1)} fusion(bf16[32,64,3,3,3]{1,0,4,3,2:T(8,128)(2,1)S(1)} %copy-done.14, bf16[32,3,34,1,7,2]{0,4,5,2,1,3:T(8,128)(2,1)S(1)} %slice.266, bf16[32,3,34,1,8,17]{0,4,5,2,1,3:T(8,128)(2,1)} %copy.258, pred[8,17]{0,1:T(8,128)(4,1)S(1)} %copy-done.18), kind=kOutput, calls=%fused_computation.79 | convolution fusion | flops 484551680 | bytes 2204040 | tf_op jit(solution)/shard_map/conv_general_dilated | solution.py:27
  53.7 1.5 slice_bitcast_fusion.1
  55.3 1.7 fusion.272
  57.2 5.4 %reshape.246 = bf16[32,4,18,1,8,33]{5,4,0,2,1,3:T(8,128)(2,1)} reshape(bf16[32,4,18,1,264]{4,0,2,1,3:T(8,128)(2,1)S(1)} %pad.15) | data formatting | bytes 2433024 | tf_op jit(solution)/shard_map/conv_general_dilated | solution.py:27
  62.6 19.7 %copy.249 = bf16[32,4,18,1,8,33]{0,4,5,2,1,3:T(8,128)(2,1)} copy(bf16[32,4,18,1,8,33]{5,4,0,2,1,3:T(8,128)(2,1)} %reshape.246) | data formatting | bytes 2433024 | tf_op jit(solution)/shard_map/conv_general_dilated | solution.py:27
  83.4 12.3 %compare_select_fusion = (f32[2,16,8,33,64]{4,2,3,1,0:T(8,128)}, f32[2,16,8,33,64]{4,2,3,1,0:T(8,128)S(1)}, f32[2,16,8,33,64]{4,2,3,1,0:T(8,128)}) fusion(f32[64]{0:T(128)S(1)} %copy-done.13, bf16[64,32,3,3,3]{0,1,4,3,2:T(8,128)(2,1)S(1)} %copy-done, bf16[32,4,18,1,7,2]{0,4,5,2,1,3:T(8,128)(2,1)S(1)} %slice.262, bf16[32,4,18,1,8,33]{0,4,5,2,1,3:T(8,128)(2,1)} %copy.249, ...), kind=kOutput, calls=%fused_computation.32 | convolution fusion | flops 941395968 | bytes 7880200 | tf_op jit(solution)/shard_map/conv_general_dilated | solution.py:27
  96.9 3.3 reduce_sum.36
  101.4 4.2 %collective-permute-start.4 = (bf16[64,1,8,128]{3,0,2,1:T(8,128)(2,1)S(1)}, bf16[64,1,8,128]{3,0,2,1:T(8,128)(2,1)}, u32[]{:S(2)}, u32[]{:S(2)}) collective-permute-start(bf16[64,1,8,128]{3,0,2,1:T(8,128)(2,1)S(1)} %fusion.178), channel_id=1, source_target_pairs={{0,8},{8,16},{16,24},{1,9},{9,17},{17,25},{2,10},{10,18},{18,26},{... | collective-permute-start | bytes 393224 | tf_op jit(solution)/shard_map/ppermute | solution.py:17
  105.6 1.3 collective-permute-start.5
  106.9 3.1 copy.261
  110.0 2.2 slice.268
  112.2 5.1 %copy.346 = f32[2,16,1,256,64]{3,1,0,4,2:T(8,128)} copy(f32[2,16,1,256,64]{4,1,3,0,2:T(8,128)} %slice.268) | data formatting | bytes 4194304
  117.3 5.1 %copy.276 = f32[2,16,8,33,64]{4,1,3,2,0:T(8,128)} copy(f32[2,16,8,33,64]{4,2,3,1,0:T(8,128)} %get-tuple-element.27) | data formatting | bytes 4325376 | tf_op jit(solution)/shard_map/jit(_where)/select_n | solution.py:86
  122.4 1.6 pad_maximum_fusion
  124.0 3.0 select_maximum_fusion
  128.7 2.3 copy.260
  131.0 2.4 multiply_convert_fusion
  135.9 1.3 fusion.68
  137.2 1.2 fusion.67
  138.5 1.3 fusion.66
  139.8 1.3 fusion.65
  143.5 1.5 fusion.62
  146.3 1.2 fusion.60
  147.5 1.3 fusion.59
  148.8 1.2 fusion.58
  152.1 1.3 fusion.57
  153.4 1.2 fusion.56
  154.6 1.2 fusion.55
  155.9 1.5 fusion.54
  157.4 1.2 fusion.53
  158.6 1.2 fusion.52
  159.9 1.3 fusion.51
  161.2 1.2 fusion.50
  162.4 1.3 fusion.49
  163.7 1.3 fusion.48
  165.0 1.2 fusion.47
  166.2 1.2 fusion.46
  167.5 1.3 fusion.45
  169.7 1.8 pad_maximum_fusion.6
  171.8 14.5 %psum.31 = f32[32]{0:T(128)S(1)} all-reduce(f32[32]{0:T(128)S(1)} %convert_reduce_fusion.1), channel_id=1, replica_groups=mesh['sx'=4,'sy'=4,'rep'=2] {'sx','rep'}, use_global_device_ids=true, to_apply=%region_8.9 | all-reduce | flops 32 | bytes 256 | tf_op jit(solution)/shard_map/psum | solution.py:84
  186.9 38.5 %psum.29 = f32[64]{0:T(128)S(1)} all-reduce(f32[64]{0:T(128)S(1)} %get-tuple-element.25), channel_id=1, replica_groups=mesh['sx'=4,'sy'=4,'rep'=2] {'sx','sy','rep'}, use_global_device_ids=true, to_apply=%region_5.6 | all-reduce | flops 64 | bytes 512 | tf_op jit(solution)/shard_map/psum | solution.py:89
  225.9 70.9 %all-reduce.6.cloned.1.call-done = f32[64,32,3,3,3]{0,1,4,3,2:T(8,128)} async-done(((f32[64,32,3,3,3]{0,1,4,3,2:T(8,128)}), f32[64,32,3,3,3]{0,1,4,3,2:T(8,128)}) %all-reduce.6.cloned.1.call-update) | async-done | bytes 221200 | tf_op jit(solution)/shard_map/psum | solution.py:89
  296.8 1.8 broadcast_multiply_fusion.1
  298.6 32.6 %all-gather.2.cloned.1.call-done = bf16[64,3,32,128]{3,0,2,1:T(8,128)(2,1)} async-done(((bf16[64,3,8,128]{3,0,2,1:T(8,128)(2,1)}), bf16[64,3,32,128]{3,0,2,1:T(8,128)(2,1)}) %all-gather.2.cloned.1.call-update) | async-done | bytes 1572880 | tf_op jit(solution)/shard_map/all_gather | solution.py:73
  331.2 1.5 fusion.97
  342.1 2.9 pad_bitcast_fusion
  345.0 8.6 %copy.347 = bf16[64,3,34,1,130]{0,2,4,1,3:T(8,128)(2,1)} copy(bf16[64,3,34,1,130]{4,0,2,1,3:T(8,128)(2,1)} %pad_bitcast_fusion) | data formatting | bytes 3394560
  353.6 3.0 pad.17.clone
  357.6 8.6 %select_add_fusion = f32[1,32,8,17,32]{4,2,3,1,0:T(8,128)S(1)} fusion(bf16[32,64,3,3,3]{1,0,4,3,2:T(8,128)(2,1)S(1)} %copy-done.15, bf16[64,3,34,1,7,2]{0,4,5,2,1,3:T(8,128)(2,1)S(1)} %slice.264, bf16[64,3,34,1,8,17]{0,4,5,2,1,3:T(8,128)(2,1)S(1)} %copy.254, f32[32]{0:T(128)S(1)} %copy-done.16, pred[8,17]{0,1:T(8,128)(4,1)S(1)} %copy-done.18), kind=kOutput, calls=%fused_computation.61 | convolution fusion | flops 487528448 | bytes 2626312 | tf_op jit(solution)/shard_map/conv_general_dilated | solution.py:27
  366.8 2.2 copy.318
  369.0 28.3 %all-reduce.8.cloned.1.call-done = f32[32,64,3,3,3]{1,0,4,3,2:T(8,128)} async-done(((f32[32,64,3,3,3]{1,0,4,3,2:T(8,128)}), f32[32,64,3,3,3]{1,0,4,3,2:T(8,128)}) %all-reduce.8.cloned.1.call-update) | async-done | bytes 221200 | tf_op jit(solution)/shard_map/psum | solution.py:84
  397.3 1.8 broadcast_multiply_fusion
  (113 shorter events, 29.2 us)
Async XLA Ops:
  7.2 76.2 %copy-start = (bf16[64,32,3,3,3]{0,1,4,3,2:T(8,128)(2,1)S(1)}, bf16[64,32,3,3,3]{0,1,4,3,2:T(8,128)(2,1)}, u32[]{:S(2)}) copy-start(bf16[64,32,3,3,3]{0,1,4,3,2:T(8,128)(2,1)} %param.7) | copy-start | bytes 331780
  7.2 7.8 %copy-start.3 = (bf16[1,32,1,32,128]{4,3,2,1,0:T(8,128)(2,1)S(1)}, bf16[1,32,1,32,128]{4,3,2,1,0:T(8,128)(2,1)}, u32[]{:S(2)}) copy-start(bf16[1,32,1,32,128]{4,3,2,1,0:T(8,128)(2,1)} %param.11) | copy-start | bytes 786436
  7.2 119.9 %reduce-scatter.2.cloned.1.call-start = ((), (), s32[]{:S(2)}) async-start(), calls=%async_computation.2 | async-start | bytes 2621440 | tf_op jit(solution)/shard_map/reduce_scatter | solution.py:83
  8.7 12.1 %collective-permute-start = (bf16[32,1,16,256]{3,0,2,1:T(8,128)(2,1)S(1)}, bf16[32,1,16,256]{3,0,2,1:T(8,128)(2,1)S(1)}, u32[]{:S(2)}, u32[]{:S(2)}) collective-permute-start(bf16[32,1,16,256]{3,0,2,1:T(8,128)(2,1)S(1)} %get-tuple-element.33), channel_id=1, source_target_pairs={{0,8},{8,16},{16,24},{1,9},{9,17},{17,25},{2,10},{10,18},{18,26},{... | collective-permute-start | bytes 786440 | tf_op jit(solution)/shard_map/ppermute | solution.py:17
  13.6 9.9 %collective-permute-start.1 = (bf16[32,1,16,256]{3,0,2,1:T(8,128)(2,1)S(1)}, bf16[32,1,16,256]{3,0,2,1:T(8,128)(2,1)S(1)}, u32[]{:S(2)}, u32[]{:S(2)}) collective-permute-start(bf16[32,1,16,256]{3,0,2,1:T(8,128)(2,1)S(1)} %get-tuple-element.34), channel_id=1, source_target_pairs={{8,0},{16,8},{24,16},{9,1},{17,9},{25,17},{10,2},{18,10},{26,18},{... | collective-permute-start | bytes 786440 | tf_op jit(solution)/shard_map/ppermute | solution.py:19
  14.9 13.3 %collective-permute-start.6 = (bf16[32,1,32,128]{3,2,1,0:T(8,128)(2,1)S(1)}, bf16[32,1,32,128]{3,2,1,0:T(8,128)(2,1)S(1)}, u32[]{:S(2)}, u32[]{:S(2)}) collective-permute-start(bf16[32,1,32,128]{3,2,1,0:T(8,128)(2,1)S(1)} %bitcast.598), channel_id=1, source_target_pairs={{0,8},{8,16},{16,24},{1,9},{9,17},{17,25},{2,10},{10,18},{18,26},{... | collective-permute-start | bytes 786440 | tf_op jit(solution)/shard_map/ppermute | solution.py:17
  19.5 9.4 %collective-permute-start.7 = (bf16[32,1,32,128]{3,2,1,0:T(8,128)(2,1)S(1)}, bf16[32,1,32,128]{3,2,1,0:T(8,128)(2,1)S(1)}, u32[]{:S(2)}, u32[]{:S(2)}) collective-permute-start(bf16[32,1,32,128]{3,2,1,0:T(8,128)(2,1)S(1)} %bitcast.599), channel_id=1, source_target_pairs={{8,0},{16,8},{24,16},{9,1},{17,9},{25,17},{10,2},{18,10},{26,18},{... | collective-permute-start | bytes 786440 | tf_op jit(solution)/shard_map/ppermute | solution.py:19
  20.8 34.5 %copy-start.4 = (bf16[32,1,16,256]{3,0,2,1:T(8,128)(2,1)}, bf16[32,1,16,256]{3,0,2,1:T(8,128)(2,1)S(1)}, u32[]{:S(2)}) copy-start(bf16[32,1,16,256]{3,0,2,1:T(8,128)(2,1)S(1)} %collective-permute-done) | copy-start | bytes 786436
  23.5 31.7 %collective-permute-start.2 = (bf16[32,4,1,256]{3,0,2,1:T(8,128)(2,1)S(1)}, bf16[32,4,1,256]{3,0,2,1:T(8,128)(2,1)S(1)}, u32[]{:S(2)}, u32[]{:S(2)}) collective-permute-start(bf16[32,4,1,256]{3,0,2,1:T(8,128)(2,1)S(1)} %get-tuple-element.31), channel_id=1, source_target_pairs={{0,2},{2,4},{4,6},{1,3},{3,5},{5,7},{8,10},{10,12},{12,14},{9,11},... | collective-permute-start | bytes 196616 | tf_op jit(solution)/shard_map/ppermute | solution.py:17
  27.0 28.3 %collective-permute-start.3 = (bf16[32,4,1,256]{3,0,2,1:T(8,128)(2,1)S(1)}, bf16[32,4,1,256]{3,0,2,1:T(8,128)(2,1)S(1)}, u32[]{:S(2)}, u32[]{:S(2)}) collective-permute-start(bf16[32,4,1,256]{3,0,2,1:T(8,128)(2,1)S(1)} %get-tuple-element.32), channel_id=1, source_target_pairs={{2,0},{4,2},{6,4},{3,1},{5,3},{7,5},{10,8},{12,10},{14,12},{11,9},... | collective-permute-start | bytes 196616 | tf_op jit(solution)/shard_map/ppermute | solution.py:19
  39.3 8.0 %copy-start.14 = (bf16[32,64,3,3,3]{1,0,4,3,2:T(8,128)(2,1)S(1)}, bf16[32,64,3,3,3]{1,0,4,3,2:T(8,128)(2,1)}, u32[]{:S(2)}) copy-start(bf16[32,64,3,3,3]{1,0,4,3,2:T(8,128)(2,1)} %param.9) | copy-start | bytes 331780
  39.3 8.0 %copy-start.18 = (pred[8,17]{0,1:T(8,128)(4,1)S(1)}, pred[8,17]{0,1:T(8,128)(4,1)}, u32[]{:S(2)}) copy-start(pred[8,17]{0,1:T(8,128)(4,1)} %constant.40) | copy-start | bytes 412
  55.2 241.6 %all-reduce.6.cloned.1.call-start = ((), (), s32[]{:S(2)}) async-start(), calls=%async_computation.3 | async-start | bytes 884736 | tf_op jit(solution)/shard_map/psum | solution.py:89
  62.6 20.8 %copy-start.13 = (f32[64]{0:T(128)S(1)}, f32[64]{0:T(128)}, u32[]{:S(2)}) copy-start(f32[64]{0:T(128)} %param.8) | copy-start | bytes 772
  62.6 20.8 %copy-start.17 = (pred[8,33]{0,1:T(8,128)(4,1)S(1)}, pred[8,33]{0,1:T(8,128)(4,1)}, u32[]{:S(2)}) copy-start(pred[8,33]{0,1:T(8,128)(4,1)} %constant.41) | copy-start | bytes 796
  101.4 68.2 %collective-permute-start.4 = (bf16[64,1,8,128]{3,0,2,1:T(8,128)(2,1)S(1)}, bf16[64,1,8,128]{3,0,2,1:T(8,128)(2,1)}, u32[]{:S(2)}, u32[]{:S(2)}) collective-permute-start(bf16[64,1,8,128]{3,0,2,1:T(8,128)(2,1)S(1)} %fusion.178), channel_id=1, source_target_pairs={{0,8},{8,16},{16,24},{1,9},{9,17},{17,25},{2,10},{10,18},{18,26},{... | collective-permute-start | bytes 393224 | tf_op jit(solution)/shard_map/ppermute | solution.py:17
  105.6 64.0 %collective-permute-start.5 = (bf16[64,1,8,128]{3,0,2,1:T(8,128)(2,1)S(1)}, bf16[64,1,8,128]{3,0,2,1:T(8,128)(2,1)}, u32[]{:S(2)}, u32[]{:S(2)}) collective-permute-start(bf16[64,1,8,128]{3,0,2,1:T(8,128)(2,1)S(1)} %fusion.178), channel_id=1, source_target_pairs={{8,0},{16,8},{24,16},{9,1},{17,9},{25,17},{10,2},{18,10},{26,18},{... | collective-permute-start | bytes 393224 | tf_op jit(solution)/shard_map/ppermute | solution.py:19
  117.3 5.1 %copy-start.5 = (bf16[32,1,16,256]{3,0,2,1:T(8,128)(2,1)S(1)}, bf16[32,1,16,256]{3,0,2,1:T(8,128)(2,1)}, u32[]{:S(2)}) copy-start(bf16[32,1,16,256]{3,0,2,1:T(8,128)(2,1)} %copy-done.4) | copy-start | bytes 786436
  131.0 2.4 copy-start.7
  131.0 3.7 copy-start.9
  135.9 2.6 copy-start.6
  139.7 2.6 copy-start.8
  141.0 9.0 %slice-start = ((s8[4325376]{0:T(1024)(128)(4,1)}), s8[4194304]{0:T(1024)(128)(4,1)S(1)}, s32[]{:S(2)}) async-start(s8[4325376]{0:T(1024)(128)(4,1)} %bitcast.638), calls=%async_computation.5 | async-start | bytes 8388608
  145.0 5.1 %slice-start.1 = ((s8[4325376]{0:T(1024)(128)(4,1)}), s8[131072]{0:T(1024)(128)(4,1)S(1)}, s32[]{:S(2)}) async-start(s8[4325376]{0:T(1024)(128)(4,1)} %bitcast.638), calls=%async_computation.6 | async-start | bytes 262144
  150.1 1.1 copy-start.10
  168.8 0.8 copy-start.12
  169.6 161.6 %all-gather.2.cloned.1.call-start = ((), (), s32[]{:S(2)}) async-start(), calls=%async_computation.1 | async-start | bytes 1966080 | tf_op jit(solution)/shard_map/all_gather | solution.py:73
  171.4 225.9 %all-reduce.8.cloned.1.call-start = ((), (), s32[]{:S(2)}) async-start(), calls=%async_computation.4 | async-start | bytes 884736 | tf_op jit(solution)/shard_map/psum | solution.py:84
  331.2 1.6 copy-start.2
  341.3 0.8 copy-start.11
  356.6 0.9 copy-start.15
  356.6 0.9 copy-start.16
  366.6 32.5 %copy-start.1 = (bf16[64,32,3,3,3]{0,1,4,3,2:T(8,128)(2,1)S(1)}, bf16[64,32,3,3,3]{0,1,4,3,2:T(8,128)(2,1)}, u32[]{:S(2)}) copy-start(bf16[64,32,3,3,3]{0,1,4,3,2:T(8,128)(2,1)} %param.7) | copy-start | bytes 331780
Sparse Core Ops, SparseCore 0:
  55.3 35.9 reduce-scatter.1
  169.7 126.9 all-reduce.5
  299.2 31.9 all-gather.1
  342.2 55.0 all-reduce.7
where the time goes:
time: 410 us; the launch traced here: 406 us
  waiting for transfers between devices  135 us (33%)
  local copies, waits for them, and re-layouts  88.3 us (22%)
  matrix products  70.9 us (17%)
  blocking collectives  53 us (13%)
  starting transfers between devices  22.4 us (5%)
  other arithmetic  21.4 us (5%)
  between operations  14.6 us (4%)
    psum x1, waiting for transfers between devices, per_device(): summed_w1, summed_b1 = lax.psum((local_w1, local_b1), ('sx', 'sy', 'rep'))  70.9 us
    dot_general x54, matrix products, weight_terms(): jnp.einsum('oxyz,cxyz->oc', cotan, piece, preferred_element_type=jnp.floa...  44.1 us
    conv_general_dilated x10, local copies, waits for them, and re-layouts, convolve(): lax.conv_general_dilated(padded[None], kernel, (1, 1, 1), ((0, 0), (0, 0)...  40.4 us
    psum x1, blocking collectives, per_device(): summed_w1, summed_b1 = lax.psum((local_w1, local_b1), ('sx', 'sy', 'rep'))  38.5 us
    all_gather x1, waiting for transfers between devices, per_device(): gathered = lax.all_gather(pooled_x, 'sy', axis=2, tiled=True)  32.6 us
    psum x1, waiting for transfers between devices, per_device(): summed_w2, summed_b2 = lax.psum((local_w2, local_b2), ('sx', 'rep'))  28.3 us
    conv_general_dilated x3, matrix products, convolve(): lax.conv_general_dilated(padded[None], kernel, (1, 1, 1), ((0, 0), (0, 0)...  26.8 us
    unnamed x46, local copies, waits for them, and re-layouts  19.4 us
  transfers between devices with their start and end apart: 12, of which 5 were waited for; matrix products, arithmetic and copies ran while one was open for 41% of the time, Pallas kernels for 0%

commit v1 on v0

v1 whole, which is shorter than its diff:
```python
import functools
import math

import jax
import jax.numpy as jnp
from jax import lax
from jax.experimental import pallas as pl
from jax.experimental.pallas import tpu as pltpu
from jax.sharding import PartitionSpec as P

BF = jnp.bfloat16
F32 = jnp.float32
VMEM_BYTES = 48 * 1024 * 1024


def dot(a, b):
    return jnp.dot(a, b, preferred_element_type=F32)


def dot_nt(a, b):
    return lax.dot_general(a, b, (((1,), (1,)), ((), ())), preferred_element_type=F32)


def index_pair(rows, cols):
    shape = (rows, cols)
    return (
        lax.broadcasted_iota(jnp.int32, shape, 0),
        lax.broadcasted_iota(jnp.int32, shape, 1),
    )


def one_where(cond):
    return jnp.where(cond, 1.0, 0.0).astype(BF)


def swap_majors(outer, inner):
    r, c = index_pair(outer * inner, outer * inner)
    return one_where(lax.rem(r, outer) * inner + lax.div(r, outer) == c)


def shift_both(width):
    r, c = index_pair(width, 2 * width)
    return one_where(((c < width) & (r == c - 1)) | ((c >= width) & (r == c - width + 1)))


def identity(size):
    r, c = index_pair(size, size)
    return one_where(r == c)


def call(body, name, outs, scratch, ins, smem_ins=0, flops=0):
    vm = pl.BlockSpec(memory_space=pltpu.VMEM)
    sm = pl.BlockSpec(memory_space=pltpu.SMEM)
    return pl.pallas_call(
        body,
        name=name,
        out_shape=outs,
        in_specs=[sm] * smem_ins + [vm] * (len(ins) - smem_ins),
        out_specs=jax.tree.map(lambda _: vm, outs),
        scratch_shapes=scratch,
        compiler_params=pltpu.CompilerParams(vmem_limit_bytes=VMEM_BYTES),
        cost_estimate=pl.CostEstimate(flops=flops, bytes_accessed=1 << 20, transcendentals=0),
    )(*ins)


def prep_body(me, vol, cot, vt, cp, cpad):
    cin, planes, rows, width = vol.shape
    swap = swap_majors(cin, rows)
    half = width // 2
    r, c = index_pair(width, width)
    split = one_where(r == 2 * lax.rem(c, half) + lax.div(c, half))
    for x in range(planes):
        cells = dot(swap, vol[:, x].reshape(cin * rows, width)).astype(BF)
        vt[x] = dot(cells, split).astype(BF).reshape(rows, cin, width)
    nf, rows2, width2 = cot.shape
    step = 16
    swap2 = swap if nf == cin and rows == step else swap_majors(nf, step)
    for h in range(0, rows2, step):
        got = dot(swap2, cot[:, h : h + step].reshape(nf * step, width2))
        cpad[1 + h : 1 + h + step] = got.astype(BF).reshape(step, nf, width2)
    zero = jnp.zeros((1, nf, width2), BF)
    cpad[0:1] = zero
    cpad[rows2 + 1 : rows2 + 2] = zero
    count, rim_rows = cp.shape[0], cp.shape[1]
    for s in range(count):
        cp[s] = cpad[pl.ds((me[0] ^ s) * (rim_rows - 2), rim_rows)]


def conv1_body(odd, vr, za, zb, w1q, bias, cells, mask, pooled, w1b):
    planes, rows, cin, width = vr.shape
    half = width // 2
    c1 = bias.shape[0] // 4
    eye = identity(4 * c1)
    nothing = jnp.zeros((cin, 2 * c1), BF)
    for i in range(3):
        blocks = []
        for ys in range(4):
            for slot in range(4):
                left = w1q[i, ys, slot] if ys < 3 else nothing
                right = w1q[i, ys - 1, slot] if ys > 0 else nothing
                blocks.append(jnp.concatenate([left, right], axis=1))
        w1b[i] = dot_nt(eye, jnp.concatenate(blocks, axis=0)).astype(BF)
    r, c = index_pair(width, width)
    moved = one_where(
        ((c < half) & (c > 0) & (r == half + c - 1)) | ((c >= half) & (r == c - half + 1) & (r < half))
    )
    is_odd = odd[0] == 1
    for x in range(planes + 2):
        if x == 0:
            plane = jnp.where(is_odd, za[...], zb[...])
        elif x == planes + 1:
            plane = jnp.where(is_odd, zb[...], za[...])
        else:
            plane = vr[x - 1]
        out = dot(plane.reshape(rows * cin, width), moved).astype(BF).reshape(rows, cin, width)
        cells[x, :, 0:cin] = out[:, :, :half]
        cells[x, :, cin : 2 * cin] = plane[:, :, :half]
        cells[x, :, 2 * cin : 3 * cin] = plane[:, :, half:]
        cells[x, :, 3 * cin : 4 * cin] = out[:, :, half:]
    pairs = pooled.shape[0] // 2
    deep = 16 * cin
    for t in range(pairs):
        total = None
        for xp in range(2):
            acc = None
            for i in range(3):
                rhs = jnp.concatenate(
                    [
                        cells[xp + i, 4 * t : 4 * t + 4].reshape(deep, half),
                        cells[xp + i, 4 * t + 2 : 4 * t + 6].reshape(deep, half),
                    ],
                    axis=1,
                )
                part = dot(w1b[i], rhs)
                acc = part if acc is None else acc + part
            pre = acc + bias[...]
            above = pre > 0
            mask[xp, t] = jnp.where(above, 1.0, 0.0).astype(BF)
            act = jnp.where(above, pre, 0.3 * pre)
            for b in range(4):
                piece = act[b * c1 : (b + 1) * c1]
                total = piece if total is None else total + piece
        mean = (total * 0.125).astype(BF)
        pooled[2 * t] = mean[:, :half]
        pooled[2 * t + 1] = mean[:, half:]


def with_shifts(store, plane, shifts):
    rows, chans, width = plane.shape
    out = dot(plane.reshape(rows * chans, width), shifts).astype(BF).reshape(rows, chans, 2 * width)
    store(0, out[:, :, :width])
    store(1, plane)
    store(2, out[:, :, width:])


def conv2_body(odd, ur, ua, ub, w2r, pieces, u):
    rows, c1, width = ur.shape
    count, pairs, nf, _ = w2r.shape
    shifts = shift_both(width)
    is_odd = odd[0] == 1
    planes = (
        jnp.where(is_odd, ua[...], ub[...]),
        ur[...],
        jnp.where(is_odd, ub[...], ua[...]),
    )
    for x in range(3):

        def store(k, value, x=x):
            u[x, :, k] = value

        with_shifts(store, planes[x], shifts)
    weights = jnp.concatenate(
        [jnp.concatenate([w2r[s, p] for s in range(count)], axis=0) for p in range(pairs)], axis=1
    )

    def tap(y, d):
        d = d if d < 27 else 0
        return u[d // 9, y + (d // 3) % 3, d % 3]

    def deep(y):
        return jnp.concatenate(
            [tap(y, d) for p in range(pairs) for d in (p, p + pairs)], axis=0
        )

    for y in range(0, rows - 2, 2):
        rhs = jnp.concatenate([deep(y), deep(y + 1)], axis=1)
        out = dot(weights, rhs).astype(BF)
        for s in range(count):
            pieces[s, y] = out[s * nf : (s + 1) * nf, :width]
            pieces[s, y + 1] = out[s * nf : (s + 1) * nf, width:]


def back_body(odd, cells, mask, pooled, co, ca, cb, w2r, red, t_ref, wb, gp, g2):
    count, rows, nf, width = co.shape
    pairs = w2r.shape[1]
    c1 = pooled.shape[1]
    c2 = count * nf
    cin = cells.shape[2] // 4
    shifts = shift_both(width)
    is_odd = odd[0] == 1
    for x in range(3):
        for s in range(count):
            if x == 1:
                plane = co[s]
            elif x == 0:
                plane = jnp.where(is_odd, ca[s], cb[s])
            else:
                plane = jnp.where(is_odd, cb[s], ca[s])

            def store(k, value, x=x, s=s):
                t_ref[x, :, k, s * nf : (s + 1) * nf] = value

            with_shifts(store, plane, shifts)
    eye = identity(2 * c1)
    for p in range(pairs):
        block = jnp.concatenate([w2r[s, p] for s in range(count)], axis=0)
        turned = dot_nt(eye, block)
        for half, d in ((0, p), (1, p + pairs)):
            if d < 27:
                i, j, k = d // 9, (d // 3) % 3, d % 3
                at = ((2 - j) * 3 + (2 - k)) * c2
                wb[2 - i, :, at : at + c2] = turned[half * c1 : (half + 1) * c1].astype(BF)
    deep = 9 * c2
    bias1 = jnp.zeros((8, 4 * c1), F32)
    ones = jnp.ones((8, 2 * width), BF)
    for t in range((rows - 2) // 2):
        acc = None
        for x in range(3):
            rhs = jnp.concatenate(
                [
                    t_ref[x, 2 * t : 2 * t + 3].reshape(deep, width),
                    t_ref[x, 2 * t + 1 : 2 * t + 4].reshape(deep, width),
                ],
                axis=1,
            )
            part = dot(wb[x], rhs)
            acc = part if acc is None else acc + part
        eighth = acc * 0.125
        spread = jnp.concatenate([eighth] * 4, axis=0)
        for xp in range(2):
            grad = (spread * jnp.where(mask[xp, t] > 0, 1.0, 0.3)).astype(BF)
            gp[xp, t] = grad
            bias1 = bias1 + dot_nt(ones, grad)
    n_pairs = (rows - 2) // 2
    lane = lax.broadcasted_iota(jnp.int32, (cin, 2 * c1), 1)
    low_half = lane < c1
    lows, highs = {}, {}
    for i in range(3):
        acc = None
        for xp in range(2):
            for t in range(n_pairs):
                lhs = jnp.concatenate(
                    [
                        cells[xp + i, 4 * t : 4 * t + 4].reshape(16 * cin, width),
                        cells[xp + i, 4 * t + 2 : 4 * t + 6].reshape(16 * cin, width),
                    ],
                    axis=1,
                )
                part = dot_nt(lhs, gp[xp, t])
                acc = part if acc is None else acc + part
        for j in range(3):
            slots = []
            for slot in range(4):
                r0 = (j * 4 + slot) * cin
                r1 = ((j + 1) * 4 + slot) * cin
                slots.append(acc[r0 : r0 + cin, : 2 * c1] + acc[r1 : r1 + cin, 2 * c1 :])
            turned = [pltpu.roll(v, c1, 1) for v in slots]
            for k in range(3):
                d = (i * 3 + j) * 3 + k
                if d < pairs:
                    lows[d] = slots[k] + turned[k + 1]
                    red[d, c2 : c2 + cin] = lows[d]
                else:
                    high = slots[k + 1] + turned[k]
                    p = d - pairs
                    red[p, c2 : c2 + cin] = jnp.where(low_half, red[p, c2 : c2 + cin], high)
    b1 = bias1[:, : 2 * c1] + bias1[:, 2 * c1 :]
    b1 = b1 + pltpu.roll(b1, c1, 1)
    b1 = jnp.concatenate([b1] * (cin // 8), axis=0)
    red[pairs - 1, c2 : c2 + cin] = jnp.where(low_half, red[pairs - 1, c2 : c2 + cin], b1)
    rhs = jnp.concatenate(
        [jnp.concatenate([pooled[y], pooled[y]], axis=0) for y in range(rows - 2)], axis=1
    )
    low_wide = lax.broadcasted_iota(jnp.int32, (c2, 2 * c1), 1) < c1
    for x in range(3):
        for ys in range(3):
            lhs = jnp.concatenate(
                [t_ref[x, y + ys].reshape(3 * c2, width) for y in range(rows - 2)], axis=1
            )
            out = dot_nt(lhs, rhs)
            for zs in range(3):
                d = ((2 - x) * 3 + (2 - ys)) * 3 + (2 - zs)
                g2[d] = out[zs * c2 : (zs + 1) * c2]
    sums = None
    for y in range(1, rows - 1):
        v = t_ref[1, y, 1].astype(F32)
        sums = v if sums is None else sums + v
    b2 = jnp.broadcast_to(jnp.sum(sums, axis=1, keepdims=True), (c2, 2 * c1))
    for p in range(pairs):
        other = g2[p + pairs] if p + pairs < 27 else b2
        red[p, 0:c2] = jnp.where(low_wide, g2[p], other)


def unpack_body(me, *refs):
    pieces, bias, out = refs[:-2], refs[-2], refs[-1]
    rows, nf, width = pieces[0].shape
    swap = swap_majors(rows, nf)
    for s, piece in enumerate(pieces):
        got = dot(swap, piece[...].reshape(rows * nf, width)).reshape(nf, rows, width)
        out[:, pl.ds(pl.multiple_of((me[0] ^ s) * rows, rows), rows), :] = got + bias[...]


def swap_first(value, axis):
    count = lax.axis_size(axis)
    return lax.ppermute(value, axis, [(i, i ^ 1) for i in range(count)])


def swap_second(value, axis):
    count = lax.axis_size(axis)
    pairs = [(i, i + 1) for i in range(1, count - 1, 2)]
    return lax.ppermute(value, axis, pairs + [(b, a) for a, b in pairs])


def to_partner(value, axis, s):
    count = lax.axis_size(axis)
    return lax.ppermute(value, axis, [(i, i ^ s) for i in range(count)])


def tree_sum(values):
    values = list(values)
    while len(values) > 1:
        values = [values[n] + values[n + 1] for n in range(0, len(values), 2)]
    return values[0]


def per_device(volume, first_kernel, first_bias, second_kernel, second_bias, cotangent):
    source = volume[0]
    cotan = cotangent[0, :, 0]
    n_sy, n_sx = lax.axis_size("sy"), lax.axis_size("sx")
    sx, sy, rep = (lax.axis_index(a) for a in ("sx", "sy", "rep"))
    odd_x = (sx % 2).astype(jnp.int32)
    odd_y = (sy % 2).astype(jnp.int32)
    cin, planes, rows, width = source.shape
    nf, rows2, width2 = cotan.shape
    c1 = first_kernel.shape[0]
    c2 = nf * n_sy
    own2 = rows // 2
    pairs = 14
    scale = 1.0 / math.sqrt(
        lax.axis_size("rep") * n_sx * n_sy * (planes // 2) * own2 * (width // 2)
    )
    me = sy.astype(jnp.int32).reshape(1)
    odd = odd_x.reshape(1)

    w1 = first_kernel.transpose(2, 3, 4, 1, 0)
    w1q = jnp.concatenate(
        [
            jnp.pad(w1, ((0, 0), (0, 0), (0, 1), (0, 0), (0, 0))),
            jnp.pad(w1, ((0, 0), (0, 0), (1, 0), (0, 0), (0, 0))),
        ],
        axis=-1,
    )
    bias4 = jnp.tile(first_bias, 4)[:, None]
    w2 = second_kernel.transpose(2, 3, 4, 0, 1).reshape(27, nf, c1)
    w2p = jnp.concatenate([w2[:pairs], jnp.pad(w2[pairs:], ((0, 1), (0, 0), (0, 0)))], axis=-1)

    vt, cp = call(
        prep_body,
        "prep",
        [
            jax.ShapeDtypeStruct((planes, rows, cin, width), BF),
            jax.ShapeDtypeStruct((n_sy, own2 + 2, nf, width2), BF),
        ],
        [pltpu.VMEM((rows2 + 2, nf, width2), BF)],
        (me, source, cotan),
        smem_ins=1,
        flops=1 << 30,
    )

    edge_lo, edge_hi = vt[:, 0], vt[:, rows - 1]
    ya = swap_first(jnp.where(odd_y == 1, edge_lo, edge_hi), "sy")
    yb = swap_second(jnp.where(odd_y == 1, edge_hi, edge_lo), "sy")
    rim_lo = jnp.where(odd_y == 1, ya, yb)
    rim_hi = jnp.where(odd_y == 1, yb, ya)
    vr = jnp.concatenate([rim_lo[:, None], vt, rim_hi[:, None]], axis=1)
    za = swap_first(jnp.where(odd_x == 1, vr[0], vr[planes - 1]), "sx")
    zb = swap_second(jnp.where(odd_x == 1, vr[planes - 1], vr[0]), "sx")

    cgot = [cp[0]] + [to_partner(cp[s], "sy", s) for s in range(1, n_sy)]
    co = jnp.stack(cgot)
    ca = swap_first(co, "sx")
    cb = swap_second(co, "sx")
    w2r = jnp.stack([w2p] + [to_partner(w2p, "sy", s) for s in range(1, n_sy)])

    cells, mask, pooled = call(
        conv1_body,
        "conv1",
        [
            jax.ShapeDtypeStruct((planes + 2, rows + 2, 4 * cin, width // 2), BF),
            jax.ShapeDtypeStruct((2, own2 // 2, 4 * c1, width), BF),
            jax.ShapeDtypeStruct((own2, c1, width // 2), BF),
        ],
        [pltpu.VMEM((3, 4 * c1, 16 * cin), BF)],
        (odd, vr, za, zb, w1q, bias4),
        smem_ins=1,
        flops=3 << 30,
    )

    pa = swap_first(jnp.where(odd_y == 1, pooled[0], pooled[own2 - 1]), "sy")
    pb = swap_second(jnp.where(odd_y == 1, pooled[own2 - 1], pooled[0]), "sy")
    ur = jnp.concatenate(
        [
            jnp.where(odd_y == 1, pa, pb)[None],
            pooled,
            jnp.where(odd_y == 1, pb, pa)[None],
        ],
        axis=0,
    )
    ua = swap_first(ur, "sx")
    ub = swap_second(ur, "sx")

    red = call(
        back_body,
        "backward",
        jax.ShapeDtypeStruct((pairs, c2 + cin, 2 * c1), F32),
        [
            pltpu.VMEM((3, own2 + 2, 3, c2, width2), BF),
            pltpu.VMEM((3, c1, 9 * c2), BF),
            pltpu.VMEM((2, own2 // 2, 4 * c1, width), BF),
            pltpu.VMEM((27, c2, 2 * c1), F32),
        ],
        (odd, cells, mask, pooled, co, ca, cb, w2r),
        smem_ins=1,
        flops=6 << 30,
    )

    pieces = call(
        conv2_body,
        "conv2",
        jax.ShapeDtypeStruct((n_sy, own2, nf, width2), BF),
        [pltpu.VMEM((3, own2 + 2, 3, c1, width2), BF)],
        (odd, ur, ua, ub, w2r),
        smem_ins=1,
        flops=1 << 30,
    )
    out_got = [pieces[0]] + [to_partner(pieces[s], "sy", s) for s in range(1, n_sy)]
    bias_wide = jnp.broadcast_to(second_bias[:, None, None], (nf, 1, width2))
    second_out = call(
        unpack_body,
        "unpack",
        jax.ShapeDtypeStruct((nf, rows2, width2), F32),
        [],
        (me, *out_got, bias_wide),
        smem_ins=1,
        flops=1 << 28,
    )

    hp = pairs // 2
    keep = lax.dynamic_slice_in_dim(red, rep * hp, hp, axis=0)
    send = lax.dynamic_slice_in_dim(red, (1 - rep) * hp, hp, axis=0)
    half = keep + swap_first(send, "rep")
    half_bf = half.astype(BF)
    w1_part = half_bf[:, c2:]
    got = [
        to_partner(
            jnp.concatenate([half_bf[:, s * nf : (s + 1) * nf], w1_part], axis=1), "sy", s
        )
        for s in range(1, n_sy)
    ]
    sum2 = tree_sum([half[:, :nf]] + [g[:, :nf].astype(F32) for g in got])
    sum1 = tree_sum([w1_part.astype(F32)] + [g[:, nf:].astype(F32) for g in got])
    both = jnp.concatenate([sum2, sum1], axis=1).astype(BF)
    total = tree_sum(
        [both.astype(F32)] + [to_partner(both, "sx", s).astype(F32) for s in range(1, n_sx)]
    )
    total = total * scale
    other = swap_first(total, "rep")
    full = jnp.where(rep == 0, jnp.stack([total, other]), jnp.stack([other, total]))
    full = full.reshape(pairs, nf + cin, 2 * c1)

    def taps(block):
        wide = jnp.concatenate([block[:, :, :c1], block[:, :, c1:]], axis=0)
        return wide[:27].reshape(3, 3, 3, block.shape[1], c1), wide[27]

    g2, t2 = taps(full[:, :nf])
    g1, t1 = taps(full[:, nf:])
    return (
        second_out[None, :, None],
        g1.transpose(4, 3, 0, 1, 2),
        t1[0],
        g2.transpose(3, 4, 0, 1, 2),
        t2[:, 0],
    )


def solution(mesh):
    placed = (
        P("rep", None, "sx", "sy", None),
        P(),
        P(),
        P("sy", None, None, None, None),
        P("sy"),
        P("rep", "sy", "sx", None, None),
    )
    return jax.shard_map(
        per_device,
        mesh=mesh,
        in_specs=placed,
        out_specs=(
            P("rep", "sy", "sx", None, None),
            P(),
            P(),
            P("sy", None, None, None, None),
            P("sy"),
        ),
        check_vma=False,
    )
```

time: 410 us -> 81.8 us (0.20)
  waiting for transfers between devices: 135 us -> 16.7 us
  local copies, waits for them, and re-layouts: 88.3 us -> 3.81 us
  matrix products: 70.9 us -> 0 us
  blocking collectives: 53 us -> 0 us
  starting transfers between devices: 22.4 us -> 45.5 us
  other arithmetic: 21.4 us -> 1.84 us
  between operations: 14.6 us -> 1.09 us
  Pallas kernels: 0 us -> 12.6 us
    psum x2 -> x0, waiting for transfers between devices: 99.2 us -> none  [the longest x1 70.9 us: per_device(): summed_w1, summed_b1 = lax.psum((local_w1, local_b1), ('sx', 'sy', 'rep'))]
    psum x2 -> x0, blocking collectives: 53 us -> none  [the longest x1 38.5 us: per_device(): summed_w1, summed_b1 = lax.psum((local_w1, local_b1), ('sx', 'sy', 'rep'))]
    dot_general x54 -> x0, matrix products: 44.1 us -> none  [weight_terms(): jnp.einsum('oxyz,cxyz->oc', cotan, piece, preferred_element_type=jnp.floa...]
    conv_general_dilated x10 -> x0, local copies, waits for them, and re-layouts: 40.4 us -> none  [convolve(): lax.conv_general_dilated(padded[None], kernel, (1, 1, 1), ((0, 0), (0, 0)...]
    all_gather x1 -> x0, waiting for transfers between devices: 32.6 us -> none  [per_device(): gathered = lax.all_gather(pooled_x, 'sy', axis=2, tiled=True)]
    conv_general_dilated x3 -> x0, matrix products: 26.8 us -> none  [convolve(): lax.conv_general_dilated(padded[None], kernel, (1, 1, 1), ((0, 0), (0, 0)...]
    ppermute x8 -> x27, starting transfers between devices: 22.3 us -> 45.5 us  [the longest x15 26 us: to_partner(): return lax.ppermute(value, axis, [(i, i ^ s) for i in range(count)])]
    unnamed x46 -> x13, local copies, waits for them, and re-layouts: 19.4 us -> 2.09 us
  transfers between devices with their start and end apart: 12 -> 27, of which waited for: 5 -> 8; matrix products, arithmetic and copies ran while one was open for 41% -> 1% of each run, Pallas kernels for 0% -> 6%
where the time goes in v1:
time: 81.8 us; the launch traced here: 81.5 us
  starting transfers between devices  45.5 us (56%)
  waiting for transfers between devices  16.7 us (20%)
  Pallas kernels  12.6 us (15%)
  local copies, waits for them, and re-layouts  3.81 us (5%)
  other arithmetic  1.84 us (2%)
  between operations  1.09 us (1%)
    ppermute x15, starting transfers between devices, to_partner(): return lax.ppermute(value, axis, [(i, i ^ s) for i in range(count)])  26 us
    ppermute x7, starting transfers between devices, swap_first(): return lax.ppermute(value, axis, [(i, i ^ 1) for i in range(count)])  16.2 us
    ppermute x15, waiting for transfers between devices, to_partner(): return lax.ppermute(value, axis, [(i, i ^ s) for i in range(count)])  12.7 us
    pallas_call x5, Pallas kernels, call(): pl.pallas_call(body, name=name, out_shape=outs, in_specs=[sm] * smem_ins...  12.6 us
    ppermute x7, waiting for transfers between devices, swap_first(): return lax.ppermute(value, axis, [(i, i ^ 1) for i in range(count)])  3.93 us
    ppermute x5, starting transfers between devices, swap_second(): return lax.ppermute(value, axis, pairs + [(b, a) for a, b in pairs])  3.3 us
    unnamed x13, local copies, waits for them, and re-layouts  2.09 us
  transfers between devices with their start and end apart: 27, of which 8 were waited for; matrix products, arithmetic and copies ran while one was open for 1% of the time, Pallas kernels for 6%

profile of v1, /device:TPU:0, one launch (start us, length us, event | category | flops | bytes accessed | tf_op | source)
XLA Modules:
  0.0 81.5 jit_solution(1152500185538287108)
XLA Ops:
  0.7 1.0 %copy-done = bf16[1,32,2,16,256]{4,3,2,1,0:T(8,128)(2,1)S(1)} copy-done((bf16[1,32,2,16,256]{4,3,2,1,0:T(8,128)(2,1)S(1)}, bf16[1,32,2,16,256]{4,3,2,1,0:T(8,128)(2,1)}, u32[]{:S(2)}) %copy-start) | copy-done | bytes 524312
  1.7 0.9 %copy-done.1 = bf16[1,32,1,32,128]{4,3,2,1,0:T(8,128)(2,1)S(1)} copy-done((bf16[1,32,1,32,128]{4,3,2,1,0:T(8,128)(2,1)S(1)}, bf16[1,32,1,32,128]{4,3,2,1,0:T(8,128)(2,1)}, u32[]{:S(2)}) %copy-start.1) | copy-done | bytes 262168
  2.6 1.2 %prep.1 = (bf16[2,16,32,256]{3,2,1,0:T(8,128)(2,1)S(1)}, bf16[4,10,32,128]{3,2,1,0:T(8,128)(2,1)S(1)}) custom-call(s32[1]{0:T(128)} %bitcast.me, bf16[32,2,16,256]{3,2,1,0:T(8,128)(2,1)S(1)} %bitcast.68, bf16[32,32,128]{2,1,0:T(8,128)(2,1)S(1)} %bitcast.69), custom_call_target="tpu_custom_call" | custom-call | flops 1073741824 | bytes 1048576 | tf_op jit(solution)/shard_map/prep/pallas_call | solution.py:54
  3.9 0.0 copy-start.2
  3.9 3.0 %collective-permute-start = (bf16[2,32,256]{2,1,0:T(8,128)(2,1)S(1)}, bf16[2,32,256]{2,1,0:T(8,128)(2,1)S(1)}, u32[]{:S(2)}, u32[]{:S(2)}) collective-permute-start(bf16[2,32,256]{2,1,0:T(8,128)(2,1)S(1)} %get-tuple-element.29), channel_id=1, source_target_pairs={{0,2},{2,0},{4,6},{6,4},{1,3},{3,1},{5,7},{7,5},{8,10},{10,8},{12,... | collective-permute-start | bytes 98312 | tf_op jit(solution)/shard_map/ppermute | solution.py:315
  6.9 0.7 collective-permute-start.1
  7.6 4.3 %collective-permute-start.14 = (bf16[10,32,128]{2,1,0:T(8,128)(2,1)S(1)}, bf16[10,32,128]{2,1,0:T(8,128)(2,1)S(1)}, u32[]{:S(2)}, u32[]{:S(2)}) collective-permute-start(bf16[10,32,128]{2,1,0:T(8,128)(2,1)S(1)} %get-tuple-element.40), channel_id=1, source_target_pairs={{0,2},{2,0},{4,6},{6,4},{1,3},{3,1},{5,7},{7,5},{8,10},{10,8},{12,... | collective-permute-start | bytes 245768 | tf_op jit(solution)/shard_map/ppermute | solution.py:326
  11.9 1.5 %collective-permute-start.16 = (bf16[10,32,128]{2,1,0:T(8,128)(2,1)S(1)}, bf16[10,32,128]{2,1,0:T(8,128)(2,1)S(1)}, u32[]{:S(2)}, u32[]{:S(2)}) collective-permute-start(bf16[10,32,128]{2,1,0:T(8,128)(2,1)S(1)} %get-tuple-element.38), channel_id=1, source_target_pairs={{0,6},{2,4},{4,2},{6,0},{1,7},{3,5},{5,3},{7,1},{8,14},{10,12},{12... | collective-permute-start | bytes 245768 | tf_op jit(solution)/shard_map/ppermute | solution.py:326
  13.4 0.2 fusion.2.w1q
  13.7 0.0 collective-permute-done.1
  13.7 0.0 copy-start.4
  13.7 0.1 pad_maximum_fusion.vr
  13.9 1.6 %collective-permute-start.2 = (bf16[18,32,256]{2,1,0:T(8,128)(2,1)S(1)}, bf16[18,32,256]{2,1,0:T(8,128)(2,1)S(1)}, u32[]{:S(2)}, u32[]{:S(2)}) collective-permute-start(bf16[18,32,256]{2,1,0:T(8,128)(2,1)S(1)} %get-tuple-element.28), channel_id=1, source_target_pairs={{0,8},{8,0},{16,24},{24,16},{1,9},{9,1},{17,25},{25,17},{2,10},{10... | collective-permute-start | bytes 884744 | tf_op jit(solution)/shard_map/ppermute | solution.py:315
  15.5 0.7 collective-permute-start.3
  16.2 0.1 fusion.4
  16.3 0.1 broadcast_in_dim_tile.4.bias
  16.5 2.0 %collective-permute-start.8 = (bf16[14,32,128]{2,1,0:T(8,128)(2,1)S(1)}, bf16[14,32,128]{2,1,0:T(8,128)(2,1)S(1)}, u32[]{:S(2)}, u32[]{:S(2)}) collective-permute-start(bf16[14,32,128]{2,1,0:T(8,128)(2,1)S(1)} %fusion.4), channel_id=1, source_target_pairs={{0,2},{2,0},{4,6},{6,4},{1,3},{3,1},{5,7},{7,5},{8,10},{10,8},{12,... | collective-permute-start | bytes 344072 | tf_op jit(solution)/shard_map/ppermute | solution.py:326
  18.5 0.0 collective-permute-done.15
  18.5 0.0 collective-permute-start.9
  18.5 0.0 collective-permute-done.16
  18.5 1.5 %collective-permute-start.10 = (bf16[14,32,128]{2,1,0:T(8,128)(2,1)S(1)}, bf16[14,32,128]{2,1,0:T(8,128)(2,1)S(1)}, u32[]{:S(2)}, u32[]{:S(2)}) collective-permute-start(bf16[14,32,128]{2,1,0:T(8,128)(2,1)S(1)} %fusion.4), channel_id=1, source_target_pairs={{0,6},{2,4},{4,2},{6,0},{1,7},{3,5},{5,3},{7,1},{8,14},{10,12},{12... | collective-permute-start | bytes 344072 | tf_op jit(solution)/shard_map/ppermute | solution.py:326
  20.1 2.4 %collective-permute-done.8 = bf16[14,32,128]{2,1,0:T(8,128)(2,1)S(1)} collective-permute-done((bf16[14,32,128]{2,1,0:T(8,128)(2,1)S(1)}, bf16[14,32,128]{2,1,0:T(8,128)(2,1)S(1)}, u32[]{:S(2)}, u32[]{:S(2)}) %collective-permute-start.8) | collective-permute-done | bytes 114720 | tf_op jit(solution)/shard_map/ppermute | solution.py:326
  22.5 4.2 %collective-permute-start.17 = (bf16[4,10,32,128]{3,2,1,0:T(8,128)(2,1)S(1)}, bf16[4,10,32,128]{3,2,1,0:T(8,128)(2,1)S(1)}, u32[]{:S(2)}, u32[]{:S(2)}) collective-permute-start(bf16[4,10,32,128]{3,2,1,0:T(8,128)(2,1)S(1)} %pad_maximum_fusion.4.co), channel_id=1, source_target_pairs={{0,8},{8,0},{16,24},{24,16},{1,9},{9,1},{17,25},{25,17},{2,10},{10... | collective-permute-start | bytes 983048 | tf_op jit(solution)/shard_map/ppermute | solution.py:315
  26.7 0.7 collective-permute-start.18
  27.4 0.1 pad_maximum_fusion.1.w2r
  27.5 0.0 collective-permute-done.3.zb
  27.5 2.5 %conv1.1 = (bf16[4,18,128,128]{3,2,1,0:T(8,128)(2,1)S(1)}, bf16[2,4,256,256]{3,2,1,0:T(8,128)(2,1)S(1)}, bf16[8,64,128]{2,1,0:T(8,128)(2,1)S(1)}) custom-call(s32[1]{0:T(128)} %bitcast.1.odd, bf16[2,18,32,256]{3,2,1,0:T(8,128)(2,1)S(1)} %pad_maximum_fusion.vr, bf16[18,32,256]{2,1,0:T(8,128)(2,1)S(1)} %collective-permute-done.2.za, ...), custom_call_target="tpu_custom_call" | custom-call | flops 3221225472 | bytes 1048576 | tf_op jit(solution)/shard_map/conv1/pallas_call | solution.py:54
  30.0 1.8 %collective-permute-done.17.ca = bf16[4,10,32,128]{3,2,1,0:T(8,128)(2,1)S(1)} collective-permute-done((bf16[4,10,32,128]{3,2,1,0:T(8,128)(2,1)S(1)}, bf16[4,10,32,128]{3,2,1,0:T(8,128)(2,1)S(1)}, u32[]{:S(2)}, u32[]{:S(2)}) %collective-permute-start.17) | collective-permute-done | bytes 327712 | tf_op jit(solution)/shard_map/ppermute | solution.py:315
  31.8 0.0 collective-permute-done.18.cb
  31.8 6.8 %backward.1 = f32[14,160,128]{2,1,0:T(8,128)S(1)} custom-call(s32[1]{0:T(128)} %bitcast.1.odd, bf16[4,18,128,128]{3,2,1,0:T(8,128)(2,1)S(1)} %get-tuple-element.12.cells, bf16[2,4,256,256]{3,2,1,0:T(8,128)(2,1)S(1)} %get-tuple-element.13.mask, bf16[8,64,128]{2,1,0:T(8,128)(2,1)S(1)} %get-tuple-element.11.pooled, ...), custom_call_target="tpu_custom_call" | custom-call | flops 6442450944 | bytes 1048576 | tf_op jit(solution)/shard_map/backward/pallas_call | solution.py:54
  38.7 0.1 collective-permute-start.19
  38.8 1.0 %collective-permute-start.4 = (bf16[64,128]{1,0:T(8,128)(2,1)S(1)}, bf16[64,128]{1,0:T(8,128)(2,1)S(1)}, u32[]{:S(2)}, u32[]{:S(2)}) collective-permute-start(bf16[64,128]{1,0:T(8,128)(2,1)S(1)} %get-tuple-element.48), channel_id=1, source_target_pairs={{0,2},{2,0},{4,6},{6,4},{1,3},{3,1},{5,7},{7,5},{8,10},{10,8},{12,... | collective-permute-start | bytes 49160 | tf_op jit(solution)/shard_map/ppermute | solution.py:315
  39.8 0.7 collective-permute-start.5
  40.5 2.1 %collective-permute-done.4 = bf16[64,128]{1,0:T(8,128)(2,1)S(1)} collective-permute-done((bf16[64,128]{1,0:T(8,128)(2,1)S(1)}, bf16[64,128]{1,0:T(8,128)(2,1)S(1)}, u32[]{:S(2)}, u32[]{:S(2)}) %collective-permute-start.4) | collective-permute-done | bytes 16416 | tf_op jit(solution)/shard_map/ppermute | solution.py:315
  42.6 0.0 collective-permute-done.5
  42.6 0.1 fusion.7
  42.8 4.9 %collective-permute-start.20 = (bf16[7,64,128]{2,1,0:T(8,128)(2,1)S(1)}, bf16[7,64,128]{2,1,0:T(8,128)(2,1)S(1)}, u32[]{:S(2)}, u32[]{:S(2)}) collective-permute-start(bf16[7,64,128]{2,1,0:T(8,128)(2,1)S(1)} %get-tuple-element.52), channel_id=1, source_target_pairs={{0,2},{2,0},{4,6},{6,4},{1,3},{3,1},{5,7},{7,5},{8,10},{10,8},{12,... | collective-permute-start | bytes 344072 | tf_op jit(solution)/shard_map/ppermute | solution.py:326
  47.6 0.0 collective-permute-start.21
  47.6 1.5 %collective-permute-start.22 = (bf16[7,64,128]{2,1,0:T(8,128)(2,1)S(1)}, bf16[7,64,128]{2,1,0:T(8,128)(2,1)S(1)}, u32[]{:S(2)}, u32[]{:S(2)}) collective-permute-start(bf16[7,64,128]{2,1,0:T(8,128)(2,1)S(1)} %concatenate.41), channel_id=1, source_target_pairs={{0,6},{2,4},{4,2},{6,0},{1,7},{3,5},{5,3},{7,1},{8,14},{10,12},{12... | collective-permute-start | bytes 344072 | tf_op jit(solution)/shard_map/ppermute | solution.py:326
  49.2 6.2 %collective-permute-start.6 = (bf16[10,64,128]{2,1,0:T(8,128)(2,1)S(1)}, bf16[10,64,128]{2,1,0:T(8,128)(2,1)S(1)}, u32[]{:S(2)}, u32[]{:S(2)}) collective-permute-start(bf16[10,64,128]{2,1,0:T(8,128)(2,1)S(1)} %pad_maximum_fusion.5.ur), channel_id=1, source_target_pairs={{0,8},{8,0},{16,24},{24,16},{1,9},{9,1},{17,25},{25,17},{2,10},{10... | collective-permute-start | bytes 491528 | tf_op jit(solution)/shard_map/ppermute | solution.py:315
  55.4 0.7 collective-permute-start.7
  56.1 0.1 fusion.6
  56.1 4.2 %collective-permute-start.23 = (bf16[7,64,128]{2,1,0:T(8,128)(2,1)S(1)}, bf16[7,64,128]{2,1,0:T(8,128)(2,1)S(1)}, u32[]{:S(2)}, u32[]{:S(2)}) collective-permute-start(bf16[7,64,128]{2,1,0:T(8,128)(2,1)S(1)} %pad_maximum_fusion.8), channel_id=1, source_target_pairs={{0,8},{8,0},{16,24},{24,16},{1,9},{9,1},{17,25},{25,17},{2,10},{10... | collective-permute-start | bytes 344072 | tf_op jit(solution)/shard_map/ppermute | solution.py:326
  60.3 2.4 %collective-permute-start.25 = (bf16[7,64,128]{2,1,0:T(8,128)(2,1)S(1)}, bf16[7,64,128]{2,1,0:T(8,128)(2,1)S(1)}, u32[]{:S(2)}, u32[]{:S(2)}) collective-permute-start(bf16[7,64,128]{2,1,0:T(8,128)(2,1)S(1)} %pad_maximum_fusion.8), channel_id=1, source_target_pairs={{0,24},{8,16},{16,8},{24,0},{1,25},{9,17},{17,9},{25,1},{2,26},{10... | collective-permute-start | bytes 344072 | tf_op jit(solution)/shard_map/ppermute | solution.py:326
  62.8 1.0 %conv2.1 = bf16[4,8,32,128]{3,2,1,0:T(8,128)(2,1)S(1)} custom-call(s32[1]{0:T(128)} %bitcast.1.odd, bf16[10,64,128]{2,1,0:T(8,128)(2,1)S(1)} %pad_maximum_fusion.5.ur, bf16[10,64,128]{2,1,0:T(8,128)(2,1)S(1)} %collective-permute-done.6.ua, bf16[10,64,128]{2,1,0:T(8,128)(2,1)S(1)} %collective-permute-done.7.ub, bf16[4,14,32,128]{3,2,1,0:T(8,128)(2,1)S(1)} %pad_maximum_fusion.1.w2r), custom_call_target="tpu_custom_call" | custom-call | flops 1073741824 | bytes 1048576 | tf_op jit(solution)/shard_map/conv2/pallas_call | solution.py:54
  63.8 0.0 copy-start.5
  63.8 1.2 %collective-permute-done.23 = bf16[7,64,128]{2,1,0:T(8,128)(2,1)S(1)} collective-permute-done((bf16[7,64,128]{2,1,0:T(8,128)(2,1)S(1)}, bf16[7,64,128]{2,1,0:T(8,128)(2,1)S(1)}, u32[]{:S(2)}, u32[]{:S(2)}) %collective-permute-start.23) | collective-permute-done | bytes 114720 | tf_op jit(solution)/shard_map/ppermute | solution.py:326
  65.0 5.6 %collective-permute-done.24 = bf16[7,64,128]{2,1,0:T(8,128)(2,1)S(1)} collective-permute-done((bf16[7,64,128]{2,1,0:T(8,128)(2,1)S(1)}, bf16[7,64,128]{2,1,0:T(8,128)(2,1)S(1)}, u32[]{:S(2)}, u32[]{:S(2)}) %collective-permute-start.24) | collective-permute-done | bytes 114720 | tf_op jit(solution)/shard_map/ppermute | solution.py:326
  70.6 0.1 add_multiply_fusion
  70.7 0.1 collective-permute-start.26
  70.8 1.2 %collective-permute-start.11 = (bf16[8,32,128]{2,1,0:T(8,128)(2,1)S(1)}, bf16[8,32,128]{2,1,0:T(8,128)(2,1)S(1)}, u32[]{:S(2)}, u32[]{:S(2)}) collective-permute-start(bf16[8,32,128]{2,1,0:T(8,128)(2,1)S(1)} %get-tuple-element.46), channel_id=1, source_target_pairs={{0,2},{2,0},{4,6},{6,4},{1,3},{3,1},{5,7},{7,5},{8,10},{10,8},{12,... | collective-permute-start | bytes 196616 | tf_op jit(solution)/shard_map/ppermute | solution.py:326
  72.0 0.7 collective-permute-start.12
  72.7 1.7 %collective-permute-start.13 = (bf16[8,32,128]{2,1,0:T(8,128)(2,1)S(1)}, bf16[8,32,128]{2,1,0:T(8,128)(2,1)S(1)}, u32[]{:S(2)}, u32[]{:S(2)}) collective-permute-start(bf16[8,32,128]{2,1,0:T(8,128)(2,1)S(1)} %get-tuple-element.44), channel_id=1, source_target_pairs={{0,6},{2,4},{4,2},{6,0},{1,7},{3,5},{5,3},{7,1},{8,14},{10,12},{12... | collective-permute-start | bytes 196616 | tf_op jit(solution)/shard_map/ppermute | solution.py:326
  74.3 1.0 %collective-permute-done.11.refs_1_ = bf16[8,32,128]{2,1,0:T(8,128)(2,1)S(1)} collective-permute-done((bf16[8,32,128]{2,1,0:T(8,128)(2,1)S(1)}, bf16[8,32,128]{2,1,0:T(8,128)(2,1)S(1)}, u32[]{:S(2)}, u32[]{:S(2)}) %collective-permute-start.11) | collective-permute-done | bytes 65568 | tf_op jit(solution)/shard_map/ppermute | solution.py:326
  75.3 1.6 %collective-permute-done.12.refs_2_ = bf16[8,32,128]{2,1,0:T(8,128)(2,1)S(1)} collective-permute-done((bf16[8,32,128]{2,1,0:T(8,128)(2,1)S(1)}, bf16[8,32,128]{2,1,0:T(8,128)(2,1)S(1)}, u32[]{:S(2)}, u32[]{:S(2)}) %collective-permute-start.12) | collective-permute-done | bytes 65568 | tf_op jit(solution)/shard_map/ppermute | solution.py:326
  76.9 0.9 %collective-permute-done.13.refs_3_ = bf16[8,32,128]{2,1,0:T(8,128)(2,1)S(1)} collective-permute-done((bf16[8,32,128]{2,1,0:T(8,128)(2,1)S(1)}, bf16[8,32,128]{2,1,0:T(8,128)(2,1)S(1)}, u32[]{:S(2)}, u32[]{:S(2)}) %collective-permute-start.13) | collective-permute-done | bytes 65568 | tf_op jit(solution)/shard_map/ppermute | solution.py:326
  77.8 0.1 broadcast_in_dim.25.refs_4_
  77.9 1.1 %unpack.1 = f32[32,32,128]{2,1,0:T(8,128)} custom-call(s32[1]{0:T(128)} %bitcast.me, bf16[8,32,128]{2,1,0:T(8,128)(2,1)S(1)} %get-tuple-element.47.refs_0_, bf16[8,32,128]{2,1,0:T(8,128)(2,1)S(1)} %collective-permute-done.11.refs_1_, bf16[8,32,128]{2,1,0:T(8,128)(2,1)S(1)} %collective-permute-done.12.refs_2_, ...), custom_call_target="tpu_custom_call" | custom-call | flops 268435456 | bytes 1048576 | tf_op jit(solution)/shard_map/unpack/pallas_call | solution.py:54
  79.1 0.2 fusion.8
  79.3 0.1 slice.182
  79.3 0.6 slice_bitcast_fusion.8
  79.9 0.1 copy.22
  80.0 0.5 slice_bitcast_fusion.7
  80.5 1.0 %pad_maximum_fusion.2 = (f32[27,32,64]{2,1,0:T(8,128)}, f32[27,32,64]{2,1,0:T(8,128)}) fusion(f32[14,32,64]{2,1,0:T(8,128)S(1)} %get-tuple-element.32, f32[14,32,64]{2,1,0:T(8,128)S(1)} %get-tuple-element.31, f32[14,32,64]{2,1,0:T(8,128)S(1)} %get-tuple-element.33, f32[14,32,64]{2,1,0:T(8,128)S(1)} %get-tuple-element.34), kind=kLoop, calls=%fused_computation.8 | loop fusion | flops 110592 | bytes 901120 | tf_op jit(solution)/shard_map/concatenate | solution.py:482
  (40 shorter events, 0.4 us)
Async XLA Ops:
  0.6 1.0 %copy-start = (bf16[1,32,2,16,256]{4,3,2,1,0:T(8,128)(2,1)S(1)}, bf16[1,32,2,16,256]{4,3,2,1,0:T(8,128)(2,1)}, u32[]{:S(2)}) copy-start(bf16[1,32,2,16,256]{4,3,2,1,0:T(8,128)(2,1)} %param.6) | copy-start | bytes 1572868
  1.7 0.9 %copy-start.1 = (bf16[1,32,1,32,128]{4,3,2,1,0:T(8,128)(2,1)S(1)}, bf16[1,32,1,32,128]{4,3,2,1,0:T(8,128)(2,1)}, u32[]{:S(2)}) copy-start(bf16[1,32,1,32,128]{4,3,2,1,0:T(8,128)(2,1)} %param.11) | copy-start | bytes 786436
  2.6 10.8 %copy-start.3 = (bf16[64,32,3,3,3]{0,1,4,3,2:T(8,128)(2,1)S(1)}, bf16[64,32,3,3,3]{0,1,4,3,2:T(8,128)(2,1)}, u32[]{:S(2)}) copy-start(bf16[64,32,3,3,3]{0,1,4,3,2:T(8,128)(2,1)} %param.7) | copy-start | bytes 331780
  3.9 9.7 %copy-start.2 = (bf16[32,64,3,3,3]{1,0,4,3,2:T(8,128)(2,1)S(1)}, bf16[32,64,3,3,3]{1,0,4,3,2:T(8,128)(2,1)}, u32[]{:S(2)}) copy-start(bf16[32,64,3,3,3]{1,0,4,3,2:T(8,128)(2,1)} %param.9) | copy-start | bytes 331780
  3.9 9.8 %collective-permute-start = (bf16[2,32,256]{2,1,0:T(8,128)(2,1)S(1)}, bf16[2,32,256]{2,1,0:T(8,128)(2,1)S(1)}, u32[]{:S(2)}, u32[]{:S(2)}) collective-permute-start(bf16[2,32,256]{2,1,0:T(8,128)(2,1)S(1)} %get-tuple-element.29), channel_id=1, source_target_pairs={{0,2},{2,0},{4,6},{6,4},{1,3},{3,1},{5,7},{7,5},{8,10},{10,8},{12,... | collective-permute-start | bytes 98312 | tf_op jit(solution)/shard_map/ppermute | solution.py:315
  6.9 6.8 %collective-permute-start.1 = (bf16[2,32,256]{2,1,0:T(8,128)(2,1)S(1)}, bf16[2,32,256]{2,1,0:T(8,128)(2,1)S(1)}, u32[]{:S(2)}, u32[]{:S(2)}) collective-permute-start(bf16[2,32,256]{2,1,0:T(8,128)(2,1)S(1)} %get-tuple-element.30), channel_id=1, source_target_pairs={{2,4},{4,2},{3,5},{5,3},{10,12},{12,10},{11,13},{13,11},{18,20},{2... | collective-permute-start | bytes 98312 | tf_op jit(solution)/shard_map/ppermute | solution.py:321
  7.6 8.9 %collective-permute-start.14 = (bf16[10,32,128]{2,1,0:T(8,128)(2,1)S(1)}, bf16[10,32,128]{2,1,0:T(8,128)(2,1)S(1)}, u32[]{:S(2)}, u32[]{:S(2)}) collective-permute-start(bf16[10,32,128]{2,1,0:T(8,128)(2,1)S(1)} %get-tuple-element.40), channel_id=1, source_target_pairs={{0,2},{2,0},{4,6},{6,4},{1,3},{3,1},{5,7},{7,5},{8,10},{10,8},{12,... | collective-permute-start | bytes 245768 | tf_op jit(solution)/shard_map/ppermute | solution.py:326
  11.9 6.6 %collective-permute-start.15 = (bf16[10,32,128]{2,1,0:T(8,128)(2,1)S(1)}, bf16[10,32,128]{2,1,0:T(8,128)(2,1)S(1)}, u32[]{:S(2)}, u32[]{:S(2)}) collective-permute-start(bf16[10,32,128]{2,1,0:T(8,128)(2,1)S(1)} %get-tuple-element.39), channel_id=1, source_target_pairs={{0,4},{2,6},{4,0},{6,2},{1,5},{3,7},{5,1},{7,3},{8,12},{10,14},{12... | collective-permute-start | bytes 245768 | tf_op jit(solution)/shard_map/ppermute | solution.py:326
  11.9 6.6 %collective-permute-start.16 = (bf16[10,32,128]{2,1,0:T(8,128)(2,1)S(1)}, bf16[10,32,128]{2,1,0:T(8,128)(2,1)S(1)}, u32[]{:S(2)}, u32[]{:S(2)}) collective-permute-start(bf16[10,32,128]{2,1,0:T(8,128)(2,1)S(1)} %get-tuple-element.38), channel_id=1, source_target_pairs={{0,6},{2,4},{4,2},{6,0},{1,7},{3,5},{5,3},{7,1},{8,14},{10,12},{12... | collective-permute-start | bytes 245768 | tf_op jit(solution)/shard_map/ppermute | solution.py:326
  13.7 2.6 %copy-start.4 = (f32[64]{0:T(128)S(1)}, f32[64]{0:T(128)}, u32[]{:S(2)}) copy-start(f32[64]{0:T(128)} %param.8) | copy-start | bytes 772
  13.9 13.6 %collective-permute-start.2 = (bf16[18,32,256]{2,1,0:T(8,128)(2,1)S(1)}, bf16[18,32,256]{2,1,0:T(8,128)(2,1)S(1)}, u32[]{:S(2)}, u32[]{:S(2)}) collective-permute-start(bf16[18,32,256]{2,1,0:T(8,128)(2,1)S(1)} %get-tuple-element.28), channel_id=1, source_target_pairs={{0,8},{8,0},{16,24},{24,16},{1,9},{9,1},{17,25},{25,17},{2,10},{10... | collective-permute-start | bytes 884744 | tf_op jit(solution)/shard_map/ppermute | solution.py:315
  15.5 12.0 %collective-permute-start.3 = (bf16[18,32,256]{2,1,0:T(8,128)(2,1)S(1)}, bf16[18,32,256]{2,1,0:T(8,128)(2,1)S(1)}, u32[]{:S(2)}, u32[]{:S(2)}) collective-permute-start(bf16[18,32,256]{2,1,0:T(8,128)(2,1)S(1)} %get-tuple-element.27), channel_id=1, source_target_pairs={{8,16},{16,8},{9,17},{17,9},{10,18},{18,10},{11,19},{19,11},{12,20... | collective-permute-start | bytes 884744 | tf_op jit(solution)/shard_map/ppermute | solution.py:321
  16.5 6.0 %collective-permute-start.8 = (bf16[14,32,128]{2,1,0:T(8,128)(2,1)S(1)}, bf16[14,32,128]{2,1,0:T(8,128)(2,1)S(1)}, u32[]{:S(2)}, u32[]{:S(2)}) collective-permute-start(bf16[14,32,128]{2,1,0:T(8,128)(2,1)S(1)} %fusion.4), channel_id=1, source_target_pairs={{0,2},{2,0},{4,6},{6,4},{1,3},{3,1},{5,7},{7,5},{8,10},{10,8},{12,... | collective-permute-start | bytes 344072 | tf_op jit(solution)/shard_map/ppermute | solution.py:326
  18.5 8.2 %collective-permute-start.9 = (bf16[14,32,128]{2,1,0:T(8,128)(2,1)S(1)}, bf16[14,32,128]{2,1,0:T(8,128)(2,1)S(1)}, u32[]{:S(2)}, u32[]{:S(2)}) collective-permute-start(bf16[14,32,128]{2,1,0:T(8,128)(2,1)S(1)} %fusion.4), channel_id=1, source_target_pairs={{0,4},{2,6},{4,0},{6,2},{1,5},{3,7},{5,1},{7,3},{8,12},{10,14},{12... | collective-permute-start | bytes 344072 | tf_op jit(solution)/shard_map/ppermute | solution.py:326
  18.5 8.9 %collective-permute-start.10 = (bf16[14,32,128]{2,1,0:T(8,128)(2,1)S(1)}, bf16[14,32,128]{2,1,0:T(8,128)(2,1)S(1)}, u32[]{:S(2)}, u32[]{:S(2)}) collective-permute-start(bf16[14,32,128]{2,1,0:T(8,128)(2,1)S(1)} %fusion.4), channel_id=1, source_target_pairs={{0,6},{2,4},{4,2},{6,0},{1,7},{3,5},{5,3},{7,1},{8,14},{10,12},{12... | collective-permute-start | bytes 344072 | tf_op jit(solution)/shard_map/ppermute | solution.py:326
  22.5 9.2 %collective-permute-start.17 = (bf16[4,10,32,128]{3,2,1,0:T(8,128)(2,1)S(1)}, bf16[4,10,32,128]{3,2,1,0:T(8,128)(2,1)S(1)}, u32[]{:S(2)}, u32[]{:S(2)}) collective-permute-start(bf16[4,10,32,128]{3,2,1,0:T(8,128)(2,1)S(1)} %pad_maximum_fusion.4.co), channel_id=1, source_target_pairs={{0,8},{8,0},{16,24},{24,16},{1,9},{9,1},{17,25},{25,17},{2,10},{10... | collective-permute-start | bytes 983048 | tf_op jit(solution)/shard_map/ppermute | solution.py:315
  26.7 5.1 %collective-permute-start.18 = (bf16[4,10,32,128]{3,2,1,0:T(8,128)(2,1)S(1)}, bf16[4,10,32,128]{3,2,1,0:T(8,128)(2,1)S(1)}, u32[]{:S(2)}, u32[]{:S(2)}) collective-permute-start(bf16[4,10,32,128]{3,2,1,0:T(8,128)(2,1)S(1)} %pad_maximum_fusion.4.co), channel_id=1, source_target_pairs={{8,16},{16,8},{9,17},{17,9},{10,18},{18,10},{11,19},{19,11},{12,20... | collective-permute-start | bytes 983048 | tf_op jit(solution)/shard_map/ppermute | solution.py:321
  38.7 3.9 %collective-permute-start.19 = (f32[7,160,128]{2,1,0:T(8,128)S(1)}, f32[7,160,128]{2,1,0:T(8,128)S(1)}, u32[]{:S(2)}, u32[]{:S(2)}) collective-permute-start(f32[7,160,128]{2,1,0:T(8,128)S(1)} %constant_dynamic-slice_fusion), channel_id=1, source_target_pairs={{0,1},{1,0},{2,3},{3,2},{4,5},{5,4},{6,7},{7,6},{8,9},{9,8},{10,11... | collective-permute-start | bytes 1720328 | tf_op jit(solution)/shard_map/ppermute | solution.py:315
  38.8 3.8 %collective-permute-start.4 = (bf16[64,128]{1,0:T(8,128)(2,1)S(1)}, bf16[64,128]{1,0:T(8,128)(2,1)S(1)}, u32[]{:S(2)}, u32[]{:S(2)}) collective-permute-start(bf16[64,128]{1,0:T(8,128)(2,1)S(1)} %get-tuple-element.48), channel_id=1, source_target_pairs={{0,2},{2,0},{4,6},{6,4},{1,3},{3,1},{5,7},{7,5},{8,10},{10,8},{12,... | collective-permute-start | bytes 49160 | tf_op jit(solution)/shard_map/ppermute | solution.py:315
  39.8 2.8 %collective-permute-start.5 = (bf16[64,128]{1,0:T(8,128)(2,1)S(1)}, bf16[64,128]{1,0:T(8,128)(2,1)S(1)}, u32[]{:S(2)}, u32[]{:S(2)}) collective-permute-start(bf16[64,128]{1,0:T(8,128)(2,1)S(1)} %get-tuple-element.49), channel_id=1, source_target_pairs={{2,4},{4,2},{3,5},{5,3},{10,12},{12,10},{11,13},{13,11},{18,20},{2... | collective-permute-start | bytes 49160 | tf_op jit(solution)/shard_map/ppermute | solution.py:321
  42.8 13.3 %collective-permute-start.20 = (bf16[7,64,128]{2,1,0:T(8,128)(2,1)S(1)}, bf16[7,64,128]{2,1,0:T(8,128)(2,1)S(1)}, u32[]{:S(2)}, u32[]{:S(2)}) collective-permute-start(bf16[7,64,128]{2,1,0:T(8,128)(2,1)S(1)} %get-tuple-element.52), channel_id=1, source_target_pairs={{0,2},{2,0},{4,6},{6,4},{1,3},{3,1},{5,7},{7,5},{8,10},{10,8},{12,... | collective-permute-start | bytes 344072 | tf_op jit(solution)/shard_map/ppermute | solution.py:326
  47.6 8.4 %collective-permute-start.21 = (bf16[7,64,128]{2,1,0:T(8,128)(2,1)S(1)}, bf16[7,64,128]{2,1,0:T(8,128)(2,1)S(1)}, u32[]{:S(2)}, u32[]{:S(2)}) collective-permute-start(bf16[7,64,128]{2,1,0:T(8,128)(2,1)S(1)} %get-tuple-element.53), channel_id=1, source_target_pairs={{0,4},{2,6},{4,0},{6,2},{1,5},{3,7},{5,1},{7,3},{8,12},{10,14},{12... | collective-permute-start | bytes 344072 | tf_op jit(solution)/shard_map/ppermute | solution.py:326
  47.6 8.4 %collective-permute-start.22 = (bf16[7,64,128]{2,1,0:T(8,128)(2,1)S(1)}, bf16[7,64,128]{2,1,0:T(8,128)(2,1)S(1)}, u32[]{:S(2)}, u32[]{:S(2)}) collective-permute-start(bf16[7,64,128]{2,1,0:T(8,128)(2,1)S(1)} %concatenate.41), channel_id=1, source_target_pairs={{0,6},{2,4},{4,2},{6,0},{1,7},{3,5},{5,3},{7,1},{8,14},{10,12},{12... | collective-permute-start | bytes 344072 | tf_op jit(solution)/shard_map/ppermute | solution.py:326
  49.2 13.6 %collective-permute-start.6 = (bf16[10,64,128]{2,1,0:T(8,128)(2,1)S(1)}, bf16[10,64,128]{2,1,0:T(8,128)(2,1)S(1)}, u32[]{:S(2)}, u32[]{:S(2)}) collective-permute-start(bf16[10,64,128]{2,1,0:T(8,128)(2,1)S(1)} %pad_maximum_fusion.5.ur), channel_id=1, source_target_pairs={{0,8},{8,0},{16,24},{24,16},{1,9},{9,1},{17,25},{25,17},{2,10},{10... | collective-permute-start | bytes 491528 | tf_op jit(solution)/shard_map/ppermute | solution.py:315
  55.4 7.4 %collective-permute-start.7 = (bf16[10,64,128]{2,1,0:T(8,128)(2,1)S(1)}, bf16[10,64,128]{2,1,0:T(8,128)(2,1)S(1)}, u32[]{:S(2)}, u32[]{:S(2)}) collective-permute-start(bf16[10,64,128]{2,1,0:T(8,128)(2,1)S(1)} %pad_maximum_fusion.5.ur), channel_id=1, source_target_pairs={{8,16},{16,8},{9,17},{17,9},{10,18},{18,10},{11,19},{19,11},{12,20... | collective-permute-start | bytes 491528 | tf_op jit(solution)/shard_map/ppermute | solution.py:321
  56.1 8.8 %collective-permute-start.23 = (bf16[7,64,128]{2,1,0:T(8,128)(2,1)S(1)}, bf16[7,64,128]{2,1,0:T(8,128)(2,1)S(1)}, u32[]{:S(2)}, u32[]{:S(2)}) collective-permute-start(bf16[7,64,128]{2,1,0:T(8,128)(2,1)S(1)} %pad_maximum_fusion.8), channel_id=1, source_target_pairs={{0,8},{8,0},{16,24},{24,16},{1,9},{9,1},{17,25},{25,17},{2,10},{10... | collective-permute-start | bytes 344072 | tf_op jit(solution)/shard_map/ppermute | solution.py:326
  60.3 10.3 %collective-permute-start.24 = (bf16[7,64,128]{2,1,0:T(8,128)(2,1)S(1)}, bf16[7,64,128]{2,1,0:T(8,128)(2,1)S(1)}, u32[]{:S(2)}, u32[]{:S(2)}) collective-permute-start(bf16[7,64,128]{2,1,0:T(8,128)(2,1)S(1)} %pad_maximum_fusion.8), channel_id=1, source_target_pairs={{0,16},{8,24},{16,0},{24,8},{1,17},{9,25},{17,1},{25,9},{2,18},{10... | collective-permute-start | bytes 344072 | tf_op jit(solution)/shard_map/ppermute | solution.py:326
  60.3 10.3 %collective-permute-start.25 = (bf16[7,64,128]{2,1,0:T(8,128)(2,1)S(1)}, bf16[7,64,128]{2,1,0:T(8,128)(2,1)S(1)}, u32[]{:S(2)}, u32[]{:S(2)}) collective-permute-start(bf16[7,64,128]{2,1,0:T(8,128)(2,1)S(1)} %pad_maximum_fusion.8), channel_id=1, source_target_pairs={{0,24},{8,16},{16,8},{24,0},{1,25},{9,17},{17,9},{25,1},{2,26},{10... | collective-permute-start | bytes 344072 | tf_op jit(solution)/shard_map/ppermute | solution.py:326
  63.8 14.0 %copy-start.5 = (f32[32]{0:T(128)S(1)}, f32[32]{0:T(128)}, u32[]{:S(2)}) copy-start(f32[32]{0:T(128)} %param.10) | copy-start | bytes 388
  70.7 8.4 %collective-permute-start.26 = (f32[7,64,128]{2,1,0:T(8,128)S(1)}, f32[7,64,128]{2,1,0:T(8,128)S(1)}, u32[]{:S(2)}, u32[]{:S(2)}) collective-permute-start(f32[7,64,128]{2,1,0:T(8,128)S(1)} %add_multiply_fusion), channel_id=1, source_target_pairs={{0,1},{1,0},{2,3},{3,2},{4,5},{5,4},{6,7},{7,6},{8,9},{9,8},{10,11... | collective-permute-start | bytes 688136 | tf_op jit(solution)/shard_map/ppermute | solution.py:315
  70.8 4.6 %collective-permute-start.11 = (bf16[8,32,128]{2,1,0:T(8,128)(2,1)S(1)}, bf16[8,32,128]{2,1,0:T(8,128)(2,1)S(1)}, u32[]{:S(2)}, u32[]{:S(2)}) collective-permute-start(bf16[8,32,128]{2,1,0:T(8,128)(2,1)S(1)} %get-tuple-element.46), channel_id=1, source_target_pairs={{0,2},{2,0},{4,6},{6,4},{1,3},{3,1},{5,7},{7,5},{8,10},{10,8},{12,... | collective-permute-start | bytes 196616 | tf_op jit(solution)/shard_map/ppermute | solution.py:326
  72.0 5.0 %collective-permute-start.12 = (bf16[8,32,128]{2,1,0:T(8,128)(2,1)S(1)}, bf16[8,32,128]{2,1,0:T(8,128)(2,1)S(1)}, u32[]{:S(2)}, u32[]{:S(2)}) collective-permute-start(bf16[8,32,128]{2,1,0:T(8,128)(2,1)S(1)} %get-tuple-element.45), channel_id=1, source_target_pairs={{0,4},{2,6},{4,0},{6,2},{1,5},{3,7},{5,1},{7,3},{8,12},{10,14},{12... | collective-permute-start | bytes 196616 | tf_op jit(solution)/shard_map/ppermute | solution.py:326
  72.7 5.2 %collective-permute-start.13 = (bf16[8,32,128]{2,1,0:T(8,128)(2,1)S(1)}, bf16[8,32,128]{2,1,0:T(8,128)(2,1)S(1)}, u32[]{:S(2)}, u32[]{:S(2)}) collective-permute-start(bf16[8,32,128]{2,1,0:T(8,128)(2,1)S(1)} %get-tuple-element.44), channel_id=1, source_target_pairs={{0,6},{2,4},{4,2},{6,0},{1,7},{3,5},{5,3},{7,1},{8,14},{10,12},{12... | collective-permute-start | bytes 196616 | tf_op jit(solution)/shard_map/ppermute | solution.py:326

commit v2 on v1

v2 whole, which is shorter than its diff:
```python
import functools
import math

import jax
import jax.numpy as jnp
from jax import lax
from jax.experimental import pallas as pl
from jax.experimental.pallas import tpu as pltpu
from jax.sharding import PartitionSpec as P

BF = jnp.bfloat16
F32 = jnp.float32
VMEM_BYTES = 20 * 1024 * 1024


def dot(a, b):
    return jnp.dot(a, b, preferred_element_type=F32)


def dot_nt(a, b):
    return lax.dot_general(a, b, (((1,), (1,)), ((), ())), preferred_element_type=F32)


def index_pair(rows, cols):
    shape = (rows, cols)
    return (
        lax.broadcasted_iota(jnp.int32, shape, 0),
        lax.broadcasted_iota(jnp.int32, shape, 1),
    )


def one_where(cond):
    return jnp.where(cond, 1.0, 0.0).astype(BF)


def swap_majors(outer, inner):
    r, c = index_pair(outer * inner, outer * inner)
    return one_where(lax.rem(r, outer) * inner + lax.div(r, outer) == c)


def shift_both(width):
    r, c = index_pair(width, 2 * width)
    return one_where(((c < width) & (r == c - 1)) | ((c >= width) & (r == c - width + 1)))


def identity(size):
    r, c = index_pair(size, size)
    return one_where(r == c)


def beside(place, below, first, second):
    second = jnp.where(place[5] == 1, second, jnp.zeros_like(second))
    return jnp.where((place[0] == 1) == below, first, second)


def call(body, name, outs, scratch, ins, smem_ins=0, flops=0):
    vm = pl.BlockSpec(memory_space=pltpu.VMEM)
    sm = pl.BlockSpec(memory_space=pltpu.SMEM)
    return pl.pallas_call(
        body,
        name=name,
        out_shape=outs,
        in_specs=[sm] * smem_ins + [vm] * (len(ins) - smem_ins),
        out_specs=jax.tree.map(lambda _: vm, outs),
        scratch_shapes=scratch,
        compiler_params=pltpu.CompilerParams(vmem_limit_bytes=VMEM_BYTES),
        cost_estimate=pl.CostEstimate(flops=flops, bytes_accessed=1 << 20, transcendentals=0),
    )(*ins)


def prep_body(me, vol, cot, w2, vt, cp, w2p, cpad):
    cin, planes, rows, width = vol.shape
    swap = swap_majors(cin, rows)
    half = width // 2
    r, c = index_pair(width, width)
    split = one_where(r == 2 * lax.rem(c, half) + lax.div(c, half))
    for x in range(planes):
        cells = dot(swap, vol[:, x].reshape(cin * rows, width)).astype(BF)
        vt[x] = dot(cells, split).astype(BF).reshape(rows, cin, width)
    nf, rows2, width2 = cot.shape
    step = 16
    swap2 = swap if nf == cin and rows == step else swap_majors(nf, step)
    for h in range(0, rows2, step):
        got = dot(swap2, cot[:, h : h + step].reshape(nf * step, width2))
        cpad[1 + h : 1 + h + step] = got.astype(BF).reshape(step, nf, width2)
    zero = jnp.zeros((1, nf, width2), BF)
    cpad[0:1] = zero
    cpad[rows2 + 1 : rows2 + 2] = zero
    count, rim_rows = cp.shape[0], cp.shape[1]
    for s in range(count):
        cp[s] = cpad[pl.ds((me[0] ^ s) * (rim_rows - 2), rim_rows)]
    taps, _, c1 = w2.shape
    pairs = w2p.shape[0]
    r, c = index_pair(c1, 2 * c1)
    low = dot(w2[:pairs].reshape(pairs * nf, c1), one_where(r == c))
    high = dot(w2[pairs:].reshape((taps - pairs) * nf, c1), one_where(r + c1 == c))
    for p in range(pairs):
        both = low[p * nf : (p + 1) * nf]
        if p + pairs < taps:
            both = both + high[p * nf : (p + 1) * nf]
        w2p[p] = both.astype(BF)


def conv1_body(place, vr, za, zb, w1q, bias, cells, mask, pooled, w1b):
    planes, rows, cin, width = vr.shape
    half = width // 2
    c1 = bias.shape[0] // 4
    eye = identity(4 * c1)
    nothing = jnp.zeros((cin, 2 * c1), BF)
    for i in range(3):
        blocks = []
        for ys in range(4):
            for slot in range(4):
                left = w1q[i, ys, slot] if ys < 3 else nothing
                right = w1q[i, ys - 1, slot] if ys > 0 else nothing
                blocks.append(jnp.concatenate([left, right], axis=1))
        w1b[i] = dot_nt(eye, jnp.concatenate(blocks, axis=0)).astype(BF)
    r, c = index_pair(width, width)
    moved = one_where(
        ((c < half) & (c > 0) & (r == half + c - 1)) | ((c >= half) & (r == c - half + 1) & (r < half))
    )
    for x in range(planes + 2):
        if x in (0, planes + 1):
            plane = beside(place, x == 0, za[...], zb[...])
        else:
            plane = vr[x - 1]
        out = dot(plane.reshape(rows * cin, width), moved).astype(BF).reshape(rows, cin, width)
        cells[x, :, 0:cin] = out[:, :, :half]
        cells[x, :, cin : 2 * cin] = plane[:, :, :half]
        cells[x, :, 2 * cin : 3 * cin] = plane[:, :, half:]
        cells[x, :, 3 * cin : 4 * cin] = out[:, :, half:]
    rows2 = pooled.shape[0]
    deep = 16 * cin
    for t in range(rows2 // 2):
        total = None
        for xp in range(2):
            acc = None
            for i in range(3):
                rhs = jnp.concatenate(
                    [
                        cells[xp + i, 4 * t : 4 * t + 4].reshape(deep, half),
                        cells[xp + i, 4 * t + 2 : 4 * t + 6].reshape(deep, half),
                    ],
                    axis=1,
                )
                part = dot(w1b[i], rhs)
                acc = part if acc is None else acc + part
            pre = acc + bias[...]
            above = pre > 0
            flags = jnp.where(above, 1.0, 0.0).astype(BF)
            if t > 0:
                mask[xp, 2 * t - 1] = flags[:, :half]
            if 2 * t < rows2 - 2:
                mask[xp, 2 * t] = flags[:, half:]
            act = jnp.where(above, pre, 0.3 * pre)
            for b in range(4):
                piece = act[b * c1 : (b + 1) * c1]
                total = piece if total is None else total + piece
        mean = (total * 0.125).astype(BF)
        first, second = mean[:, :half], mean[:, half:]
        if t == 0:
            first = jnp.where(place[1] == 1, first, jnp.zeros_like(first))
        if t == rows2 // 2 - 1:
            second = jnp.where(place[2] == 1, second, jnp.zeros_like(second))
        pooled[2 * t] = first
        pooled[2 * t + 1] = second


def with_shifts(store, plane, shifts):
    rows, chans, width = plane.shape
    out = dot(plane.reshape(rows * chans, width), shifts).astype(BF).reshape(rows, chans, 2 * width)
    store(0, out[:, :, :width])
    store(1, plane)
    store(2, out[:, :, width:])


def conv2_body(place, ur, ua, ub, w2r, pieces, u):
    rows, c1, width = ur.shape
    count, pairs, nf, _ = w2r.shape
    shifts = shift_both(width)
    planes = (
        beside(place, True, ua[...], ub[...]),
        ur[...],
        beside(place, False, ua[...], ub[...]),
    )
    for x in range(3):

        def store(k, value, x=x):
            u[x, :, k] = value

        with_shifts(store, planes[x], shifts)
    weights = jnp.concatenate(
        [jnp.concatenate([w2r[s, p] for s in range(count)], axis=0) for p in range(pairs)], axis=1
    )

    def tap(y, d):
        d = d if d < 27 else 0
        return u[d // 9, y + (d // 3) % 3, d % 3]

    def deep(y):
        return jnp.concatenate(
            [tap(y, d) for p in range(pairs) for d in (p, p + pairs)], axis=0
        )

    for y in range(0, rows - 2, 2):
        rhs = jnp.concatenate([deep(y), deep(y + 1)], axis=1)
        out = dot(weights, rhs).astype(BF)
        for s in range(count):
            pieces[s, y] = out[s * nf : (s + 1) * nf, :width]
            pieces[s, y + 1] = out[s * nf : (s + 1) * nf, width:]


def own_body(co, pooled, w2r, wb, own_back, own_g2, own_b2, t_ref):
    count, rows, nf, width = co.shape
    pairs = w2r.shape[1]
    c1 = pooled.shape[1]
    c2 = count * nf
    fill_planes(t_ref, co, shift_both(width))
    eye = identity(2 * c1)
    for p in range(pairs):
        block = jnp.concatenate([w2r[s, p] for s in range(count)], axis=0)
        turned = dot_nt(eye, block)
        for half, d in ((0, p), (1, p + pairs)):
            if d < 27:
                i, j, k = d // 9, (d // 3) % 3, d % 3
                at = ((2 - j) * 3 + (2 - k)) * c2
                wb[2 - i, :, at : at + c2] = turned[half * c1 : (half + 1) * c1].astype(BF)
    for t in range((rows - 2) // 2):
        own_back[t] = dot(wb[1], pair_rows(t_ref, t))
    rhs = pooled_wide(pooled)
    for ys in range(3):
        out = dot_nt(rows_wide(t_ref, ys, rows - 2), rhs)
        for zs in range(3):
            own_g2[(2 - ys) * 3 + (2 - zs)] = out[zs * c2 : (zs + 1) * c2]
    sums = None
    for y in range(1, rows - 1):
        v = t_ref[y, 1].astype(F32)
        sums = v if sums is None else sums + v
    own_b2[...] = jnp.broadcast_to(jnp.sum(sums, axis=1, keepdims=True), own_b2.shape)


def fill_planes(t_ref, plane, shifts):
    nf = plane.shape[2]
    for s in range(plane.shape[0]):

        def store(k, value, s=s):
            t_ref[:, k, s * nf : (s + 1) * nf] = value

        with_shifts(store, plane[s], shifts)


def pair_rows(t_ref, t):
    rows, slots, chans, width = t_ref.shape
    return jnp.concatenate(
        [t_ref[2 * t + n : 2 * t + n + 3].reshape(3 * slots * chans, width) for n in range(2)],
        axis=1,
    )


def rows_wide(t_ref, ys, count):
    rows, slots, chans, width = t_ref.shape
    return jnp.concatenate(
        [t_ref[y + ys].reshape(slots * chans, width) for y in range(count)], axis=1
    )


def pooled_wide(pooled):
    return jnp.concatenate(
        [
            jnp.concatenate([pooled[y], pooled[y]], axis=0)
            for y in range(1, pooled.shape[0] - 1)
        ],
        axis=1,
    )


def back_body(place, cells, mask, pooled, ca, cb, wb, own_back, own_g2, own_b2,
              keep, send, t0, t2, gp, g2, red):
    count, rows, nf, width = ca.shape
    pairs = 14
    c1 = pooled.shape[1]
    c2 = count * nf
    cin = cells.shape[2] // 4
    shifts = shift_both(width)
    fill_planes(t0, beside(place, True, ca[...], cb[...]), shifts)
    fill_planes(t2, beside(place, False, ca[...], cb[...]), shifts)
    bias1 = jnp.zeros((8, 4 * c1), F32)
    ones = jnp.ones((8, 2 * width), BF)
    n_pairs = (rows - 2) // 2
    for t in range(n_pairs):
        acc = own_back[t] + dot(wb[0], pair_rows(t0, t)) + dot(wb[2], pair_rows(t2, t))
        eighth = acc * 0.125
        spread = jnp.concatenate([eighth] * 4, axis=0)
        for xp in range(2):
            flags = jnp.concatenate([mask[xp, 2 * t], mask[xp, 2 * t + 1]], axis=1)
            grad = (spread * jnp.where(flags > 0, 1.0, 0.3)).astype(BF)
            gp[xp, t] = grad
            bias1 = bias1 + dot_nt(ones, grad)
    rhs = pooled_wide(pooled)
    for x, t_ref in ((0, t0), (2, t2)):
        for ys in range(3):
            out = dot_nt(rows_wide(t_ref, ys, rows - 2), rhs)
            for zs in range(3):
                d = ((2 - x) * 3 + (2 - ys)) * 3 + (2 - zs)
                g2[d] = out[zs * c2 : (zs + 1) * c2]

    def part2(d):
        if d == 27:
            return own_b2[...]
        return own_g2[d - 9] if 9 <= d < 18 else g2[d]

    parts = keep.shape[0]
    hp = pairs // 2
    share2, share1 = nf // parts, cin // parts
    low_wide = lax.broadcasted_iota(jnp.int32, (c2, 2 * c1), 1) < c1

    def put(p, start, share, block):
        for part in range(parts):
            red[p // hp, part, p % hp, start : start + share] = block[
                part * share : (part + 1) * share
            ]

    for p in range(pairs):
        wide = jnp.where(low_wide, part2(p), part2(p + pairs))
        for s in range(count):
            put(p, s * share2, share2, wide[s * nf : (s + 1) * nf])
    lane = lax.broadcasted_iota(jnp.int32, (cin, 2 * c1), 1)
    low_half = lane < c1
    lows, highs = {}, {}
    for i in range(3):
        acc = None
        for xp in range(2):
            for t in range(n_pairs):
                lhs = jnp.concatenate(
                    [
                        cells[xp + i, 4 * t + 2 : 4 * t + 6].reshape(16 * cin, width),
                        cells[xp + i, 4 * t + 4 : 4 * t + 8].reshape(16 * cin, width),
                    ],
                    axis=1,
                )
                part = dot_nt(lhs, gp[xp, t])
                acc = part if acc is None else acc + part
        for j in range(3):
            slots = []
            for slot in range(4):
                r0 = (j * 4 + slot) * cin
                r1 = ((j + 1) * 4 + slot) * cin
                slots.append(acc[r0 : r0 + cin, : 2 * c1] + acc[r1 : r1 + cin, 2 * c1 :])
            turned = [pltpu.roll(v, c1, 1) for v in slots]
            for k in range(3):
                d = (i * 3 + j) * 3 + k
                if d < pairs:
                    lows[d] = slots[k] + turned[k + 1]
                else:
                    highs[d - pairs] = slots[k + 1] + turned[k]
    b1 = bias1[:, : 2 * c1] + bias1[:, 2 * c1 :]
    b1 = b1 + pltpu.roll(b1, c1, 1)
    highs[pairs - 1] = jnp.concatenate([b1] * (cin // 8), axis=0)
    for p in range(pairs):
        put(p, count * share2, share1, jnp.where(low_half, lows[p], highs[p]))
    for part in range(parts):
        keep[part] = red[place[4], part ^ place[3]]
        send[part] = red[1 - place[4], part ^ place[3]]


def unpack_body(me, *refs):
    pieces, bias, out = refs[:-2], refs[-2], refs[-1]
    nf, _, width = bias.shape
    rows = out.shape[1] // len(pieces)
    swap = swap_majors(rows, nf)
    for s, piece in enumerate(pieces):
        got = dot(swap, piece[: rows * nf]).reshape(nf, rows, width)
        out[:, pl.ds(pl.multiple_of((me[0] ^ s) * rows, rows), rows), :] = got + bias[...]


def finish_body(place, mine, other, g2, b2, g1, b1):
    parts, hp, _, width = mine.shape
    nf, cin, c1 = g2.shape[1], g1.shape[1], g2.shape[2]
    share2, share1 = nf // parts, cin // parts
    first = place[4] == 0
    for part in range(parts):
        slot = part ^ place[3]
        got = mine[slot].astype(F32)
        more = other[slot].astype(F32)
        halves = (jnp.where(first, got, more), jnp.where(first, more, got))
        for p in range(2 * hp):
            block = halves[p // hp][p % hp]
            turned = pltpu.roll(block, c1, 1)
            for d, v in ((p, block), (p + 2 * hp, turned)):
                low = v[:share2, :c1]
                high = v[share2:, :c1]
                if d < 27:
                    g2[d, part * share2 : (part + 1) * share2] = low
                    g1[d, part * share1 : (part + 1) * share1] = high
                else:
                    b2[part * share2 : (part + 1) * share2] = low
                    if part == 0:
                        b1[0:1] = high[0:1]


def swap_first(value, axis):
    count = lax.axis_size(axis)
    return lax.ppermute(value, axis, [(i, i ^ 1) for i in range(count)])


def swap_second(value, axis):
    count = lax.axis_size(axis)
    both = lax.axis_size("rep")
    pairs = []
    for i in range(count):
        for r in range(both):
            if i in (0, count - 1):
                pairs.append((i * both + r, i * both + (r ^ 1)))
            else:
                pairs.append((i * both + r, (i + 1 if i % 2 else i - 1) * both + r))
    return lax.ppermute(value, (axis, "rep"), pairs)


def to_partner(value, axis, s):
    count = lax.axis_size(axis)
    return lax.ppermute(value, axis, [(i, i ^ s) for i in range(count)])


def tree_sum(values):
    values = list(values)
    while len(values) > 1:
        values = [values[n] + values[n + 1] for n in range(0, len(values), 2)]
    return values[0]


def per_device(volume, first_kernel, first_bias, second_kernel, second_bias, cotangent):
    source = volume[0]
    cotan = cotangent[0, :, 0]
    n_sy, n_sx = lax.axis_size("sy"), lax.axis_size("sx")
    sx, sy, rep = (lax.axis_index(a) for a in ("sx", "sy", "rep"))
    odd_x = (sx % 2).astype(jnp.int32)
    odd_y = (sy % 2).astype(jnp.int32)
    cin, planes, rows, width = source.shape
    nf, rows2, width2 = cotan.shape
    c1 = first_kernel.shape[0]
    c2 = nf * n_sy
    own2 = rows // 2
    pairs = 14
    scale = 1.0 / math.sqrt(
        lax.axis_size("rep") * n_sx * n_sy * (planes // 2) * own2 * (width // 2)
    )
    me = sy.astype(jnp.int32).reshape(1)
    place = jnp.stack(
        [
            jnp.asarray(v, jnp.int32)
            for v in (odd_x, sy > 0, sy < n_sy - 1, sx, rep, (sx > 0) & (sx < n_sx - 1))
        ]
    )
    rim = 3

    w1 = first_kernel.transpose(2, 3, 4, 1, 0)
    w1q = jnp.concatenate(
        [
            jnp.pad(w1, ((0, 0), (0, 0), (0, 1), (0, 0), (0, 0))),
            jnp.pad(w1, ((0, 0), (0, 0), (1, 0), (0, 0), (0, 0))),
        ],
        axis=-1,
    )
    bias4 = jnp.tile(first_bias, 4)[:, None]
    w2 = second_kernel.transpose(2, 3, 4, 0, 1).reshape(27, nf, c1)
    vt, cp, w2p = call(
        prep_body,
        "prep",
        [
            jax.ShapeDtypeStruct((planes, rows, cin, width), BF),
            jax.ShapeDtypeStruct((n_sy, own2 + 2, nf, width2), BF),
            jax.ShapeDtypeStruct((pairs, nf, 2 * c1), BF),
        ],
        [pltpu.VMEM((rows2 + 2, nf, width2), BF)],
        (me, source, cotan, w2),
        smem_ins=1,
        flops=1 << 30,
    )

    edge_lo, edge_hi = vt[:, :rim], vt[:, rows - rim :]
    ya = swap_first(jnp.where(odd_y == 1, edge_lo, edge_hi), "sy")
    yb = swap_second(jnp.where(odd_y == 1, edge_hi, edge_lo), "sy")
    yb = jnp.where((sy > 0) & (sy < n_sy - 1), yb, jnp.zeros_like(yb))
    rim_lo = jnp.where(odd_y == 1, ya, yb)
    rim_hi = jnp.where(odd_y == 1, yb, ya)
    vr = jnp.concatenate([rim_lo, vt, rim_hi], axis=1)
    za = swap_first(jnp.where(odd_x == 1, vr[0], vr[planes - 1]), "sx")
    zb = swap_second(jnp.where(odd_x == 1, vr[planes - 1], vr[0]), "sx")

    co = jnp.stack([cp[0]] + [to_partner(cp[s], "sy", s) for s in range(1, n_sy)])
    ca = swap_first(co, "sx")
    cb = swap_second(co, "sx")
    w2p, vr = lax.optimization_barrier((w2p, vr))
    w2r = jnp.stack([w2p] + [to_partner(w2p, "sy", s) for s in range(1, n_sy)])

    cells, mask, pooled = call(
        conv1_body,
        "conv1",
        [
            jax.ShapeDtypeStruct((planes + 2, rows + 2 * rim, 4 * cin, width // 2), BF),
            jax.ShapeDtypeStruct((2, own2, 4 * c1, width // 2), BF),
            jax.ShapeDtypeStruct((own2 + 2, c1, width // 2), BF),
        ],
        [pltpu.VMEM((3, 4 * c1, 16 * cin), BF)],
        (place, vr, za, zb, w1q, bias4),
        smem_ins=1,
        flops=3 << 30,
    )
    ua = swap_first(pooled, "sx")
    ub = swap_second(pooled, "sx")

    ca, cb, ua, ub = lax.optimization_barrier((ca, cb, ua, ub))

    plane_shape = (own2 + 2, 3, c2, width2)
    wb, own_back, own_g2, own_b2 = call(
        own_body,
        "backward_own",
        [
            jax.ShapeDtypeStruct((3, c1, 9 * c2), BF),
            jax.ShapeDtypeStruct((own2 // 2, c1, 2 * width2), F32),
            jax.ShapeDtypeStruct((9, c2, 2 * c1), F32),
            jax.ShapeDtypeStruct((c2, 2 * c1), F32),
        ],
        [pltpu.VMEM(plane_shape, BF)],
        (co, pooled, w2r),
        flops=2 << 30,
    )
    hp = pairs // 2
    share = (c2 + cin) // n_sx
    half_shape = jax.ShapeDtypeStruct((n_sx, hp, share, 2 * c1), F32)
    keep, send = call(
        back_body,
        "backward",
        [half_shape, half_shape],
        [
            pltpu.VMEM(plane_shape, BF),
            pltpu.VMEM(plane_shape, BF),
            pltpu.VMEM((2, own2 // 2, 4 * c1, width), BF),
            pltpu.VMEM((27, c2, 2 * c1), F32),
            pltpu.VMEM((2, *half_shape.shape), F32),
        ],
        (place, cells, mask, pooled, ca, cb, wb, own_back, own_g2, own_b2),
        smem_ins=1,
        flops=5 << 30,
    )

    half = keep + swap_first(send, "rep")
    half, ua, ub = lax.optimization_barrier((half, ua, ub))
    pieces = call(
        conv2_body,
        "conv2",
        jax.ShapeDtypeStruct((n_sy, own2, nf, width2), BF),
        [pltpu.VMEM((3, own2 + 2, 3, c1, width2), BF)],
        (place, pooled, ua, ub, w2r),
        smem_ins=1,
        flops=1 << 30,
    )
    part = tree_sum(
        [half[0]]
        + [to_partner(half[s].astype(BF), "sx", s).astype(F32) for s in range(1, n_sx)]
    )
    own_rows = own2 * nf
    share2, share1 = nf // n_sx, cin // n_sx
    part_bf = part.astype(BF)
    tail = part_bf[:, n_sy * share2 :]

    def sy_message(s):
        w2_rows = part_bf[:, s * share2 : (s + 1) * share2]
        return jnp.concatenate(
            [
                pieces[s].reshape(own_rows, width2),
                jnp.concatenate([w2_rows, tail], axis=1).reshape(-1, width2),
            ],
            axis=0,
        )

    own_piece = pieces[0].reshape(own_rows, width2)
    passed = [to_partner(sy_message(s), "sy", s) for s in range(1, n_sy)]
    bias_wide = jnp.broadcast_to(second_bias[:, None, None], (nf, 1, width2))
    second_out = call(
        unpack_body,
        "unpack",
        jax.ShapeDtypeStruct((nf, rows2, width2), F32),
        [],
        (me, own_piece, *passed, bias_wide),
        smem_ins=1,
        flops=1 << 28,
    )
    sums = [g[own_rows:].reshape(hp, share2 + share1, width2).astype(F32) for g in passed]
    own = jnp.concatenate([part[:, :share2], tail.astype(F32)], axis=1)
    total = (tree_sum([own] + sums) * scale).astype(BF)
    spread = jnp.stack([total] + [to_partner(total, "sx", s) for s in range(1, n_sx)])
    spread, second_out = lax.optimization_barrier((spread, second_out))
    other = swap_first(spread, "rep")
    g2, t2, g1, t1 = call(
        finish_body,
        "finish",
        [
            jax.ShapeDtypeStruct((27, nf, c1), F32),
            jax.ShapeDtypeStruct((nf, c1), F32),
            jax.ShapeDtypeStruct((27, cin, c1), F32),
            jax.ShapeDtypeStruct((1, c1), F32),
        ],
        [],
        (place, spread, other),
        smem_ins=1,
        flops=1 << 20,
    )
    return (
        second_out[None, :, None],
        g1.reshape(3, 3, 3, cin, c1).transpose(4, 3, 0, 1, 2),
        t1[0],
        g2.reshape(3, 3, 3, nf, c1).transpose(3, 4, 0, 1, 2),
        t2[:, 0],
    )


def solution(mesh):
    placed = (
        P("rep", None, "sx", "sy", None),
        P(),
        P(),
        P("sy", None, None, None, None),
        P("sy"),
        P("rep", "sy", "sx", None, None),
    )
    return jax.shard_map(
        per_device,
        mesh=mesh,
        in_specs=placed,
        out_specs=(
            P("rep", "sy", "sx", None, None),
            P(),
            P(),
            P("sy", None, None, None, None),
            P("sy"),
        ),
        check_vma=False,
    )
```

time: 81.8 us -> 74.5 us (0.911)
  starting transfers between devices: 45.5 us -> 32.3 us
  Pallas kernels: 12.6 us -> 16.5 us
  waiting for transfers between devices: 16.7 us -> 19.9 us
  other arithmetic: 1.84 us -> 0.71 us
    ppermute x7 -> x6, starting transfers between devices: 16.2 us -> 9.9 us  [swap_first(): return lax.ppermute(value, axis, [(i, i ^ 1) for i in range(count)])]
    ppermute x15, starting transfers between devices: 26 us -> 21.9 us  [to_partner(): return lax.ppermute(value, axis, [(i, i ^ s) for i in range(count)])]
    pallas_call x5 -> x7, Pallas kernels: 12.6 us -> 16.5 us  [call(): pl.pallas_call(body, name=name, out_shape=outs, in_specs=[sm] * smem_ins...]
    ppermute x5 -> x4, starting transfers between devices: 3.3 us -> 0.58 us  [swap_second(): return lax.ppermute(value, (axis, 'rep'), pairs)]
    ppermute x15, waiting for transfers between devices: 12.7 us -> 15 us  [to_partner(): return lax.ppermute(value, axis, [(i, i ^ s) for i in range(count)])]
    squeeze x3 -> x0, local copies, waits for them, and re-layouts: 1.12 us -> none  [the longest x1 0.59 us: per_device(): t1[0]]
    concatenate x6, other arithmetic: 1.22 us -> 0.14 us  [the longest x1 0.09 us: per_device(): vr = jnp.concatenate([rim_lo, vt, rim_hi], axis=1)]
    ppermute x7 -> x6, waiting for transfers between devices: 3.93 us -> 4.85 us  [swap_first(): return lax.ppermute(value, axis, [(i, i ^ 1) for i in range(count)])]
  transfers between devices with their start and end apart: 27 -> 25, of which waited for: 8 -> 11; matrix products, arithmetic and copies ran while one was open for 1% -> 1% of each run, Pallas kernels for 6% -> 11%
where the time goes in v2:
time: 74.5 us; the launch traced here: 74.3 us
  starting transfers between devices  32.3 us (43%)
  waiting for transfers between devices  19.9 us (27%)
  Pallas kernels  16.5 us (22%)
  local copies, waits for them, and re-layouts  3.95 us (5%)
  between operations  0.94 us (1%)
    ppermute x15, starting transfers between devices, to_partner(): return lax.ppermute(value, axis, [(i, i ^ s) for i in range(count)])  21.9 us
    pallas_call x7, Pallas kernels, call(): pl.pallas_call(body, name=name, out_shape=outs, in_specs=[sm] * smem_ins...  16.5 us
    ppermute x15, waiting for transfers between devices, to_partner(): return lax.ppermute(value, axis, [(i, i ^ s) for i in range(count)])  15 us
    ppermute x6, starting transfers between devices, swap_first(): return lax.ppermute(value, axis, [(i, i ^ 1) for i in range(count)])  9.9 us
    ppermute x6, waiting for transfers between devices, swap_first(): return lax.ppermute(value, axis, [(i, i ^ 1) for i in range(count)])  4.85 us
    unnamed x12, local copies, waits for them, and re-layouts  2.93 us
  transfers between devices with their start and end apart: 25, of which 11 were waited for; matrix products, arithmetic and copies ran while one was open for 1% of the time, Pallas kernels for 11%

profile of v2, /device:TPU:0, one launch (start us, length us, event | category | flops | bytes accessed | tf_op | source)
XLA Modules:
  0.0 74.3 jit_solution(16437994958255111868)
XLA Ops:
  0.7 1.0 %copy-done = bf16[1,32,2,16,256]{4,3,2,1,0:T(8,128)(2,1)S(1)} copy-done((bf16[1,32,2,16,256]{4,3,2,1,0:T(8,128)(2,1)S(1)}, bf16[1,32,2,16,256]{4,3,2,1,0:T(8,128)(2,1)}, u32[]{:S(2)}) %copy-start) | copy-done | bytes 524312
  1.7 0.9 %copy-done.1 = bf16[1,32,1,32,128]{4,3,2,1,0:T(8,128)(2,1)S(1)} copy-done((bf16[1,32,1,32,128]{4,3,2,1,0:T(8,128)(2,1)S(1)}, bf16[1,32,1,32,128]{4,3,2,1,0:T(8,128)(2,1)}, u32[]{:S(2)}) %copy-start.1) | copy-done | bytes 262168
  2.7 0.9 %copy-done.2 = bf16[32,64,3,3,3]{1,0,4,3,2:T(8,128)(2,1)S(1)} copy-done((bf16[32,64,3,3,3]{1,0,4,3,2:T(8,128)(2,1)S(1)}, bf16[32,64,3,3,3]{1,0,4,3,2:T(8,128)(2,1)}, u32[]{:S(2)}) %copy-start.2) | copy-done | bytes 110616
  3.6 1.3 %prep.1 = (bf16[2,16,32,256]{3,2,1,0:T(8,128)(2,1)S(1)}, bf16[4,10,32,128]{3,2,1,0:T(8,128)(2,1)S(1)}, bf16[14,32,128]{2,1,0:T(8,128)(2,1)S(1)}) custom-call(s32[1]{0:T(128)} %bitcast.6.me, bf16[32,2,16,256]{3,2,1,0:T(8,128)(2,1)S(1)} %bitcast.71, bf16[32,32,128]{2,1,0:T(8,128)(2,1)S(1)} %bitcast.72, bf16[27,32,64]{2,1,0:T(8,128)(2,1)S(1)} %bitcast.73), custom_call_target="tpu_custom_call" | custom-call | flops 1073741824 | bytes 1048576 | tf_op jit(solution)/shard_map/prep/pallas_call | solution.py:59
  4.9 0.0 copy-start.3
  4.9 3.0 %collective-permute-start = (bf16[2,3,32,256]{3,2,1,0:T(8,128)(2,1)S(1)}, bf16[2,3,32,256]{3,2,1,0:T(8,128)(2,1)S(1)}, u32[]{:S(2)}, u32[]{:S(2)}) collective-permute-start(bf16[2,3,32,256]{3,2,1,0:T(8,128)(2,1)S(1)} %get-tuple-element.74), channel_id=1, source_target_pairs={{0,2},{2,0},{4,6},{6,4},{1,3},{3,1},{5,7},{7,5},{8,10},{10,8},{12,... | collective-permute-start | bytes 294920 | tf_op jit(solution)/shard_map/ppermute | solution.py:403
  7.9 0.0 collective-permute-start.1
  8.0 3.0 %collective-permute-start.4 = (bf16[10,32,128]{2,1,0:T(8,128)(2,1)S(1)}, bf16[10,32,128]{2,1,0:T(8,128)(2,1)S(1)}, u32[]{:S(2)}, u32[]{:S(2)}) collective-permute-start(bf16[10,32,128]{2,1,0:T(8,128)(2,1)S(1)} %get-tuple-element.78), channel_id=1, source_target_pairs={{0,2},{2,0},{4,6},{6,4},{1,3},{3,1},{5,7},{7,5},{8,10},{10,8},{12,... | collective-permute-start | bytes 245768 | tf_op jit(solution)/shard_map/ppermute | solution.py:421
  11.0 0.0 collective-permute-start.5
  11.0 1.5 %collective-permute-start.6 = (bf16[10,32,128]{2,1,0:T(8,128)(2,1)S(1)}, bf16[10,32,128]{2,1,0:T(8,128)(2,1)S(1)}, u32[]{:S(2)}, u32[]{:S(2)}) collective-permute-start(bf16[10,32,128]{2,1,0:T(8,128)(2,1)S(1)} %get-tuple-element.76), channel_id=1, source_target_pairs={{0,6},{2,4},{4,2},{6,0},{1,7},{3,5},{5,3},{7,1},{8,14},{10,12},{12... | collective-permute-start | bytes 245768 | tf_op jit(solution)/shard_map/ppermute | solution.py:421
  12.5 0.1 broadcast_in_dim_tile.4.bias
  12.7 0.1 stack.79.place
  12.8 0.0 collective-permute-done
  12.8 0.0 collective-permute-done.1
  12.8 0.1 pad_maximum_fusion.vr
  12.9 0.1 select_bitcast_fusion
  13.0 1.6 %collective-permute-start.2 = (bf16[22,32,256]{2,1,0:T(8,128)(2,1)S(1)}, bf16[22,32,256]{2,1,0:T(8,128)(2,1)S(1)}, u32[]{:S(2)}, u32[]{:S(2)}) collective-permute-start(bf16[22,32,256]{2,1,0:T(8,128)(2,1)S(1)} %get-tuple-element.72), channel_id=1, source_target_pairs={{0,8},{8,0},{16,24},{24,16},{1,9},{9,1},{17,25},{25,17},{2,10},{10... | collective-permute-start | bytes 1081352 | tf_op jit(solution)/shard_map/ppermute | solution.py:403
  14.6 0.0 collective-permute-start.3
  14.6 0.2 fusion.2.w1q
  14.8 1.0 %collective-permute-done.4 = bf16[10,32,128]{2,1,0:T(8,128)(2,1)S(1)} collective-permute-done((bf16[10,32,128]{2,1,0:T(8,128)(2,1)S(1)}, bf16[10,32,128]{2,1,0:T(8,128)(2,1)S(1)}, u32[]{:S(2)}, u32[]{:S(2)}) %collective-permute-start.4) | collective-permute-done | bytes 81952 | tf_op jit(solution)/shard_map/ppermute | solution.py:421
  15.8 3.1 %collective-permute-start.11 = (bf16[14,32,128]{2,1,0:T(8,128)(2,1)S(1)}, bf16[14,32,128]{2,1,0:T(8,128)(2,1)S(1)}, u32[]{:S(2)}, u32[]{:S(2)}) collective-permute-start(bf16[14,32,128]{2,1,0:T(8,128)(2,1)S(1)} %get-tuple-element.41), channel_id=1, source_target_pairs={{0,2},{2,0},{4,6},{6,4},{1,3},{3,1},{5,7},{7,5},{8,10},{10,8},{12,... | collective-permute-start | bytes 344072 | tf_op jit(solution)/shard_map/ppermute | solution.py:421
  18.8 0.0 collective-permute-done.5
  18.8 0.0 collective-permute-start.12
  18.8 0.0 collective-permute-done.6
  18.9 1.5 %collective-permute-start.13 = (bf16[14,32,128]{2,1,0:T(8,128)(2,1)S(1)}, bf16[14,32,128]{2,1,0:T(8,128)(2,1)S(1)}, u32[]{:S(2)}, u32[]{:S(2)}) collective-permute-start(bf16[14,32,128]{2,1,0:T(8,128)(2,1)S(1)} %get-tuple-element.41), channel_id=1, source_target_pairs={{0,6},{2,4},{4,2},{6,0},{1,7},{3,5},{5,3},{7,1},{8,14},{10,12},{12... | collective-permute-start | bytes 344072 | tf_op jit(solution)/shard_map/ppermute | solution.py:421
  20.4 2.2 %collective-permute-done.11 = bf16[14,32,128]{2,1,0:T(8,128)(2,1)S(1)} collective-permute-done((bf16[14,32,128]{2,1,0:T(8,128)(2,1)S(1)}, bf16[14,32,128]{2,1,0:T(8,128)(2,1)S(1)}, u32[]{:S(2)}, u32[]{:S(2)}) %collective-permute-start.11) | collective-permute-done | bytes 114720 | tf_op jit(solution)/shard_map/ppermute | solution.py:421
  22.7 2.2 %collective-permute-start.7 = (bf16[4,10,32,128]{3,2,1,0:T(8,128)(2,1)S(1)}, bf16[4,10,32,128]{3,2,1,0:T(8,128)(2,1)S(1)}, u32[]{:S(2)}, u32[]{:S(2)}) collective-permute-start(bf16[4,10,32,128]{3,2,1,0:T(8,128)(2,1)S(1)} %pad_maximum_fusion.2.co), channel_id=1, source_target_pairs={{0,8},{8,0},{16,24},{24,16},{1,9},{9,1},{17,25},{25,17},{2,10},{10... | collective-permute-start | bytes 983048 | tf_op jit(solution)/shard_map/ppermute | solution.py:403
  24.8 1.8 %collective-permute-done.12 = bf16[14,32,128]{2,1,0:T(8,128)(2,1)S(1)} collective-permute-done((bf16[14,32,128]{2,1,0:T(8,128)(2,1)S(1)}, bf16[14,32,128]{2,1,0:T(8,128)(2,1)S(1)}, u32[]{:S(2)}, u32[]{:S(2)}) %collective-permute-start.12) | collective-permute-done | bytes 114720 | tf_op jit(solution)/shard_map/ppermute | solution.py:421
  26.6 0.0 collective-permute-start.8
  26.6 0.0 collective-permute-done.13
  26.6 0.1 pad_maximum_fusion.1.w2r
  26.7 0.0 collective-permute-done.2.za
  26.7 3.5 %conv1.1 = (bf16[4,22,128,128]{3,2,1,0:T(8,128)(2,1)S(1)}, bf16[2,8,256,128]{3,2,1,0:T(8,128)(2,1)S(1)}, bf16[10,64,128]{2,1,0:T(8,128)(2,1)S(1)}) custom-call(s32[6]{0:T(128)S(1)} %stack.79.place, bf16[2,22,32,256]{3,2,1,0:T(8,128)(2,1)S(1)} %pad_maximum_fusion.vr, bf16[22,32,256]{2,1,0:T(8,128)(2,1)S(1)} %collective-permute-done.2.za, ...), custom_call_target="tpu_custom_call" | custom-call | flops 3221225472 | bytes 1048576 | tf_op jit(solution)/shard_map/conv1/pallas_call | solution.py:59
  30.1 0.6 collective-permute-start.10
  30.7 3.0 %collective-permute-start.9 = (bf16[10,64,128]{2,1,0:T(8,128)(2,1)S(1)}, bf16[10,64,128]{2,1,0:T(8,128)(2,1)S(1)}, u32[]{:S(2)}, u32[]{:S(2)}) collective-permute-start(bf16[10,64,128]{2,1,0:T(8,128)(2,1)S(1)} %get-tuple-element.37.pooled.ur), channel_id=1, source_target_pairs={{0,8},{8,0},{16,24},{24,16},{1,9},{9,1},{17,25},{25,17},{2,10},{10... | collective-permute-start | bytes 491528 | tf_op jit(solution)/shard_map/ppermute | solution.py:403
  33.7 1.7 %backward_own.1 = (bf16[3,64,1152]{2,1,0:T(8,128)(2,1)S(1)}, f32[4,64,256]{2,1,0:T(8,128)S(1)}, f32[9,128,128]{2,1,0:T(8,128)S(1)}, f32[128,128]{1,0:T(8,128)S(1)}) custom-call(bf16[4,10,32,128]{3,2,1,0:T(8,128)(2,1)S(1)} %pad_maximum_fusion.2.co, bf16[10,64,128]{2,1,0:T(8,128)(2,1)S(1)} %get-tuple-element.37.pooled.ur, ...), custom_call_target="tpu_custom_call" | custom-call | flops 2147483648 | bytes 1048576 | tf_op jit(solution)/shard_map/backward_own/pallas_call | solution.py:59
  35.4 0.0 collective-permute-done.7.ca
  35.4 0.0 collective-permute-done.10.ub
  35.4 1.6 %collective-permute-done.9.ua = bf16[10,64,128]{2,1,0:T(8,128)(2,1)S(1)} collective-permute-done((bf16[10,64,128]{2,1,0:T(8,128)(2,1)S(1)}, bf16[10,64,128]{2,1,0:T(8,128)(2,1)S(1)}, u32[]{:S(2)}, u32[]{:S(2)}) %collective-permute-start.9) | collective-permute-done | bytes 163872 | tf_op jit(solution)/shard_map/ppermute | solution.py:403
  37.0 5.8 %backward.1 = (f32[4,7,40,128]{3,2,1,0:T(8,128)S(1)}, f32[4,7,40,128]{3,2,1,0:T(8,128)S(1)}) custom-call(s32[6]{0:T(128)S(1)} %stack.79.place, bf16[4,22,128,128]{3,2,1,0:T(8,128)(2,1)S(1)} %get-tuple-element.35.cells, bf16[2,8,256,128]{3,2,1,0:T(8,128)(2,1)S(1)} %get-tuple-element.36.mask, bf16[10,64,128]{2,1,0:T(8,128)(2,1)S(1)} %get-tuple-element.37.pooled.ur, ...), custom_call_target="tpu_custom_call" | custom-call | flops 5368709120 | bytes 1048576 | tf_op jit(solution)/shard_map/backward/pallas_call | solution.py:59
  42.7 0.1 collective-permute-start.14
  42.8 2.0 %collective-permute-done.14 = f32[4,7,40,128]{3,2,1,0:T(8,128)S(1)} collective-permute-done((f32[4,7,40,128]{3,2,1,0:T(8,128)S(1)}, f32[4,7,40,128]{3,2,1,0:T(8,128)S(1)}, u32[]{:S(2)}, u32[]{:S(2)}) %collective-permute-start.14) | collective-permute-done | bytes 573472 | tf_op jit(solution)/shard_map/ppermute | solution.py:403
  44.8 0.1 add.65
  44.9 2.1 %collective-permute-start.15 = (bf16[7,40,128]{2,1,0:T(8,128)(2,1)S(1)}, bf16[7,40,128]{2,1,0:T(8,128)(2,1)S(1)}, u32[]{:S(2)}, u32[]{:S(2)}) collective-permute-start(bf16[7,40,128]{2,1,0:T(8,128)(2,1)S(1)} %get-tuple-element.79), channel_id=1, source_target_pairs={{0,8},{8,0},{16,24},{24,16},{1,9},{9,1},{17,25},{25,17},{2,10},{10... | collective-permute-start | bytes 215048 | tf_op jit(solution)/shard_map/ppermute | solution.py:421
  47.0 0.9 %collective-permute-start.16 = (bf16[7,40,128]{2,1,0:T(8,128)(2,1)S(1)}, bf16[7,40,128]{2,1,0:T(8,128)(2,1)S(1)}, u32[]{:S(2)}, u32[]{:S(2)}) collective-permute-start(bf16[7,40,128]{2,1,0:T(8,128)(2,1)S(1)} %get-tuple-element.81), channel_id=1, source_target_pairs={{0,16},{8,24},{16,0},{24,8},{1,17},{9,25},{17,1},{25,9},{2,18},{10... | collective-permute-start | bytes 215048 | tf_op jit(solution)/shard_map/ppermute | solution.py:421
  48.0 1.5 %collective-permute-start.17 = (bf16[7,40,128]{2,1,0:T(8,128)(2,1)S(1)}, bf16[7,40,128]{2,1,0:T(8,128)(2,1)S(1)}, u32[]{:S(2)}, u32[]{:S(2)}) collective-permute-start(bf16[7,40,128]{2,1,0:T(8,128)(2,1)S(1)} %get-tuple-element.80), channel_id=1, source_target_pairs={{0,24},{8,16},{16,8},{24,0},{1,25},{9,17},{17,9},{25,1},{2,26},{10... | collective-permute-start | bytes 215048 | tf_op jit(solution)/shard_map/ppermute | solution.py:421
  49.5 1.6 %conv2.1 = bf16[4,8,32,128]{3,2,1,0:T(8,128)(2,1)S(1)} custom-call(s32[6]{0:T(128)S(1)} %stack.79.place, bf16[10,64,128]{2,1,0:T(8,128)(2,1)S(1)} %get-tuple-element.37.pooled.ur, bf16[10,64,128]{2,1,0:T(8,128)(2,1)S(1)} %collective-permute-done.9.ua, bf16[10,64,128]{2,1,0:T(8,128)(2,1)S(1)} %collective-permute-done.10.ub, ...), custom_call_target="tpu_custom_call" | custom-call | flops 1073741824 | bytes 1048576 | tf_op jit(solution)/shard_map/conv2/pallas_call | solution.py:59
  51.1 3.9 %collective-permute-done.16 = bf16[7,40,128]{2,1,0:T(8,128)(2,1)S(1)} collective-permute-done((bf16[7,40,128]{2,1,0:T(8,128)(2,1)S(1)}, bf16[7,40,128]{2,1,0:T(8,128)(2,1)S(1)}, u32[]{:S(2)}, u32[]{:S(2)}) %collective-permute-start.16) | collective-permute-done | bytes 71712 | tf_op jit(solution)/shard_map/ppermute | solution.py:421
  55.1 0.8 %collective-permute-start.18 = (bf16[368,128]{1,0:T(8,128)(2,1)S(1)}, bf16[368,128]{1,0:T(8,128)(2,1)S(1)}, u32[]{:S(2)}, u32[]{:S(2)}) collective-permute-start(bf16[368,128]{1,0:T(8,128)(2,1)S(1)} %pad_maximum_fusion.4), channel_id=1, source_target_pairs={{0,2},{2,0},{4,6},{6,4},{1,3},{3,1},{5,7},{7,5},{8,10},{10,8},{12,... | collective-permute-start | bytes 282632 | tf_op jit(solution)/shard_map/ppermute | solution.py:421
  55.9 0.2 collective-permute-start.19
  56.1 2.7 %collective-permute-start.20 = (bf16[368,128]{1,0:T(8,128)(2,1)S(1)}, bf16[368,128]{1,0:T(8,128)(2,1)S(1)}, u32[]{:S(2)}, u32[]{:S(2)}) collective-permute-start(bf16[368,128]{1,0:T(8,128)(2,1)S(1)} %pad_maximum_fusion.6), channel_id=1, source_target_pairs={{0,6},{2,4},{4,2},{6,0},{1,7},{3,5},{5,3},{7,1},{8,14},{10,12},{12... | collective-permute-start | bytes 282632 | tf_op jit(solution)/shard_map/ppermute | solution.py:421
  58.8 1.8 %collective-permute-done.18.refs_1_ = bf16[368,128]{1,0:T(8,128)(2,1)S(1)} collective-permute-done((bf16[368,128]{1,0:T(8,128)(2,1)S(1)}, bf16[368,128]{1,0:T(8,128)(2,1)S(1)}, u32[]{:S(2)}, u32[]{:S(2)}) %collective-permute-start.18) | collective-permute-done | bytes 94240 | tf_op jit(solution)/shard_map/ppermute | solution.py:421
  60.6 1.6 %collective-permute-done.19.refs_2_ = bf16[368,128]{1,0:T(8,128)(2,1)S(1)} collective-permute-done((bf16[368,128]{1,0:T(8,128)(2,1)S(1)}, bf16[368,128]{1,0:T(8,128)(2,1)S(1)}, u32[]{:S(2)}, u32[]{:S(2)}) %collective-permute-start.19) | collective-permute-done | bytes 94240 | tf_op jit(solution)/shard_map/ppermute | solution.py:421
  62.3 1.8 %collective-permute-start.21 = (bf16[7,16,128]{2,1,0:T(8,128)(2,1)S(1)}, bf16[7,16,128]{2,1,0:T(8,128)(2,1)S(1)}, u32[]{:S(2)}, u32[]{:S(2)}) collective-permute-start(bf16[7,16,128]{2,1,0:T(8,128)(2,1)S(1)} %fusion.9), channel_id=1, source_target_pairs={{0,8},{8,0},{16,24},{24,16},{1,9},{9,1},{17,25},{25,17},{2,10},{10... | collective-permute-start | bytes 86024 | tf_op jit(solution)/shard_map/ppermute | solution.py:421
  64.1 0.9 %collective-permute-start.22 = (bf16[7,16,128]{2,1,0:T(8,128)(2,1)S(1)}, bf16[7,16,128]{2,1,0:T(8,128)(2,1)S(1)}, u32[]{:S(2)}, u32[]{:S(2)}) collective-permute-start(bf16[7,16,128]{2,1,0:T(8,128)(2,1)S(1)} %fusion.9), channel_id=1, source_target_pairs={{0,16},{8,24},{16,0},{24,8},{1,17},{9,25},{17,1},{25,9},{2,18},{10... | collective-permute-start | bytes 86024 | tf_op jit(solution)/shard_map/ppermute | solution.py:421
  65.0 1.8 %collective-permute-start.23 = (bf16[7,16,128]{2,1,0:T(8,128)(2,1)S(1)}, bf16[7,16,128]{2,1,0:T(8,128)(2,1)S(1)}, u32[]{:S(2)}, u32[]{:S(2)}) collective-permute-start(bf16[7,16,128]{2,1,0:T(8,128)(2,1)S(1)} %fusion.9), channel_id=1, source_target_pairs={{0,24},{8,16},{16,8},{24,0},{1,25},{9,17},{17,9},{25,1},{2,26},{10... | collective-permute-start | bytes 86024 | tf_op jit(solution)/shard_map/ppermute | solution.py:421
  66.8 0.1 broadcast_in_dim.13.refs_4_
  66.9 1.1 %unpack.1 = f32[32,32,128]{2,1,0:T(8,128)} custom-call(s32[1]{0:T(128)} %bitcast.6.me, bf16[256,128]{1,0:T(8,128)(2,1)S(1)} %bitcast.70, bf16[368,128]{1,0:T(8,128)(2,1)S(1)} %collective-permute-done.18.refs_1_, bf16[368,128]{1,0:T(8,128)(2,1)S(1)} %collective-permute-done.19.refs_2_, bf16[368,128]{1,0:T(8,128)(2,1)S(1)} %collective-permute-done.20.refs_3_, ...), custom_call_target="tpu_custom_call" | custom-call | flops 268435456 | bytes 1048576 | tf_op jit(solution)/shard_map/unpack/pallas_call | solution.py:59
  68.0 1.0 %collective-permute-done.22 = bf16[7,16,128]{2,1,0:T(8,128)(2,1)S(1)} collective-permute-done((bf16[7,16,128]{2,1,0:T(8,128)(2,1)S(1)}, bf16[7,16,128]{2,1,0:T(8,128)(2,1)S(1)}, u32[]{:S(2)}, u32[]{:S(2)}) %collective-permute-start.22) | collective-permute-done | bytes 28704 | tf_op jit(solution)/shard_map/ppermute | solution.py:421
  69.0 1.6 %collective-permute-done.23 = bf16[7,16,128]{2,1,0:T(8,128)(2,1)S(1)} collective-permute-done((bf16[7,16,128]{2,1,0:T(8,128)(2,1)S(1)}, bf16[7,16,128]{2,1,0:T(8,128)(2,1)S(1)}, u32[]{:S(2)}, u32[]{:S(2)}) %collective-permute-start.23) | collective-permute-done | bytes 28704 | tf_op jit(solution)/shard_map/ppermute | solution.py:421
  70.7 0.1 collective-permute-start.24
  70.7 1.3 %collective-permute-done.24.other = bf16[4,7,16,128]{3,2,1,0:T(8,128)(2,1)S(1)} collective-permute-done((bf16[4,7,16,128]{3,2,1,0:T(8,128)(2,1)S(1)}, bf16[4,7,16,128]{3,2,1,0:T(8,128)(2,1)S(1)}, u32[]{:S(2)}, u32[]{:S(2)}) %collective-permute-start.24) | collective-permute-done | bytes 114720 | tf_op jit(solution)/shard_map/ppermute | solution.py:403
  72.1 1.6 %finish.1 = (f32[27,32,64]{2,1,0:T(8,128)}, f32[32,64]{1,0:T(8,128)S(1)}, f32[27,32,64]{2,1,0:T(8,128)}, f32[1,64]{1,0:T(1,128)}) custom-call(s32[6]{0:T(128)S(1)} %stack.79.place, bf16[4,7,16,128]{3,2,1,0:T(8,128)(2,1)S(1)} %pad_maximum_fusion.3.mine, bf16[4,7,16,128]{3,2,1,0:T(8,128)(2,1)S(1)} %collective-permute-done.24.other), custom_call_target="tpu_custom_call" | custom-call | flops 1048576 | bytes 1048576 | tf_op jit(solution)/shard_map/finish/pallas_call | solution.py:59
  73.7 0.6 slice_reduce_fusion
  (35 shorter events, 0.4 us)
Async XLA Ops:
  0.6 11.9 %copy-start.4 = (f32[64]{0:T(128)S(1)}, f32[64]{0:T(128)}, u32[]{:S(2)}) copy-start(f32[64]{0:T(128)} %param.8) | copy-start | bytes 772
  0.7 1.0 %copy-start = (bf16[1,32,2,16,256]{4,3,2,1,0:T(8,128)(2,1)S(1)}, bf16[1,32,2,16,256]{4,3,2,1,0:T(8,128)(2,1)}, u32[]{:S(2)}) copy-start(bf16[1,32,2,16,256]{4,3,2,1,0:T(8,128)(2,1)} %param.6) | copy-start | bytes 1572868
  1.7 0.9 %copy-start.1 = (bf16[1,32,1,32,128]{4,3,2,1,0:T(8,128)(2,1)S(1)}, bf16[1,32,1,32,128]{4,3,2,1,0:T(8,128)(2,1)}, u32[]{:S(2)}) copy-start(bf16[1,32,1,32,128]{4,3,2,1,0:T(8,128)(2,1)} %param.11) | copy-start | bytes 786436
  2.6 0.9 %copy-start.2 = (bf16[32,64,3,3,3]{1,0,4,3,2:T(8,128)(2,1)S(1)}, bf16[32,64,3,3,3]{1,0,4,3,2:T(8,128)(2,1)}, u32[]{:S(2)}) copy-start(bf16[32,64,3,3,3]{1,0,4,3,2:T(8,128)(2,1)} %param.9) | copy-start | bytes 331780
  4.9 9.7 %copy-start.3 = (bf16[64,32,3,3,3]{0,1,4,3,2:T(8,128)(2,1)S(1)}, bf16[64,32,3,3,3]{0,1,4,3,2:T(8,128)(2,1)}, u32[]{:S(2)}) copy-start(bf16[64,32,3,3,3]{0,1,4,3,2:T(8,128)(2,1)} %param.7) | copy-start | bytes 331780
  4.9 7.9 %collective-permute-start = (bf16[2,3,32,256]{3,2,1,0:T(8,128)(2,1)S(1)}, bf16[2,3,32,256]{3,2,1,0:T(8,128)(2,1)S(1)}, u32[]{:S(2)}, u32[]{:S(2)}) collective-permute-start(bf16[2,3,32,256]{3,2,1,0:T(8,128)(2,1)S(1)} %get-tuple-element.74), channel_id=1, source_target_pairs={{0,2},{2,0},{4,6},{6,4},{1,3},{3,1},{5,7},{7,5},{8,10},{10,8},{12,... | collective-permute-start | bytes 294920 | tf_op jit(solution)/shard_map/ppermute | solution.py:403
  7.9 4.9 %collective-permute-start.1 = (bf16[2,3,32,256]{3,2,1,0:T(8,128)(2,1)S(1)}, bf16[2,3,32,256]{3,2,1,0:T(8,128)(2,1)S(1)}, u32[]{:S(2)}, u32[]{:S(2)}) collective-permute-start(bf16[2,3,32,256]{3,2,1,0:T(8,128)(2,1)S(1)} %get-tuple-element.73), channel_id=1, source_target_pairs={{0,1},{1,0},{2,4},{3,5},{4,2},{5,3},{6,7},{7,6},{8,9},{9,8},{10,12... | collective-permute-start | bytes 294920 | tf_op jit(solution)/shard_map/ppermute | solution.py:416
  8.0 7.8 %collective-permute-start.4 = (bf16[10,32,128]{2,1,0:T(8,128)(2,1)S(1)}, bf16[10,32,128]{2,1,0:T(8,128)(2,1)S(1)}, u32[]{:S(2)}, u32[]{:S(2)}) collective-permute-start(bf16[10,32,128]{2,1,0:T(8,128)(2,1)S(1)} %get-tuple-element.78), channel_id=1, source_target_pairs={{0,2},{2,0},{4,6},{6,4},{1,3},{3,1},{5,7},{7,5},{8,10},{10,8},{12,... | collective-permute-start | bytes 245768 | tf_op jit(solution)/shard_map/ppermute | solution.py:421
  11.0 7.8 %collective-permute-start.5 = (bf16[10,32,128]{2,1,0:T(8,128)(2,1)S(1)}, bf16[10,32,128]{2,1,0:T(8,128)(2,1)S(1)}, u32[]{:S(2)}, u32[]{:S(2)}) collective-permute-start(bf16[10,32,128]{2,1,0:T(8,128)(2,1)S(1)} %get-tuple-element.77), channel_id=1, source_target_pairs={{0,4},{2,6},{4,0},{6,2},{1,5},{3,7},{5,1},{7,3},{8,12},{10,14},{12... | collective-permute-start | bytes 245768 | tf_op jit(solution)/shard_map/ppermute | solution.py:421
  11.0 7.8 %collective-permute-start.6 = (bf16[10,32,128]{2,1,0:T(8,128)(2,1)S(1)}, bf16[10,32,128]{2,1,0:T(8,128)(2,1)S(1)}, u32[]{:S(2)}, u32[]{:S(2)}) collective-permute-start(bf16[10,32,128]{2,1,0:T(8,128)(2,1)S(1)} %get-tuple-element.76), channel_id=1, source_target_pairs={{0,6},{2,4},{4,2},{6,0},{1,7},{3,5},{5,3},{7,1},{8,14},{10,12},{12... | collective-permute-start | bytes 245768 | tf_op jit(solution)/shard_map/ppermute | solution.py:421
  13.0 13.7 %collective-permute-start.2 = (bf16[22,32,256]{2,1,0:T(8,128)(2,1)S(1)}, bf16[22,32,256]{2,1,0:T(8,128)(2,1)S(1)}, u32[]{:S(2)}, u32[]{:S(2)}) collective-permute-start(bf16[22,32,256]{2,1,0:T(8,128)(2,1)S(1)} %get-tuple-element.72), channel_id=1, source_target_pairs={{0,8},{8,0},{16,24},{24,16},{1,9},{9,1},{17,25},{25,17},{2,10},{10... | collective-permute-start | bytes 1081352 | tf_op jit(solution)/shard_map/ppermute | solution.py:403
  14.6 12.0 %collective-permute-start.3 = (bf16[22,32,256]{2,1,0:T(8,128)(2,1)S(1)}, bf16[22,32,256]{2,1,0:T(8,128)(2,1)S(1)}, u32[]{:S(2)}, u32[]{:S(2)}) collective-permute-start(bf16[22,32,256]{2,1,0:T(8,128)(2,1)S(1)} %get-tuple-element.71), channel_id=1, source_target_pairs={{0,1},{1,0},{8,16},{9,17},{16,8},{17,9},{24,25},{25,24},{2,3},{3,2... | collective-permute-start | bytes 1081352 | tf_op jit(solution)/shard_map/ppermute | solution.py:416
  15.8 6.9 %collective-permute-start.11 = (bf16[14,32,128]{2,1,0:T(8,128)(2,1)S(1)}, bf16[14,32,128]{2,1,0:T(8,128)(2,1)S(1)}, u32[]{:S(2)}, u32[]{:S(2)}) collective-permute-start(bf16[14,32,128]{2,1,0:T(8,128)(2,1)S(1)} %get-tuple-element.41), channel_id=1, source_target_pairs={{0,2},{2,0},{4,6},{6,4},{1,3},{3,1},{5,7},{7,5},{8,10},{10,8},{12,... | collective-permute-start | bytes 344072 | tf_op jit(solution)/shard_map/ppermute | solution.py:421
  18.8 7.7 %collective-permute-start.12 = (bf16[14,32,128]{2,1,0:T(8,128)(2,1)S(1)}, bf16[14,32,128]{2,1,0:T(8,128)(2,1)S(1)}, u32[]{:S(2)}, u32[]{:S(2)}) collective-permute-start(bf16[14,32,128]{2,1,0:T(8,128)(2,1)S(1)} %get-tuple-element.41), channel_id=1, source_target_pairs={{0,4},{2,6},{4,0},{6,2},{1,5},{3,7},{5,1},{7,3},{8,12},{10,14},{12... | collective-permute-start | bytes 344072 | tf_op jit(solution)/shard_map/ppermute | solution.py:421
  18.9 7.7 %collective-permute-start.13 = (bf16[14,32,128]{2,1,0:T(8,128)(2,1)S(1)}, bf16[14,32,128]{2,1,0:T(8,128)(2,1)S(1)}, u32[]{:S(2)}, u32[]{:S(2)}) collective-permute-start(bf16[14,32,128]{2,1,0:T(8,128)(2,1)S(1)} %get-tuple-element.41), channel_id=1, source_target_pairs={{0,6},{2,4},{4,2},{6,0},{1,7},{3,5},{5,3},{7,1},{8,14},{10,12},{12... | collective-permute-start | bytes 344072 | tf_op jit(solution)/shard_map/ppermute | solution.py:421
  22.7 12.7 %collective-permute-start.7 = (bf16[4,10,32,128]{3,2,1,0:T(8,128)(2,1)S(1)}, bf16[4,10,32,128]{3,2,1,0:T(8,128)(2,1)S(1)}, u32[]{:S(2)}, u32[]{:S(2)}) collective-permute-start(bf16[4,10,32,128]{3,2,1,0:T(8,128)(2,1)S(1)} %pad_maximum_fusion.2.co), channel_id=1, source_target_pairs={{0,8},{8,0},{16,24},{24,16},{1,9},{9,1},{17,25},{25,17},{2,10},{10... | collective-permute-start | bytes 983048 | tf_op jit(solution)/shard_map/ppermute | solution.py:403
  26.6 8.8 %collective-permute-start.8 = (bf16[4,10,32,128]{3,2,1,0:T(8,128)(2,1)S(1)}, bf16[4,10,32,128]{3,2,1,0:T(8,128)(2,1)S(1)}, u32[]{:S(2)}, u32[]{:S(2)}) collective-permute-start(bf16[4,10,32,128]{3,2,1,0:T(8,128)(2,1)S(1)} %pad_maximum_fusion.2.co), channel_id=1, source_target_pairs={{0,1},{1,0},{8,16},{9,17},{16,8},{17,9},{24,25},{25,24},{2,3},{3,2... | collective-permute-start | bytes 983048 | tf_op jit(solution)/shard_map/ppermute | solution.py:416
  30.1 5.3 %collective-permute-start.10 = (bf16[10,64,128]{2,1,0:T(8,128)(2,1)S(1)}, bf16[10,64,128]{2,1,0:T(8,128)(2,1)S(1)}, u32[]{:S(2)}, u32[]{:S(2)}) collective-permute-start(bf16[10,64,128]{2,1,0:T(8,128)(2,1)S(1)} %get-tuple-element.37.pooled.ur), channel_id=1, source_target_pairs={{0,1},{1,0},{8,16},{9,17},{16,8},{17,9},{24,25},{25,24},{2,3},{3,2... | collective-permute-start | bytes 491528 | tf_op jit(solution)/shard_map/ppermute | solution.py:416
  30.7 6.3 %collective-permute-start.9 = (bf16[10,64,128]{2,1,0:T(8,128)(2,1)S(1)}, bf16[10,64,128]{2,1,0:T(8,128)(2,1)S(1)}, u32[]{:S(2)}, u32[]{:S(2)}) collective-permute-start(bf16[10,64,128]{2,1,0:T(8,128)(2,1)S(1)} %get-tuple-element.37.pooled.ur), channel_id=1, source_target_pairs={{0,8},{8,0},{16,24},{24,16},{1,9},{9,1},{17,25},{25,17},{2,10},{10... | collective-permute-start | bytes 491528 | tf_op jit(solution)/shard_map/ppermute | solution.py:403
  42.7 2.0 %collective-permute-start.14 = (f32[4,7,40,128]{3,2,1,0:T(8,128)S(1)}, f32[4,7,40,128]{3,2,1,0:T(8,128)S(1)}, u32[]{:S(2)}, u32[]{:S(2)}) collective-permute-start(f32[4,7,40,128]{3,2,1,0:T(8,128)S(1)} %get-tuple-element.47), channel_id=1, source_target_pairs={{0,1},{1,0},{2,3},{3,2},{4,5},{5,4},{6,7},{7,6},{8,9},{9,8},{10,11... | collective-permute-start | bytes 1720328 | tf_op jit(solution)/shard_map/ppermute | solution.py:403
  44.9 6.1 %collective-permute-start.15 = (bf16[7,40,128]{2,1,0:T(8,128)(2,1)S(1)}, bf16[7,40,128]{2,1,0:T(8,128)(2,1)S(1)}, u32[]{:S(2)}, u32[]{:S(2)}) collective-permute-start(bf16[7,40,128]{2,1,0:T(8,128)(2,1)S(1)} %get-tuple-element.79), channel_id=1, source_target_pairs={{0,8},{8,0},{16,24},{24,16},{1,9},{9,1},{17,25},{25,17},{2,10},{10... | collective-permute-start | bytes 215048 | tf_op jit(solution)/shard_map/ppermute | solution.py:421
  47.0 8.0 %collective-permute-start.16 = (bf16[7,40,128]{2,1,0:T(8,128)(2,1)S(1)}, bf16[7,40,128]{2,1,0:T(8,128)(2,1)S(1)}, u32[]{:S(2)}, u32[]{:S(2)}) collective-permute-start(bf16[7,40,128]{2,1,0:T(8,128)(2,1)S(1)} %get-tuple-element.81), channel_id=1, source_target_pairs={{0,16},{8,24},{16,0},{24,8},{1,17},{9,25},{17,1},{25,9},{2,18},{10... | collective-permute-start | bytes 215048 | tf_op jit(solution)/shard_map/ppermute | solution.py:421
  48.0 18.8 %copy-start.5 = (f32[32]{0:T(128)S(1)}, f32[32]{0:T(128)}, u32[]{:S(2)}) copy-start(f32[32]{0:T(128)} %param.10) | copy-start | bytes 388
  48.0 7.0 %collective-permute-start.17 = (bf16[7,40,128]{2,1,0:T(8,128)(2,1)S(1)}, bf16[7,40,128]{2,1,0:T(8,128)(2,1)S(1)}, u32[]{:S(2)}, u32[]{:S(2)}) collective-permute-start(bf16[7,40,128]{2,1,0:T(8,128)(2,1)S(1)} %get-tuple-element.80), channel_id=1, source_target_pairs={{0,24},{8,16},{16,8},{24,0},{1,25},{9,17},{17,9},{25,1},{2,26},{10... | collective-permute-start | bytes 215048 | tf_op jit(solution)/shard_map/ppermute | solution.py:421
  55.1 5.5 %collective-permute-start.18 = (bf16[368,128]{1,0:T(8,128)(2,1)S(1)}, bf16[368,128]{1,0:T(8,128)(2,1)S(1)}, u32[]{:S(2)}, u32[]{:S(2)}) collective-permute-start(bf16[368,128]{1,0:T(8,128)(2,1)S(1)} %pad_maximum_fusion.4), channel_id=1, source_target_pairs={{0,2},{2,0},{4,6},{6,4},{1,3},{3,1},{5,7},{7,5},{8,10},{10,8},{12,... | collective-permute-start | bytes 282632 | tf_op jit(solution)/shard_map/ppermute | solution.py:421
  55.9 6.3 %collective-permute-start.19 = (bf16[368,128]{1,0:T(8,128)(2,1)S(1)}, bf16[368,128]{1,0:T(8,128)(2,1)S(1)}, u32[]{:S(2)}, u32[]{:S(2)}) collective-permute-start(bf16[368,128]{1,0:T(8,128)(2,1)S(1)} %pad_maximum_fusion.5), channel_id=1, source_target_pairs={{0,4},{2,6},{4,0},{6,2},{1,5},{3,7},{5,1},{7,3},{8,12},{10,14},{12... | collective-permute-start | bytes 282632 | tf_op jit(solution)/shard_map/ppermute | solution.py:421
  56.1 6.1 %collective-permute-start.20 = (bf16[368,128]{1,0:T(8,128)(2,1)S(1)}, bf16[368,128]{1,0:T(8,128)(2,1)S(1)}, u32[]{:S(2)}, u32[]{:S(2)}) collective-permute-start(bf16[368,128]{1,0:T(8,128)(2,1)S(1)} %pad_maximum_fusion.6), channel_id=1, source_target_pairs={{0,6},{2,4},{4,2},{6,0},{1,7},{3,5},{5,3},{7,1},{8,14},{10,12},{12... | collective-permute-start | bytes 282632 | tf_op jit(solution)/shard_map/ppermute | solution.py:421
  62.3 5.7 %collective-permute-start.21 = (bf16[7,16,128]{2,1,0:T(8,128)(2,1)S(1)}, bf16[7,16,128]{2,1,0:T(8,128)(2,1)S(1)}, u32[]{:S(2)}, u32[]{:S(2)}) collective-permute-start(bf16[7,16,128]{2,1,0:T(8,128)(2,1)S(1)} %fusion.9), channel_id=1, source_target_pairs={{0,8},{8,0},{16,24},{24,16},{1,9},{9,1},{17,25},{25,17},{2,10},{10... | collective-permute-start | bytes 86024 | tf_op jit(solution)/shard_map/ppermute | solution.py:421
  64.1 4.9 %collective-permute-start.22 = (bf16[7,16,128]{2,1,0:T(8,128)(2,1)S(1)}, bf16[7,16,128]{2,1,0:T(8,128)(2,1)S(1)}, u32[]{:S(2)}, u32[]{:S(2)}) collective-permute-start(bf16[7,16,128]{2,1,0:T(8,128)(2,1)S(1)} %fusion.9), channel_id=1, source_target_pairs={{0,16},{8,24},{16,0},{24,8},{1,17},{9,25},{17,1},{25,9},{2,18},{10... | collective-permute-start | bytes 86024 | tf_op jit(solution)/shard_map/ppermute | solution.py:421
  65.0 5.7 %collective-permute-start.23 = (bf16[7,16,128]{2,1,0:T(8,128)(2,1)S(1)}, bf16[7,16,128]{2,1,0:T(8,128)(2,1)S(1)}, u32[]{:S(2)}, u32[]{:S(2)}) collective-permute-start(bf16[7,16,128]{2,1,0:T(8,128)(2,1)S(1)} %fusion.9), channel_id=1, source_target_pairs={{0,24},{8,16},{16,8},{24,0},{1,25},{9,17},{17,9},{25,1},{2,26},{10... | collective-permute-start | bytes 86024 | tf_op jit(solution)/shard_map/ppermute | solution.py:421
  70.7 1.4 %collective-permute-start.24 = (bf16[4,7,16,128]{3,2,1,0:T(8,128)(2,1)S(1)}, bf16[4,7,16,128]{3,2,1,0:T(8,128)(2,1)S(1)}, u32[]{:S(2)}, u32[]{:S(2)}) collective-permute-start(bf16[4,7,16,128]{3,2,1,0:T(8,128)(2,1)S(1)} %pad_maximum_fusion.3.mine), channel_id=1, source_target_pairs={{0,1},{1,0},{2,3},{3,2},{4,5},{5,4},{6,7},{7,6},{8,9},{9,8},{10,11... | collective-permute-start | bytes 344072 | tf_op jit(solution)/shard_map/ppermute | solution.py:403

commit v3 on v2

--- a/solution.py
+++ b/solution.py
@@ -1,4 +1,3 @@
-import functools
 import math
 
 import jax
@@ -10,7 +9,6 @@
 
 BF = jnp.bfloat16
 F32 = jnp.float32
-VMEM_BYTES = 20 * 1024 * 1024
 
 
 def dot(a, b):
@@ -49,11 +47,15 @@
 
 
 def beside(place, below, first, second):
-    second = jnp.where(place[5] == 1, second, jnp.zeros_like(second))
-    return jnp.where((place[0] == 1) == below, first, second)
-
-
-def call(body, name, outs, scratch, ins, smem_ins=0, flops=0):
+    use_first = jnp.where((place[0] == 1) == below, 1.0, 0.0)
+    use_second = (1.0 - use_first) * jnp.where(place[5] == 1, 1.0, 0.0)
+    lanes = (1, first.shape[-1])
+    return first[...] * jnp.full(lanes, use_first, F32).astype(BF) + second[...] * jnp.full(
+        lanes, use_second, F32
+    ).astype(BF)
+
+
+def call(body, name, outs, scratch, ins, smem_ins=0, flops=0, room=40):
     vm = pl.BlockSpec(memory_space=pltpu.VMEM)
     sm = pl.BlockSpec(memory_space=pltpu.SMEM)
     return pl.pallas_call(
@@ -63,13 +65,13 @@
         in_specs=[sm] * smem_ins + [vm] * (len(ins) - smem_ins),
         out_specs=jax.tree.map(lambda _: vm, outs),
         scratch_shapes=scratch,
-        compiler_params=pltpu.CompilerParams(vmem_limit_bytes=VMEM_BYTES),
+        compiler_params=pltpu.CompilerParams(vmem_limit_bytes=room << 20),
         cost_estimate=pl.CostEstimate(flops=flops, bytes_accessed=1 << 20, transcendentals=0),
     )(*ins)
 
 
-def prep_body(me, vol, cot, w2, vt, cp, w2p, cpad):
-    cin, planes, rows, width = vol.shape
+def volume_body(vol, vt):
+    planes, rows, cin, width = vt.shape
     swap = swap_majors(cin, rows)
     half = width // 2
     r, c = index_pair(width, width)
@@ -77,9 +79,12 @@
     for x in range(planes):
         cells = dot(swap, vol[:, x].reshape(cin * rows, width)).astype(BF)
         vt[x] = dot(cells, split).astype(BF).reshape(rows, cin, width)
+
+
+def prep_body(me, cot, w2, cp, w2p, cpad):
     nf, rows2, width2 = cot.shape
     step = 16
-    swap2 = swap if nf == cin and rows == step else swap_majors(nf, step)
+    swap2 = swap_majors(nf, step)
     for h in range(0, rows2, step):
         got = dot(swap2, cot[:, h : h + step].reshape(nf * step, width2))
         cpad[1 + h : 1 + h + step] = got.astype(BF).reshape(step, nf, width2)
@@ -101,9 +106,35 @@
         w2p[p] = both.astype(BF)
 
 
-def conv1_body(place, vr, za, zb, w1q, bias, cells, mask, pooled, w1b):
+def moved_by_one(width):
+    half = width // 2
+    r, c = index_pair(width, width)
+    return one_where(
+        ((c < half) & (c > 0) & (r == half + c - 1))
+        | ((c >= half) & (r == c - half + 1) & (r < half))
+    )
+
+
+def fill_cells(cells, plane, moved):
+    rows, cin, width = plane.shape
+    half = width // 2
+    out = dot(plane.reshape(rows * cin, width), moved).astype(BF).reshape(rows, cin, width)
+    cells[:, 0:cin] = out[:, :, :half]
+    cells[:, cin : 2 * cin] = plane[:, :, :half]
+    cells[:, 2 * cin : 3 * cin] = plane[:, :, half:]
+    cells[:, 3 * cin : 4 * cin] = out[:, :, half:]
+
+
+def two_rows(cells, first):
+    rows, deep, half = cells.shape
+    return jnp.concatenate(
+        [cells[first + 2 * n : first + 2 * n + 4].reshape(4 * deep, half) for n in range(2)],
+        axis=1,
+    )
+
+
+def conv1_own_body(vr, w1q, bias, cells, w1b, acc):
     planes, rows, cin, width = vr.shape
-    half = width // 2
     c1 = bias.shape[0] // 4
     eye = identity(4 * c1)
     nothing = jnp.zeros((cin, 2 * c1), BF)
@@ -115,37 +146,30 @@
                 right = w1q[i, ys - 1, slot] if ys > 0 else nothing
                 blocks.append(jnp.concatenate([left, right], axis=1))
         w1b[i] = dot_nt(eye, jnp.concatenate(blocks, axis=0)).astype(BF)
-    r, c = index_pair(width, width)
-    moved = one_where(
-        ((c < half) & (c > 0) & (r == half + c - 1)) | ((c >= half) & (r == c - half + 1) & (r < half))
-    )
-    for x in range(planes + 2):
-        if x in (0, planes + 1):
-            plane = beside(place, x == 0, za[...], zb[...])
-        else:
-            plane = vr[x - 1]
-        out = dot(plane.reshape(rows * cin, width), moved).astype(BF).reshape(rows, cin, width)
-        cells[x, :, 0:cin] = out[:, :, :half]
-        cells[x, :, cin : 2 * cin] = plane[:, :, :half]
-        cells[x, :, 2 * cin : 3 * cin] = plane[:, :, half:]
-        cells[x, :, 3 * cin : 4 * cin] = out[:, :, half:]
+    moved = moved_by_one(width)
+    for x in range(planes):
+        fill_cells(cells.at[x], vr[x], moved)
+    for t in range(acc.shape[1]):
+        for xp in range(2):
+            acc[xp, t] = (
+                dot(w1b[1 - xp], two_rows(cells.at[0], 4 * t))
+                + dot(w1b[2 - xp], two_rows(cells.at[1], 4 * t))
+                + bias[...]
+            )
+
+
+def conv1_body(place, za, zb, w1b, acc, low, high, mask, pooled):
+    rows, cin, width = za.shape
+    half = width // 2
+    c1 = pooled.shape[1]
+    moved = moved_by_one(width)
+    fill_cells(low, beside(place, True, za, zb), moved)
+    fill_cells(high, beside(place, False, za, zb), moved)
     rows2 = pooled.shape[0]
-    deep = 16 * cin
     for t in range(rows2 // 2):
         total = None
-        for xp in range(2):
-            acc = None
-            for i in range(3):
-                rhs = jnp.concatenate(
-                    [
-                        cells[xp + i, 4 * t : 4 * t + 4].reshape(deep, half),
-                        cells[xp + i, 4 * t + 2 : 4 * t + 6].reshape(deep, half),
-                    ],
-                    axis=1,
-                )
-                part = dot(w1b[i], rhs)
-                acc = part if acc is None else acc + part
-            pre = acc + bias[...]
+        for xp, cells in ((0, low), (1, high)):
+            pre = acc[xp, t] + dot(w1b[2 * xp], two_rows(cells, 4 * t))
             above = pre > 0
             flags = jnp.where(above, 1.0, 0.0).astype(BF)
             if t > 0:
@@ -156,14 +180,17 @@
             for b in range(4):
                 piece = act[b * c1 : (b + 1) * c1]
                 total = piece if total is None else total + piece
+        if t == 0:
+            total = total * jnp.where(at_low(total, half) & (place[1] == 0), 0.0, 1.0)
+        if t == rows2 // 2 - 1:
+            total = total * jnp.where(at_low(total, half) | (place[2] == 1), 1.0, 0.0)
         mean = (total * 0.125).astype(BF)
-        first, second = mean[:, :half], mean[:, half:]
-        if t == 0:
-            first = jnp.where(place[1] == 1, first, jnp.zeros_like(first))
-        if t == rows2 // 2 - 1:
-            second = jnp.where(place[2] == 1, second, jnp.zeros_like(second))
-        pooled[2 * t] = first
-        pooled[2 * t + 1] = second
+        pooled[2 * t] = mean[:, :half]
+        pooled[2 * t + 1] = mean[:, half:]
+
+
+def at_low(value, half):
+    return lax.broadcasted_iota(jnp.int32, value.shape, 1) < half
 
 
 def with_shifts(store, plane, shifts):
@@ -178,11 +205,7 @@
     rows, c1, width = ur.shape
     count, pairs, nf, _ = w2r.shape
     shifts = shift_both(width)
-    planes = (
-        beside(place, True, ua[...], ub[...]),
-        ur[...],
-        beside(place, False, ua[...], ub[...]),
-    )
+    planes = (beside(place, True, ua, ub), ur[...], beside(place, False, ua, ub))
     for x in range(3):
 
         def store(k, value, x=x):
@@ -274,17 +297,14 @@
     )
 
 
-def back_body(place, cells, mask, pooled, ca, cb, wb, own_back, own_g2, own_b2,
-              keep, send, t0, t2, gp, g2, red):
+def back_body(place, mask, pooled, ca, cb, wb, own_back, gp, g2, bias1, t0, t2):
     count, rows, nf, width = ca.shape
-    pairs = 14
     c1 = pooled.shape[1]
     c2 = count * nf
-    cin = cells.shape[2] // 4
     shifts = shift_both(width)
-    fill_planes(t0, beside(place, True, ca[...], cb[...]), shifts)
-    fill_planes(t2, beside(place, False, ca[...], cb[...]), shifts)
-    bias1 = jnp.zeros((8, 4 * c1), F32)
+    fill_planes(t0, beside(place, True, ca, cb), shifts)
+    fill_planes(t2, beside(place, False, ca, cb), shifts)
+    sums = jnp.zeros((8, 4 * c1), F32)
     ones = jnp.ones((8, 2 * width), BF)
     n_pairs = (rows - 2) // 2
     for t in range(n_pairs):
@@ -295,35 +315,32 @@
             flags = jnp.concatenate([mask[xp, 2 * t], mask[xp, 2 * t + 1]], axis=1)
             grad = (spread * jnp.where(flags > 0, 1.0, 0.3)).astype(BF)
             gp[xp, t] = grad
-            bias1 = bias1 + dot_nt(ones, grad)
+            sums = sums + dot_nt(ones, grad)
+    bias1[...] = sums
     rhs = pooled_wide(pooled)
-    for x, t_ref in ((0, t0), (2, t2)):
+    for n, t_ref in enumerate((t0, t2)):
         for ys in range(3):
             out = dot_nt(rows_wide(t_ref, ys, rows - 2), rhs)
             for zs in range(3):
-                d = ((2 - x) * 3 + (2 - ys)) * 3 + (2 - zs)
-                g2[d] = out[zs * c2 : (zs + 1) * c2]
+                g2[n, (2 - ys) * 3 + (2 - zs)] = out[zs * c2 : (zs + 1) * c2]
+
+
+def weights_body(place, cells, low, high, gp, g2, bias1, own_g2, own_b2, keep, send, red):
+    c2, wide_lanes = own_b2.shape
+    c1 = wide_lanes // 2
+    cin = cells.shape[2] // 4
+    n_pairs = gp.shape[1]
+    pairs = 14
+    sources = (low, cells.at[0], cells.at[1], high)
 
     def part2(d):
         if d == 27:
             return own_b2[...]
-        return own_g2[d - 9] if 9 <= d < 18 else g2[d]
-
-    parts = keep.shape[0]
-    hp = pairs // 2
-    share2, share1 = nf // parts, cin // parts
+        return own_g2[d - 9] if 9 <= d < 18 else g2[1 - d // 18, d % 9]
+
     low_wide = lax.broadcasted_iota(jnp.int32, (c2, 2 * c1), 1) < c1
-
-    def put(p, start, share, block):
-        for part in range(parts):
-            red[p // hp, part, p % hp, start : start + share] = block[
-                part * share : (part + 1) * share
-            ]
-
     for p in range(pairs):
-        wide = jnp.where(low_wide, part2(p), part2(p + pairs))
-        for s in range(count):
-            put(p, s * share2, share2, wide[s * nf : (s + 1) * nf])
+        red[p, :c2] = jnp.where(low_wide, part2(p), part2(p + pairs))
     lane = lax.broadcasted_iota(jnp.int32, (cin, 2 * c1), 1)
     low_half = lane < c1
     lows, highs = {}, {}
@@ -331,13 +348,7 @@
         acc = None
         for xp in range(2):
             for t in range(n_pairs):
-                lhs = jnp.concatenate(
-                    [
-                        cells[xp + i, 4 * t + 2 : 4 * t + 6].reshape(16 * cin, width),
-                        cells[xp + i, 4 * t + 4 : 4 * t + 8].reshape(16 * cin, width),
-                    ],
-                    axis=1,
-                )
+                lhs = two_rows(sources[xp + i], 4 * t + 2)
                 part = dot_nt(lhs, gp[xp, t])
                 acc = part if acc is None else acc + part
         for j in range(3):
@@ -357,10 +368,10 @@
     b1 = b1 + pltpu.roll(b1, c1, 1)
     highs[pairs - 1] = jnp.concatenate([b1] * (cin // 8), axis=0)
     for p in range(pairs):
-        put(p, count * share2, share1, jnp.where(low_half, lows[p], highs[p]))
-    for part in range(parts):
-        keep[part] = red[place[4], part ^ place[3]]
-        send[part] = red[1 - place[4], part ^ place[3]]
+        red[p, c2:] = jnp.where(low_half, lows[p], highs[p])
+    hp = pairs // 2
+    keep[...] = red[pl.ds(place[4] * hp, hp)]
+    send[...] = red[pl.ds((1 - place[4]) * hp, hp)]
 
 
 def unpack_body(me, *refs):
@@ -374,28 +385,25 @@
 
 
 def finish_body(place, mine, other, g2, b2, g1, b1):
-    parts, hp, _, width = mine.shape
-    nf, cin, c1 = g2.shape[1], g1.shape[1], g2.shape[2]
-    share2, share1 = nf // parts, cin // parts
+    hp, _, width = mine.shape
+    nf, c1 = g2.shape[1], g2.shape[2]
     first = place[4] == 0
-    for part in range(parts):
-        slot = part ^ place[3]
-        got = mine[slot].astype(F32)
-        more = other[slot].astype(F32)
-        halves = (jnp.where(first, got, more), jnp.where(first, more, got))
-        for p in range(2 * hp):
-            block = halves[p // hp][p % hp]
-            turned = pltpu.roll(block, c1, 1)
-            for d, v in ((p, block), (p + 2 * hp, turned)):
-                low = v[:share2, :c1]
-                high = v[share2:, :c1]
-                if d < 27:
-                    g2[d, part * share2 : (part + 1) * share2] = low
-                    g1[d, part * share1 : (part + 1) * share1] = high
-                else:
-                    b2[part * share2 : (part + 1) * share2] = low
-                    if part == 0:
-                        b1[0:1] = high[0:1]
+    got, more = mine[...], other[...]
+    halves = (jnp.where(first, got, more), jnp.where(first, more, got))
+    for p in range(2 * hp):
+        block = halves[p // hp][p % hp]
+        turned = pltpu.roll(block, c1, 1)
+        for d, v in ((p, block), (p + 2 * hp, turned)):
+            low, high = v[:nf, :c1], v[nf:, :c1]
+            if d < 27:
+                g2[d] = low
+                g1[d] = high
+            else:
+                column = lax.broadcasted_iota(jnp.int32, low.shape, 0)
+                lane = lax.broadcasted_iota(jnp.int32, low.shape, 1)
+                row = jnp.sum(jnp.where(column == lane, low, 0.0), axis=0, keepdims=True)
+                b2[...] = row[:, :nf]
+                b1[...] = high[0:1]
 
 
 def swap_first(value, axis):
@@ -422,7 +430,7 @@
 
 
 def tree_sum(values):
-    values = list(values)
+    values = [v.astype(F32) for v in values]
     while len(values) > 1:
         values = [values[n] + values[n + 1] for n in range(0, len(values), 2)]
     return values[0]
@@ -463,16 +471,25 @@
     )
     bias4 = jnp.tile(first_bias, 4)[:, None]
     w2 = second_kernel.transpose(2, 3, 4, 0, 1).reshape(27, nf, c1)
-    vt, cp, w2p = call(
+    vt = call(
+        volume_body,
+        "volume_cells",
+        jax.ShapeDtypeStruct((planes, rows, cin, width), BF),
+        [],
+        (source,),
+        flops=1 << 30,
+    )
+    cp, w2p = call(
         prep_body,
-        "prep",
-        [
-            jax.ShapeDtypeStruct((planes, rows, cin, width), BF),
+        "cotangent_cells",
+        [
             jax.ShapeDtypeStruct((n_sy, own2 + 2, nf, width2), BF),
             jax.ShapeDtypeStruct((pairs, nf, 2 * c1), BF),
         ],
-        [pltpu.VMEM((rows2 + 2, nf, width2), BF)],
-        (me, source, cotan, w2),
+        [
+            pltpu.VMEM((rows2 + 2, nf, width2), BF),
+        ],
+        (me, cotan, w2),
         smem_ins=1,
         flops=1 << 30,
     )
@@ -487,29 +504,46 @@
     za = swap_first(jnp.where(odd_x == 1, vr[0], vr[planes - 1]), "sx")
     zb = swap_second(jnp.where(odd_x == 1, vr[planes - 1], vr[0]), "sx")
 
-    co = jnp.stack([cp[0]] + [to_partner(cp[s], "sy", s) for s in range(1, n_sy)])
+    cgot = [cp[0]] + [to_partner(cp[s], "sy", s) for s in range(1, n_sy)]
+    w2p, vr = lax.optimization_barrier((w2p, vr))
+    wgot = [w2p] + [to_partner(w2p, "sy", s) for s in range(1, n_sy)]
+
+    pooled_rows = own2 + 2
+    cell_shape = (rows + 2 * rim, 4 * cin, width // 2)
+    cells, w1b, acc = call(
+        conv1_own_body,
+        "conv1_own",
+        [
+            jax.ShapeDtypeStruct((planes, *cell_shape), BF),
+            jax.ShapeDtypeStruct((3, 4 * c1, 16 * cin), BF),
+            jax.ShapeDtypeStruct((2, pooled_rows // 2, 4 * c1, width), F32),
+        ],
+        [],
+        (vr, w1q, bias4),
+        flops=2 << 30,
+    )
+    cgot, acc = lax.optimization_barrier((cgot, acc))
+    co = jnp.stack(cgot)
     ca = swap_first(co, "sx")
     cb = swap_second(co, "sx")
-    w2p, vr = lax.optimization_barrier((w2p, vr))
-    w2r = jnp.stack([w2p] + [to_partner(w2p, "sy", s) for s in range(1, n_sy)])
-
-    cells, mask, pooled = call(
+    low, high, mask, pooled = call(
         conv1_body,
         "conv1",
         [
-            jax.ShapeDtypeStruct((planes + 2, rows + 2 * rim, 4 * cin, width // 2), BF),
+            jax.ShapeDtypeStruct(cell_shape, BF),
+            jax.ShapeDtypeStruct(cell_shape, BF),
             jax.ShapeDtypeStruct((2, own2, 4 * c1, width // 2), BF),
-            jax.ShapeDtypeStruct((own2 + 2, c1, width // 2), BF),
-        ],
-        [pltpu.VMEM((3, 4 * c1, 16 * cin), BF)],
-        (place, vr, za, zb, w1q, bias4),
+            jax.ShapeDtypeStruct((pooled_rows, c1, width // 2), BF),
+        ],
+        [],
+        (place, za, zb, w1b, acc),
         smem_ins=1,
-        flops=3 << 30,
-    )
+        flops=1 << 30,
+    )
+    wgot, pooled = lax.optimization_barrier((wgot, pooled))
+    w2r = jnp.stack(wgot)
     ua = swap_first(pooled, "sx")
     ub = swap_second(pooled, "sx")
-
-    ca, cb, ua, ub = lax.optimization_barrier((ca, cb, ua, ub))
 
     plane_shape = (own2 + 2, 3, c2, width2)
     wb, own_back, own_g2, own_b2 = call(
@@ -526,26 +560,41 @@
         flops=2 << 30,
     )
     hp = pairs // 2
-    share = (c2 + cin) // n_sx
-    half_shape = jax.ShapeDtypeStruct((n_sx, hp, share, 2 * c1), F32)
-    keep, send = call(
+    half_shape = jax.ShapeDtypeStruct((hp, c2 + cin, 2 * c1), F32)
+    gp, back_g2, bias1 = call(
         back_body,
         "backward",
+        [
+            jax.ShapeDtypeStruct((2, own2 // 2, 4 * c1, width), BF),
+            jax.ShapeDtypeStruct((2, 9, c2, 2 * c1), F32),
+            jax.ShapeDtypeStruct((8, 4 * c1), F32),
+        ],
+        [pltpu.VMEM(plane_shape, BF), pltpu.VMEM(plane_shape, BF)],
+        (place, mask, pooled, ca, cb, wb, own_back),
+        smem_ins=1,
+        flops=2 << 30,
+    )
+    gp, ua, ub = lax.optimization_barrier((gp, ua, ub))
+    keep, send = call(
+        weights_body,
+        "first_weights",
         [half_shape, half_shape],
-        [
-            pltpu.VMEM(plane_shape, BF),
-            pltpu.VMEM(plane_shape, BF),
-            pltpu.VMEM((2, own2 // 2, 4 * c1, width), BF),
-            pltpu.VMEM((27, c2, 2 * c1), F32),
-            pltpu.VMEM((2, *half_shape.shape), F32),
-        ],
-        (place, cells, mask, pooled, ca, cb, wb, own_back, own_g2, own_b2),
+        [pltpu.VMEM((pairs, c2 + cin, 2 * c1), F32)],
+        (place, cells, low, high, gp, back_g2, bias1, own_g2, own_b2),
         smem_ins=1,
-        flops=5 << 30,
+        flops=3 << 30,
     )
 
     half = keep + swap_first(send, "rep")
     half, ua, ub = lax.optimization_barrier((half, ua, ub))
+    half_bf = half.astype(BF)
+    tail = half_bf[:, c2:]
+    got = [
+        to_partner(
+            jnp.concatenate([half_bf[:, s * nf : (s + 1) * nf], tail], axis=1), "sy", s
+        ).astype(F32)
+        for s in range(1, n_sy)
+    ]
     pieces = call(
         conv2_body,
         "conv2",
@@ -555,54 +604,36 @@
         smem_ins=1,
         flops=1 << 30,
     )
-    part = tree_sum(
-        [half[0]]
-        + [to_partner(half[s].astype(BF), "sx", s).astype(F32) for s in range(1, n_sx)]
-    )
-    own_rows = own2 * nf
-    share2, share1 = nf // n_sx, cin // n_sx
-    part_bf = part.astype(BF)
-    tail = part_bf[:, n_sy * share2 :]
-
-    def sy_message(s):
-        w2_rows = part_bf[:, s * share2 : (s + 1) * share2]
-        return jnp.concatenate(
-            [
-                pieces[s].reshape(own_rows, width2),
-                jnp.concatenate([w2_rows, tail], axis=1).reshape(-1, width2),
-            ],
-            axis=0,
-        )
-
-    own_piece = pieces[0].reshape(own_rows, width2)
-    passed = [to_partner(sy_message(s), "sy", s) for s in range(1, n_sy)]
+    own = jnp.concatenate([half[:, :nf], tail.astype(F32)], axis=1)
+    part = tree_sum([own] + got).astype(BF)
+    part, pieces = lax.optimization_barrier((part, pieces))
+    parts = [part] + [to_partner(part, "sx", s) for s in range(1, n_sx)]
+    flat = pieces.reshape(n_sy, own2 * nf, width2)
+    out_got = [flat[0]] + [to_partner(flat[s], "sy", s) for s in range(1, n_sy)]
     bias_wide = jnp.broadcast_to(second_bias[:, None, None], (nf, 1, width2))
     second_out = call(
         unpack_body,
         "unpack",
         jax.ShapeDtypeStruct((nf, rows2, width2), F32),
         [],
-        (me, own_piece, *passed, bias_wide),
+        (me, *out_got, bias_wide),
         smem_ins=1,
         flops=1 << 28,
     )
-    sums = [g[own_rows:].reshape(hp, share2 + share1, width2).astype(F32) for g in passed]
-    own = jnp.concatenate([part[:, :share2], tail.astype(F32)], axis=1)
-    total = (tree_sum([own] + sums) * scale).astype(BF)
-    spread = jnp.stack([total] + [to_partner(total, "sx", s) for s in range(1, n_sx)])
-    spread, second_out = lax.optimization_barrier((spread, second_out))
-    other = swap_first(spread, "rep")
+    parts, second_out = lax.optimization_barrier((parts, second_out))
+    total = tree_sum(parts) * scale
+    other = swap_first(total, "rep")
     g2, t2, g1, t1 = call(
         finish_body,
         "finish",
         [
             jax.ShapeDtypeStruct((27, nf, c1), F32),
-            jax.ShapeDtypeStruct((nf, c1), F32),
+            jax.ShapeDtypeStruct((1, nf), F32),
             jax.ShapeDtypeStruct((27, cin, c1), F32),
             jax.ShapeDtypeStruct((1, c1), F32),
         ],
         [],
-        (place, spread, other),
+        (place, total, other),
         smem_ins=1,
         flops=1 << 20,
     )
@@ -611,7 +642,7 @@
         g1.reshape(3, 3, 3, cin, c1).transpose(4, 3, 0, 1, 2),
         t1[0],
         g2.reshape(3, 3, 3, nf, c1).transpose(3, 4, 0, 1, 2),
-        t2[:, 0],
+        t2[0],
     )
 
 

time: 74.5 us -> 66.2 us (0.89)
  waiting for transfers between devices: 19.9 us -> 14.2 us
  local copies, waits for them, and re-layouts: 3.95 us -> 1.44 us
  starting transfers between devices: 32.3 us -> 31 us
  Pallas kernels: 16.5 us -> 17.6 us
    ppermute x15, waiting for transfers between devices: 15 us -> 9.1 us  [to_partner(): return lax.ppermute(value, axis, [(i, i ^ s) for i in range(count)])]
    unnamed x12, local copies, waits for them, and re-layouts: 2.93 us -> 1.06 us
    pallas_call x7 -> x10, Pallas kernels: 16.5 us -> 17.6 us  [call(): pl.pallas_call(body, name=name, out_shape=outs, in_specs=[sm] * smem_ins...]
  transfers between devices with their start and end apart: 25 -> 25, of which waited for: 11 -> 9; matrix products, arithmetic and copies ran while one was open for 1% -> 1% of each run, Pallas kernels for 11% -> 19%
where the time goes in v3:
time: 66.2 us; the launch traced here: 66 us
  starting transfers between devices  31 us (47%)
  Pallas kernels  17.6 us (27%)
  waiting for transfers between devices  14.2 us (21%)
  local copies, waits for them, and re-layouts  1.44 us (2%)
  between operations  0.95 us (1%)
  other arithmetic  0.77 us (1%)
    ppermute x15, starting transfers between devices, to_partner(): return lax.ppermute(value, axis, [(i, i ^ s) for i in range(count)])  21.6 us
    pallas_call x10, Pallas kernels, call(): pl.pallas_call(body, name=name, out_shape=outs, in_specs=[sm] * smem_ins...  17.6 us
    ppermute x6, starting transfers between devices, swap_first(): return lax.ppermute(value, axis, [(i, i ^ 1) for i in range(count)])  9.44 us
    ppermute x15, waiting for transfers between devices, to_partner(): return lax.ppermute(value, axis, [(i, i ^ s) for i in range(count)])  9.1 us
    ppermute x6, waiting for transfers between devices, swap_first(): return lax.ppermute(value, axis, [(i, i ^ 1) for i in range(count)])  5.12 us
  transfers between devices with their start and end apart: 25, of which 9 were waited for; matrix products, arithmetic and copies ran while one was open for 1% of the time, Pallas kernels for 19%

profile of v3, /device:TPU:0, one launch (start us, length us, event | category | flops | bytes accessed | tf_op | source)
XLA Modules:
  0.0 66.0 jit_solution(15337745899110242073)
XLA Ops:
  0.7 1.0 %copy-done = bf16[1,32,2,16,256]{4,3,2,1,0:T(8,128)(2,1)S(1)} copy-done((bf16[1,32,2,16,256]{4,3,2,1,0:T(8,128)(2,1)S(1)}, bf16[1,32,2,16,256]{4,3,2,1,0:T(8,128)(2,1)}, u32[]{:S(2)}) %copy-start) | copy-done | bytes 524312
  1.7 0.9 %volume_cells.1 = bf16[2,16,32,256]{3,2,1,0:T(8,128)(2,1)S(1)} custom-call(bf16[32,2,16,256]{3,2,1,0:T(8,128)(2,1)S(1)} %bitcast.50), custom_call_target="tpu_custom_call" | custom-call | flops 1073741824 | bytes 1048576 | tf_op jit(solution)/shard_map/volume_cells/pallas_call | solution.py:61
  2.7 3.0 %collective-permute-start = (bf16[2,3,32,256]{3,2,1,0:T(8,128)(2,1)S(1)}, bf16[2,3,32,256]{3,2,1,0:T(8,128)(2,1)S(1)}, u32[]{:S(2)}, u32[]{:S(2)}) collective-permute-start(bf16[2,3,32,256]{3,2,1,0:T(8,128)(2,1)S(1)} %get-tuple-element.112), channel_id=1, source_target_pairs={{0,2},{2,0},{4,6},{6,4},{1,3},{3,1},{5,7},{7,5},{8,10},{10,8},{12,... | collective-permute-start | bytes 294920 | tf_op jit(solution)/shard_map/ppermute | solution.py:411
  5.7 0.0 collective-permute-start.1
  5.7 0.5 cotangent_cells.1
  6.3 3.0 %collective-permute-start.4 = (bf16[10,32,128]{2,1,0:T(8,128)(2,1)S(1)}, bf16[10,32,128]{2,1,0:T(8,128)(2,1)S(1)}, u32[]{:S(2)}, u32[]{:S(2)}) collective-permute-start(bf16[10,32,128]{2,1,0:T(8,128)(2,1)S(1)} %get-tuple-element.115), channel_id=1, source_target_pairs={{0,2},{2,0},{4,6},{6,4},{1,3},{3,1},{5,7},{7,5},{8,10},{10,8},{12,... | collective-permute-start | bytes 245768 | tf_op jit(solution)/shard_map/ppermute | solution.py:429
  9.3 0.0 collective-permute-start.5
  9.3 1.5 %collective-permute-start.6 = (bf16[10,32,128]{2,1,0:T(8,128)(2,1)S(1)}, bf16[10,32,128]{2,1,0:T(8,128)(2,1)S(1)}, u32[]{:S(2)}, u32[]{:S(2)}) collective-permute-start(bf16[10,32,128]{2,1,0:T(8,128)(2,1)S(1)} %get-tuple-element.113), channel_id=1, source_target_pairs={{0,6},{2,4},{4,2},{6,0},{1,7},{3,5},{5,3},{7,1},{8,14},{10,12},{12... | collective-permute-start | bytes 245768 | tf_op jit(solution)/shard_map/ppermute | solution.py:429
  10.8 0.0 collective-permute-done
  10.8 0.0 collective-permute-done.1
  10.9 0.0 copy-start.3
  10.9 0.0 copy-start.4
  10.9 0.1 pad_maximum_fusion.vr
  11.0 0.1 select_bitcast_fusion
  11.1 1.6 %collective-permute-start.2 = (bf16[22,32,256]{2,1,0:T(8,128)(2,1)S(1)}, bf16[22,32,256]{2,1,0:T(8,128)(2,1)S(1)}, u32[]{:S(2)}, u32[]{:S(2)}) collective-permute-start(bf16[22,32,256]{2,1,0:T(8,128)(2,1)S(1)} %get-tuple-element.110), channel_id=1, source_target_pairs={{0,8},{8,0},{16,24},{24,16},{1,9},{9,1},{17,25},{25,17},{2,10},{10... | collective-permute-start | bytes 1081352 | tf_op jit(solution)/shard_map/ppermute | solution.py:411
  12.7 0.0 collective-permute-start.3
  12.7 0.2 fusion.2.w1q
  12.9 0.1 broadcast_in_dim_tile.4.bias
  13.0 0.1 stack.69.place
  13.1 2.0 %conv1_own.1 = (bf16[2,22,128,128]{3,2,1,0:T(8,128)(2,1)S(1)}, bf16[3,256,512]{2,1,0:T(8,128)(2,1)S(1)}, f32[2,5,256,256]{3,2,1,0:T(8,128)S(1)}) custom-call(bf16[2,22,32,256]{3,2,1,0:T(8,128)(2,1)S(1)} %pad_maximum_fusion.vr, bf16[3,3,4,32,128]{4,3,2,1,0:T(8,128)(2,1)S(1)} %fusion.2.w1q, f32[256,1]{1,0:T(8,128)S(1)} %broadcast_in_dim_tile.4.bias), custom_call_target="tpu_custom_call" | custom-call | flops 2147483648 | bytes 1048576 | tf_op jit(solution)/shard_map/conv1_own/pallas_call | solution.py:61
  15.2 3.7 %collective-permute-start.7 = (bf16[14,32,128]{2,1,0:T(8,128)(2,1)S(1)}, bf16[14,32,128]{2,1,0:T(8,128)(2,1)S(1)}, u32[]{:S(2)}, u32[]{:S(2)}) collective-permute-start(bf16[14,32,128]{2,1,0:T(8,128)(2,1)S(1)} %get-tuple-element.69), channel_id=1, source_target_pairs={{0,2},{2,0},{4,6},{6,4},{1,3},{3,1},{5,7},{7,5},{8,10},{10,8},{12,... | collective-permute-start | bytes 344072 | tf_op jit(solution)/shard_map/ppermute | solution.py:429
  18.9 0.0 collective-permute-done.5
  18.9 0.0 collective-permute-start.8
  18.9 0.0 collective-permute-done.6
  18.9 1.5 %collective-permute-start.9 = (bf16[14,32,128]{2,1,0:T(8,128)(2,1)S(1)}, bf16[14,32,128]{2,1,0:T(8,128)(2,1)S(1)}, u32[]{:S(2)}, u32[]{:S(2)}) collective-permute-start(bf16[14,32,128]{2,1,0:T(8,128)(2,1)S(1)} %get-tuple-element.69), channel_id=1, source_target_pairs={{0,6},{2,4},{4,2},{6,0},{1,7},{3,5},{5,3},{7,1},{8,14},{10,12},{12... | collective-permute-start | bytes 344072 | tf_op jit(solution)/shard_map/ppermute | solution.py:429
  20.5 0.0 collective-permute-done.2.za
  20.5 3.2 %collective-permute-start.10 = (bf16[4,10,32,128]{3,2,1,0:T(8,128)(2,1)S(1)}, bf16[4,10,32,128]{3,2,1,0:T(8,128)(2,1)S(1)}, u32[]{:S(2)}, u32[]{:S(2)}) collective-permute-start(bf16[4,10,32,128]{3,2,1,0:T(8,128)(2,1)S(1)} %pad_maximum_fusion.2.co), channel_id=1, source_target_pairs={{0,8},{8,0},{16,24},{24,16},{1,9},{9,1},{17,25},{25,17},{2,10},{10... | collective-permute-start | bytes 983048 | tf_op jit(solution)/shard_map/ppermute | solution.py:411
  23.7 1.8 %conv1.1 = (bf16[22,128,128]{2,1,0:T(8,128)(2,1)S(1)}, bf16[22,128,128]{2,1,0:T(8,128)(2,1)S(1)}, bf16[2,8,256,128]{3,2,1,0:T(8,128)(2,1)S(1)}, bf16[10,64,128]{2,1,0:T(8,128)(2,1)S(1)}) custom-call(s32[6]{0:T(128)S(1)} %stack.69.place, bf16[22,32,256]{2,1,0:T(8,128)(2,1)S(1)} %collective-permute-done.2.za, ...), custom_call_target="tpu_custom_call" | custom-call | flops 1073741824 | bytes 1048576 | tf_op jit(solution)/shard_map/conv1/pallas_call | solution.py:61
  25.5 1.1 %collective-permute-done.8 = bf16[14,32,128]{2,1,0:T(8,128)(2,1)S(1)} collective-permute-done((bf16[14,32,128]{2,1,0:T(8,128)(2,1)S(1)}, bf16[14,32,128]{2,1,0:T(8,128)(2,1)S(1)}, u32[]{:S(2)}, u32[]{:S(2)}) %collective-permute-start.8) | collective-permute-done | bytes 114720 | tf_op jit(solution)/shard_map/ppermute | solution.py:429
  26.6 1.4 %collective-permute-start.12 = (bf16[10,64,128]{2,1,0:T(8,128)(2,1)S(1)}, bf16[10,64,128]{2,1,0:T(8,128)(2,1)S(1)}, u32[]{:S(2)}, u32[]{:S(2)}) collective-permute-start(bf16[10,64,128]{2,1,0:T(8,128)(2,1)S(1)} %get-tuple-element.64.pooled.ur), channel_id=1, source_target_pairs={{0,8},{8,0},{16,24},{24,16},{1,9},{9,1},{17,25},{25,17},{2,10},{10... | collective-permute-start | bytes 491528 | tf_op jit(solution)/shard_map/ppermute | solution.py:411
  28.1 0.1 pad_maximum_fusion.1.w2r
  28.1 1.7 %backward_own.1 = (bf16[3,64,1152]{2,1,0:T(8,128)(2,1)S(1)}, f32[4,64,256]{2,1,0:T(8,128)S(1)}, f32[9,128,128]{2,1,0:T(8,128)S(1)}, f32[128,128]{1,0:T(8,128)S(1)}) custom-call(bf16[4,10,32,128]{3,2,1,0:T(8,128)(2,1)S(1)} %pad_maximum_fusion.2.co, bf16[10,64,128]{2,1,0:T(8,128)(2,1)S(1)} %get-tuple-element.64.pooled.ur, ...), custom_call_target="tpu_custom_call" | custom-call | flops 2147483648 | bytes 1048576 | tf_op jit(solution)/shard_map/backward_own/pallas_call | solution.py:61
  29.8 1.7 %collective-permute-done.10.ca = bf16[4,10,32,128]{3,2,1,0:T(8,128)(2,1)S(1)} collective-permute-done((bf16[4,10,32,128]{3,2,1,0:T(8,128)(2,1)S(1)}, bf16[4,10,32,128]{3,2,1,0:T(8,128)(2,1)S(1)}, u32[]{:S(2)}, u32[]{:S(2)}) %collective-permute-start.10) | collective-permute-done | bytes 327712 | tf_op jit(solution)/shard_map/ppermute | solution.py:411
  31.5 0.0 collective-permute-done.11.cb
  31.5 3.8 %backward.1 = (bf16[2,4,256,256]{3,2,1,0:T(8,128)(2,1)S(1)}, f32[2,9,128,128]{3,2,1,0:T(8,128)S(1)}, f32[8,256]{1,0:T(8,128)S(1)}) custom-call(s32[6]{0:T(128)S(1)} %stack.69.place, bf16[2,8,256,128]{3,2,1,0:T(8,128)(2,1)S(1)} %get-tuple-element.61.mask, bf16[10,64,128]{2,1,0:T(8,128)(2,1)S(1)} %get-tuple-element.64.pooled.ur, ...), custom_call_target="tpu_custom_call" | custom-call | flops 2147483648 | bytes 1048576 | tf_op jit(solution)/shard_map/backward/pallas_call | solution.py:61
  35.3 0.0 collective-permute-done.13.ub
  35.3 2.5 %first_weights.1 = (f32[7,160,128]{2,1,0:T(8,128)S(1)}, f32[7,160,128]{2,1,0:T(8,128)S(1)}) custom-call(s32[6]{0:T(128)S(1)} %stack.69.place, bf16[2,22,128,128]{3,2,1,0:T(8,128)(2,1)S(1)} %get-tuple-element.54.cells, bf16[22,128,128]{2,1,0:T(8,128)(2,1)S(1)} %get-tuple-element.59.low, bf16[22,128,128]{2,1,0:T(8,128)(2,1)S(1)} %get-tuple-element.60.high, ...), custom_call_target="tpu_custom_call" | custom-call | flops 3221225472 | bytes 1048576 | tf_op jit(solution)/shard_map/first_weights/pallas_call | solution.py:61
  37.9 0.1 collective-permute-start.14
  38.0 2.0 %collective-permute-done.14 = f32[7,160,128]{2,1,0:T(8,128)S(1)} collective-permute-done((f32[7,160,128]{2,1,0:T(8,128)S(1)}, f32[7,160,128]{2,1,0:T(8,128)S(1)}, u32[]{:S(2)}, u32[]{:S(2)}) %collective-permute-start.14) | collective-permute-done | bytes 573472 | tf_op jit(solution)/shard_map/ppermute | solution.py:411
  39.9 0.1 add.34
  40.1 1.5 %collective-permute-start.17 = (bf16[7,64,128]{2,1,0:T(8,128)(2,1)S(1)}, bf16[7,64,128]{2,1,0:T(8,128)(2,1)S(1)}, u32[]{:S(2)}, u32[]{:S(2)}) collective-permute-start(bf16[7,64,128]{2,1,0:T(8,128)(2,1)S(1)} %concatenate.24), channel_id=1, source_target_pairs={{0,6},{2,4},{4,2},{6,0},{1,7},{3,5},{5,3},{7,1},{8,14},{10,12},{12... | collective-permute-start | bytes 344072 | tf_op jit(solution)/shard_map/ppermute | solution.py:429
  41.7 1.5 %collective-permute-start.16 = (bf16[7,64,128]{2,1,0:T(8,128)(2,1)S(1)}, bf16[7,64,128]{2,1,0:T(8,128)(2,1)S(1)}, u32[]{:S(2)}, u32[]{:S(2)}) collective-permute-start(bf16[7,64,128]{2,1,0:T(8,128)(2,1)S(1)} %get-tuple-element.128), channel_id=1, source_target_pairs={{0,4},{2,6},{4,0},{6,2},{1,5},{3,7},{5,1},{7,3},{8,12},{10,14},{12... | collective-permute-start | bytes 344072 | tf_op jit(solution)/shard_map/ppermute | solution.py:429
  43.1 0.6 collective-permute-start.15
  43.8 0.0 copy-start.5
  43.8 1.5 %conv2.1 = bf16[4,8,32,128]{3,2,1,0:T(8,128)(2,1)S(1)} custom-call(s32[6]{0:T(128)S(1)} %stack.69.place, bf16[10,64,128]{2,1,0:T(8,128)(2,1)S(1)} %get-tuple-element.64.pooled.ur, bf16[10,64,128]{2,1,0:T(8,128)(2,1)S(1)} %collective-permute-done.12.ua, bf16[10,64,128]{2,1,0:T(8,128)(2,1)S(1)} %collective-permute-done.13.ub, ...), custom_call_target="tpu_custom_call" | custom-call | flops 1073741824 | bytes 1048576 | tf_op jit(solution)/shard_map/conv2/pallas_call | solution.py:61
  45.4 1.7 %collective-permute-done.17 = bf16[7,64,128]{2,1,0:T(8,128)(2,1)S(1)} collective-permute-done((bf16[7,64,128]{2,1,0:T(8,128)(2,1)S(1)}, bf16[7,64,128]{2,1,0:T(8,128)(2,1)S(1)}, u32[]{:S(2)}, u32[]{:S(2)}) %collective-permute-start.17) | collective-permute-done | bytes 114720 | tf_op jit(solution)/shard_map/ppermute | solution.py:429
  47.1 1.7 %collective-permute-done.16 = bf16[7,64,128]{2,1,0:T(8,128)(2,1)S(1)} collective-permute-done((bf16[7,64,128]{2,1,0:T(8,128)(2,1)S(1)}, bf16[7,64,128]{2,1,0:T(8,128)(2,1)S(1)}, u32[]{:S(2)}, u32[]{:S(2)}) %collective-permute-start.16) | collective-permute-done | bytes 114720 | tf_op jit(solution)/shard_map/ppermute | solution.py:429
  48.7 0.1 fusion.4
  48.8 0.9 %collective-permute-start.21 = (bf16[256,128]{1,0:T(8,128)(2,1)S(1)}, bf16[256,128]{1,0:T(8,128)(2,1)S(1)}, u32[]{:S(2)}, u32[]{:S(2)}) collective-permute-start(bf16[256,128]{1,0:T(8,128)(2,1)S(1)} %bitcast.63), channel_id=1, source_target_pairs={{0,2},{2,0},{4,6},{6,4},{1,3},{3,1},{5,7},{7,5},{8,10},{10,8},{12,... | collective-permute-start | bytes 196616 | tf_op jit(solution)/shard_map/ppermute | solution.py:429
  49.7 1.6 %collective-permute-start.18 = (bf16[7,64,128]{2,1,0:T(8,128)(2,1)S(1)}, bf16[7,64,128]{2,1,0:T(8,128)(2,1)S(1)}, u32[]{:S(2)}, u32[]{:S(2)}) collective-permute-start(bf16[7,64,128]{2,1,0:T(8,128)(2,1)S(1)} %fusion.4), channel_id=1, source_target_pairs={{0,8},{8,0},{16,24},{24,16},{1,9},{9,1},{17,25},{25,17},{2,10},{10... | collective-permute-start | bytes 344072 | tf_op jit(solution)/shard_map/ppermute | solution.py:429
  51.3 1.9 %collective-permute-start.19 = (bf16[7,64,128]{2,1,0:T(8,128)(2,1)S(1)}, bf16[7,64,128]{2,1,0:T(8,128)(2,1)S(1)}, u32[]{:S(2)}, u32[]{:S(2)}) collective-permute-start(bf16[7,64,128]{2,1,0:T(8,128)(2,1)S(1)} %fusion.4), channel_id=1, source_target_pairs={{0,16},{8,24},{16,0},{24,8},{1,17},{9,25},{17,1},{25,9},{2,18},{10... | collective-permute-start | bytes 344072 | tf_op jit(solution)/shard_map/ppermute | solution.py:429
  53.2 1.2 %collective-permute-start.20 = (bf16[7,64,128]{2,1,0:T(8,128)(2,1)S(1)}, bf16[7,64,128]{2,1,0:T(8,128)(2,1)S(1)}, u32[]{:S(2)}, u32[]{:S(2)}) collective-permute-start(bf16[7,64,128]{2,1,0:T(8,128)(2,1)S(1)} %fusion.4), channel_id=1, source_target_pairs={{0,24},{8,16},{16,8},{24,0},{1,25},{9,17},{17,9},{25,1},{2,26},{10... | collective-permute-start | bytes 344072 | tf_op jit(solution)/shard_map/ppermute | solution.py:429
  54.4 1.4 %collective-permute-start.22 = (bf16[256,128]{1,0:T(8,128)(2,1)S(1)}, bf16[256,128]{1,0:T(8,128)(2,1)S(1)}, u32[]{:S(2)}, u32[]{:S(2)}) collective-permute-start(bf16[256,128]{1,0:T(8,128)(2,1)S(1)} %bitcast.62), channel_id=1, source_target_pairs={{0,4},{2,6},{4,0},{6,2},{1,5},{3,7},{5,1},{7,3},{8,12},{10,14},{12... | collective-permute-start | bytes 196616 | tf_op jit(solution)/shard_map/ppermute | solution.py:429
  55.8 1.2 %collective-permute-start.23 = (bf16[256,128]{1,0:T(8,128)(2,1)S(1)}, bf16[256,128]{1,0:T(8,128)(2,1)S(1)}, u32[]{:S(2)}, u32[]{:S(2)}) collective-permute-start(bf16[256,128]{1,0:T(8,128)(2,1)S(1)} %bitcast.61), channel_id=1, source_target_pairs={{0,6},{2,4},{4,2},{6,0},{1,7},{3,5},{5,3},{7,1},{8,14},{10,12},{12... | collective-permute-start | bytes 196616 | tf_op jit(solution)/shard_map/ppermute | solution.py:429
  57.0 2.3 %collective-permute-done.22.refs_2_ = bf16[256,128]{1,0:T(8,128)(2,1)S(1)} collective-permute-done((bf16[256,128]{1,0:T(8,128)(2,1)S(1)}, bf16[256,128]{1,0:T(8,128)(2,1)S(1)}, u32[]{:S(2)}, u32[]{:S(2)}) %collective-permute-start.22) | collective-permute-done | bytes 65568 | tf_op jit(solution)/shard_map/ppermute | solution.py:429
  59.2 1.7 %collective-permute-done.23.refs_3_ = bf16[256,128]{1,0:T(8,128)(2,1)S(1)} collective-permute-done((bf16[256,128]{1,0:T(8,128)(2,1)S(1)}, bf16[256,128]{1,0:T(8,128)(2,1)S(1)}, u32[]{:S(2)}, u32[]{:S(2)}) %collective-permute-start.23) | collective-permute-done | bytes 65568 | tf_op jit(solution)/shard_map/ppermute | solution.py:429
  61.0 0.1 broadcast_in_dim.13.refs_4_
  61.1 1.1 %unpack.1 = f32[32,32,128]{2,1,0:T(8,128)} custom-call(s32[1]{0:T(128)} %bitcast.6.me, bf16[256,128]{1,0:T(8,128)(2,1)S(1)} %bitcast.49, bf16[256,128]{1,0:T(8,128)(2,1)S(1)} %collective-permute-done.21.refs_1_, bf16[256,128]{1,0:T(8,128)(2,1)S(1)} %collective-permute-done.22.refs_2_, bf16[256,128]{1,0:T(8,128)(2,1)S(1)} %collective-permute-done.23.refs_3_, ...), custom_call_target="tpu_custom_call" | custom-call | flops 268435456 | bytes 1048576 | tf_op jit(solution)/shard_map/unpack/pallas_call | solution.py:61
  62.2 0.5 collective-permute-done.19
  62.7 0.0 collective-permute-done.20
  62.7 0.1 add_multiply_fusion.mine
  62.8 0.1 collective-permute-start.24
  62.9 1.5 %collective-permute-done.24.other = f32[7,64,128]{2,1,0:T(8,128)S(1)} collective-permute-done((f32[7,64,128]{2,1,0:T(8,128)S(1)}, f32[7,64,128]{2,1,0:T(8,128)S(1)}, u32[]{:S(2)}, u32[]{:S(2)}) %collective-permute-start.24) | collective-permute-done | bytes 229408 | tf_op jit(solution)/shard_map/ppermute | solution.py:411
  64.3 1.7 %finish.1 = (f32[27,32,64]{2,1,0:T(8,128)}, f32[1,32]{1,0:T(1,128)}, f32[27,32,64]{2,1,0:T(8,128)}, f32[1,64]{1,0:T(1,128)}) custom-call(s32[6]{0:T(128)S(1)} %stack.69.place, f32[7,64,128]{2,1,0:T(8,128)S(1)} %add_multiply_fusion.mine, f32[7,64,128]{2,1,0:T(8,128)S(1)} %collective-permute-done.24.other), custom_call_target="tpu_custom_call" | custom-call | flops 1048576 | bytes 1048576 | tf_op jit(solution)/shard_map/finish/pallas_call | solution.py:61
  (29 shorter events, 0.3 us)
Async XLA Ops:
  0.6 1.0 %copy-start = (bf16[1,32,2,16,256]{4,3,2,1,0:T(8,128)(2,1)S(1)}, bf16[1,32,2,16,256]{4,3,2,1,0:T(8,128)(2,1)}, u32[]{:S(2)}) copy-start(bf16[1,32,2,16,256]{4,3,2,1,0:T(8,128)(2,1)} %param.6) | copy-start | bytes 1572868
  1.7 4.0 %copy-start.1 = (bf16[1,32,1,32,128]{4,3,2,1,0:T(8,128)(2,1)S(1)}, bf16[1,32,1,32,128]{4,3,2,1,0:T(8,128)(2,1)}, u32[]{:S(2)}) copy-start(bf16[1,32,1,32,128]{4,3,2,1,0:T(8,128)(2,1)} %param.11) | copy-start | bytes 786436
  1.7 4.0 %copy-start.2 = (bf16[32,64,3,3,3]{1,0,4,3,2:T(8,128)(2,1)S(1)}, bf16[32,64,3,3,3]{1,0,4,3,2:T(8,128)(2,1)}, u32[]{:S(2)}) copy-start(bf16[32,64,3,3,3]{1,0,4,3,2:T(8,128)(2,1)} %param.9) | copy-start | bytes 331780
  2.7 8.2 %collective-permute-start = (bf16[2,3,32,256]{3,2,1,0:T(8,128)(2,1)S(1)}, bf16[2,3,32,256]{3,2,1,0:T(8,128)(2,1)S(1)}, u32[]{:S(2)}, u32[]{:S(2)}) collective-permute-start(bf16[2,3,32,256]{3,2,1,0:T(8,128)(2,1)S(1)} %get-tuple-element.112), channel_id=1, source_target_pairs={{0,2},{2,0},{4,6},{6,4},{1,3},{3,1},{5,7},{7,5},{8,10},{10,8},{12,... | collective-permute-start | bytes 294920 | tf_op jit(solution)/shard_map/ppermute | solution.py:411
  5.7 5.2 %collective-permute-start.1 = (bf16[2,3,32,256]{3,2,1,0:T(8,128)(2,1)S(1)}, bf16[2,3,32,256]{3,2,1,0:T(8,128)(2,1)S(1)}, u32[]{:S(2)}, u32[]{:S(2)}) collective-permute-start(bf16[2,3,32,256]{3,2,1,0:T(8,128)(2,1)S(1)} %get-tuple-element.111), channel_id=1, source_target_pairs={{0,1},{1,0},{2,4},{3,5},{4,2},{5,3},{6,7},{7,6},{8,9},{9,8},{10,12... | collective-permute-start | bytes 294920 | tf_op jit(solution)/shard_map/ppermute | solution.py:424
  6.3 8.9 %collective-permute-start.4 = (bf16[10,32,128]{2,1,0:T(8,128)(2,1)S(1)}, bf16[10,32,128]{2,1,0:T(8,128)(2,1)S(1)}, u32[]{:S(2)}, u32[]{:S(2)}) collective-permute-start(bf16[10,32,128]{2,1,0:T(8,128)(2,1)S(1)} %get-tuple-element.115), channel_id=1, source_target_pairs={{0,2},{2,0},{4,6},{6,4},{1,3},{3,1},{5,7},{7,5},{8,10},{10,8},{12,... | collective-permute-start | bytes 245768 | tf_op jit(solution)/shard_map/ppermute | solution.py:429
  9.3 9.6 %collective-permute-start.5 = (bf16[10,32,128]{2,1,0:T(8,128)(2,1)S(1)}, bf16[10,32,128]{2,1,0:T(8,128)(2,1)S(1)}, u32[]{:S(2)}, u32[]{:S(2)}) collective-permute-start(bf16[10,32,128]{2,1,0:T(8,128)(2,1)S(1)} %get-tuple-element.114), channel_id=1, source_target_pairs={{0,4},{2,6},{4,0},{6,2},{1,5},{3,7},{5,1},{7,3},{8,12},{10,14},{12... | collective-permute-start | bytes 245768 | tf_op jit(solution)/shard_map/ppermute | solution.py:429
  9.3 9.6 %collective-permute-start.6 = (bf16[10,32,128]{2,1,0:T(8,128)(2,1)S(1)}, bf16[10,32,128]{2,1,0:T(8,128)(2,1)S(1)}, u32[]{:S(2)}, u32[]{:S(2)}) collective-permute-start(bf16[10,32,128]{2,1,0:T(8,128)(2,1)S(1)} %get-tuple-element.113), channel_id=1, source_target_pairs={{0,6},{2,4},{4,2},{6,0},{1,7},{3,5},{5,3},{7,1},{8,14},{10,12},{12... | collective-permute-start | bytes 245768 | tf_op jit(solution)/shard_map/ppermute | solution.py:429
  10.9 1.8 %copy-start.3 = (bf16[64,32,3,3,3]{0,1,4,3,2:T(8,128)(2,1)S(1)}, bf16[64,32,3,3,3]{0,1,4,3,2:T(8,128)(2,1)}, u32[]{:S(2)}) copy-start(bf16[64,32,3,3,3]{0,1,4,3,2:T(8,128)(2,1)} %param.7) | copy-start | bytes 331780
  10.9 2.0 %copy-start.4 = (f32[64]{0:T(128)S(1)}, f32[64]{0:T(128)}, u32[]{:S(2)}) copy-start(f32[64]{0:T(128)} %param.8) | copy-start | bytes 772
  11.1 9.5 %collective-permute-start.2 = (bf16[22,32,256]{2,1,0:T(8,128)(2,1)S(1)}, bf16[22,32,256]{2,1,0:T(8,128)(2,1)S(1)}, u32[]{:S(2)}, u32[]{:S(2)}) collective-permute-start(bf16[22,32,256]{2,1,0:T(8,128)(2,1)S(1)} %get-tuple-element.110), channel_id=1, source_target_pairs={{0,8},{8,0},{16,24},{24,16},{1,9},{9,1},{17,25},{25,17},{2,10},{10... | collective-permute-start | bytes 1081352 | tf_op jit(solution)/shard_map/ppermute | solution.py:411
  12.7 11.0 %collective-permute-start.3 = (bf16[22,32,256]{2,1,0:T(8,128)(2,1)S(1)}, bf16[22,32,256]{2,1,0:T(8,128)(2,1)S(1)}, u32[]{:S(2)}, u32[]{:S(2)}) collective-permute-start(bf16[22,32,256]{2,1,0:T(8,128)(2,1)S(1)} %get-tuple-element.109), channel_id=1, source_target_pairs={{0,1},{1,0},{8,16},{9,17},{16,8},{17,9},{24,25},{25,24},{2,3},{3,2... | collective-permute-start | bytes 1081352 | tf_op jit(solution)/shard_map/ppermute | solution.py:424
  15.2 10.3 %collective-permute-start.7 = (bf16[14,32,128]{2,1,0:T(8,128)(2,1)S(1)}, bf16[14,32,128]{2,1,0:T(8,128)(2,1)S(1)}, u32[]{:S(2)}, u32[]{:S(2)}) collective-permute-start(bf16[14,32,128]{2,1,0:T(8,128)(2,1)S(1)} %get-tuple-element.69), channel_id=1, source_target_pairs={{0,2},{2,0},{4,6},{6,4},{1,3},{3,1},{5,7},{7,5},{8,10},{10,8},{12,... | collective-permute-start | bytes 344072 | tf_op jit(solution)/shard_map/ppermute | solution.py:429
  18.9 7.7 %collective-permute-start.8 = (bf16[14,32,128]{2,1,0:T(8,128)(2,1)S(1)}, bf16[14,32,128]{2,1,0:T(8,128)(2,1)S(1)}, u32[]{:S(2)}, u32[]{:S(2)}) collective-permute-start(bf16[14,32,128]{2,1,0:T(8,128)(2,1)S(1)} %get-tuple-element.69), channel_id=1, source_target_pairs={{0,4},{2,6},{4,0},{6,2},{1,5},{3,7},{5,1},{7,3},{8,12},{10,14},{12... | collective-permute-start | bytes 344072 | tf_op jit(solution)/shard_map/ppermute | solution.py:429
  18.9 7.7 %collective-permute-start.9 = (bf16[14,32,128]{2,1,0:T(8,128)(2,1)S(1)}, bf16[14,32,128]{2,1,0:T(8,128)(2,1)S(1)}, u32[]{:S(2)}, u32[]{:S(2)}) collective-permute-start(bf16[14,32,128]{2,1,0:T(8,128)(2,1)S(1)} %get-tuple-element.69), channel_id=1, source_target_pairs={{0,6},{2,4},{4,2},{6,0},{1,7},{3,5},{5,3},{7,1},{8,14},{10,12},{12... | collective-permute-start | bytes 344072 | tf_op jit(solution)/shard_map/ppermute | solution.py:429
  20.5 11.0 %collective-permute-start.10 = (bf16[4,10,32,128]{3,2,1,0:T(8,128)(2,1)S(1)}, bf16[4,10,32,128]{3,2,1,0:T(8,128)(2,1)S(1)}, u32[]{:S(2)}, u32[]{:S(2)}) collective-permute-start(bf16[4,10,32,128]{3,2,1,0:T(8,128)(2,1)S(1)} %pad_maximum_fusion.2.co), channel_id=1, source_target_pairs={{0,8},{8,0},{16,24},{24,16},{1,9},{9,1},{17,25},{25,17},{2,10},{10... | collective-permute-start | bytes 983048 | tf_op jit(solution)/shard_map/ppermute | solution.py:411
  23.7 7.8 %collective-permute-start.11 = (bf16[4,10,32,128]{3,2,1,0:T(8,128)(2,1)S(1)}, bf16[4,10,32,128]{3,2,1,0:T(8,128)(2,1)S(1)}, u32[]{:S(2)}, u32[]{:S(2)}) collective-permute-start(bf16[4,10,32,128]{3,2,1,0:T(8,128)(2,1)S(1)} %pad_maximum_fusion.2.co), channel_id=1, source_target_pairs={{0,1},{1,0},{8,16},{9,17},{16,8},{17,9},{24,25},{25,24},{2,3},{3,2... | collective-permute-start | bytes 983048 | tf_op jit(solution)/shard_map/ppermute | solution.py:424
  26.6 8.7 %collective-permute-start.12 = (bf16[10,64,128]{2,1,0:T(8,128)(2,1)S(1)}, bf16[10,64,128]{2,1,0:T(8,128)(2,1)S(1)}, u32[]{:S(2)}, u32[]{:S(2)}) collective-permute-start(bf16[10,64,128]{2,1,0:T(8,128)(2,1)S(1)} %get-tuple-element.64.pooled.ur), channel_id=1, source_target_pairs={{0,8},{8,0},{16,24},{24,16},{1,9},{9,1},{17,25},{25,17},{2,10},{10... | collective-permute-start | bytes 491528 | tf_op jit(solution)/shard_map/ppermute | solution.py:411
  28.1 7.3 %collective-permute-start.13 = (bf16[10,64,128]{2,1,0:T(8,128)(2,1)S(1)}, bf16[10,64,128]{2,1,0:T(8,128)(2,1)S(1)}, u32[]{:S(2)}, u32[]{:S(2)}) collective-permute-start(bf16[10,64,128]{2,1,0:T(8,128)(2,1)S(1)} %get-tuple-element.64.pooled.ur), channel_id=1, source_target_pairs={{0,1},{1,0},{8,16},{9,17},{16,8},{17,9},{24,25},{25,24},{2,3},{3,2... | collective-permute-start | bytes 491528 | tf_op jit(solution)/shard_map/ppermute | solution.py:424
  37.9 2.0 %collective-permute-start.14 = (f32[7,160,128]{2,1,0:T(8,128)S(1)}, f32[7,160,128]{2,1,0:T(8,128)S(1)}, u32[]{:S(2)}, u32[]{:S(2)}) collective-permute-start(f32[7,160,128]{2,1,0:T(8,128)S(1)} %get-tuple-element.82), channel_id=1, source_target_pairs={{0,1},{1,0},{2,3},{3,2},{4,5},{5,4},{6,7},{7,6},{8,9},{9,8},{10,11... | collective-permute-start | bytes 1720328 | tf_op jit(solution)/shard_map/ppermute | solution.py:411
  40.1 7.0 %collective-permute-start.17 = (bf16[7,64,128]{2,1,0:T(8,128)(2,1)S(1)}, bf16[7,64,128]{2,1,0:T(8,128)(2,1)S(1)}, u32[]{:S(2)}, u32[]{:S(2)}) collective-permute-start(bf16[7,64,128]{2,1,0:T(8,128)(2,1)S(1)} %concatenate.24), channel_id=1, source_target_pairs={{0,6},{2,4},{4,2},{6,0},{1,7},{3,5},{5,3},{7,1},{8,14},{10,12},{12... | collective-permute-start | bytes 344072 | tf_op jit(solution)/shard_map/ppermute | solution.py:429
  41.7 7.1 %collective-permute-start.16 = (bf16[7,64,128]{2,1,0:T(8,128)(2,1)S(1)}, bf16[7,64,128]{2,1,0:T(8,128)(2,1)S(1)}, u32[]{:S(2)}, u32[]{:S(2)}) collective-permute-start(bf16[7,64,128]{2,1,0:T(8,128)(2,1)S(1)} %get-tuple-element.128), channel_id=1, source_target_pairs={{0,4},{2,6},{4,0},{6,2},{1,5},{3,7},{5,1},{7,3},{8,12},{10,14},{12... | collective-permute-start | bytes 344072 | tf_op jit(solution)/shard_map/ppermute | solution.py:429
  43.1 5.6 %collective-permute-start.15 = (bf16[7,64,128]{2,1,0:T(8,128)(2,1)S(1)}, bf16[7,64,128]{2,1,0:T(8,128)(2,1)S(1)}, u32[]{:S(2)}, u32[]{:S(2)}) collective-permute-start(bf16[7,64,128]{2,1,0:T(8,128)(2,1)S(1)} %get-tuple-element.127), channel_id=1, source_target_pairs={{0,2},{2,0},{4,6},{6,4},{1,3},{3,1},{5,7},{7,5},{8,10},{10,8},{12,... | collective-permute-start | bytes 344072 | tf_op jit(solution)/shard_map/ppermute | solution.py:429
  43.8 17.2 %copy-start.5 = (f32[32]{0:T(128)S(1)}, f32[32]{0:T(128)}, u32[]{:S(2)}) copy-start(f32[32]{0:T(128)} %param.10) | copy-start | bytes 388
  48.8 6.9 %collective-permute-start.21 = (bf16[256,128]{1,0:T(8,128)(2,1)S(1)}, bf16[256,128]{1,0:T(8,128)(2,1)S(1)}, u32[]{:S(2)}, u32[]{:S(2)}) collective-permute-start(bf16[256,128]{1,0:T(8,128)(2,1)S(1)} %bitcast.63), channel_id=1, source_target_pairs={{0,2},{2,0},{4,6},{6,4},{1,3},{3,1},{5,7},{7,5},{8,10},{10,8},{12,... | collective-permute-start | bytes 196616 | tf_op jit(solution)/shard_map/ppermute | solution.py:429
  49.7 12.5 %collective-permute-start.18 = (bf16[7,64,128]{2,1,0:T(8,128)(2,1)S(1)}, bf16[7,64,128]{2,1,0:T(8,128)(2,1)S(1)}, u32[]{:S(2)}, u32[]{:S(2)}) collective-permute-start(bf16[7,64,128]{2,1,0:T(8,128)(2,1)S(1)} %fusion.4), channel_id=1, source_target_pairs={{0,8},{8,0},{16,24},{24,16},{1,9},{9,1},{17,25},{25,17},{2,10},{10... | collective-permute-start | bytes 344072 | tf_op jit(solution)/shard_map/ppermute | solution.py:429
  51.3 11.4 %collective-permute-start.19 = (bf16[7,64,128]{2,1,0:T(8,128)(2,1)S(1)}, bf16[7,64,128]{2,1,0:T(8,128)(2,1)S(1)}, u32[]{:S(2)}, u32[]{:S(2)}) collective-permute-start(bf16[7,64,128]{2,1,0:T(8,128)(2,1)S(1)} %fusion.4), channel_id=1, source_target_pairs={{0,16},{8,24},{16,0},{24,8},{1,17},{9,25},{17,1},{25,9},{2,18},{10... | collective-permute-start | bytes 344072 | tf_op jit(solution)/shard_map/ppermute | solution.py:429
  53.2 9.5 %collective-permute-start.20 = (bf16[7,64,128]{2,1,0:T(8,128)(2,1)S(1)}, bf16[7,64,128]{2,1,0:T(8,128)(2,1)S(1)}, u32[]{:S(2)}, u32[]{:S(2)}) collective-permute-start(bf16[7,64,128]{2,1,0:T(8,128)(2,1)S(1)} %fusion.4), channel_id=1, source_target_pairs={{0,24},{8,16},{16,8},{24,0},{1,25},{9,17},{17,9},{25,1},{2,26},{10... | collective-permute-start | bytes 344072 | tf_op jit(solution)/shard_map/ppermute | solution.py:429
  54.4 4.8 %collective-permute-start.22 = (bf16[256,128]{1,0:T(8,128)(2,1)S(1)}, bf16[256,128]{1,0:T(8,128)(2,1)S(1)}, u32[]{:S(2)}, u32[]{:S(2)}) collective-permute-start(bf16[256,128]{1,0:T(8,128)(2,1)S(1)} %bitcast.62), channel_id=1, source_target_pairs={{0,4},{2,6},{4,0},{6,2},{1,5},{3,7},{5,1},{7,3},{8,12},{10,14},{12... | collective-permute-start | bytes 196616 | tf_op jit(solution)/shard_map/ppermute | solution.py:429
  55.8 5.2 %collective-permute-start.23 = (bf16[256,128]{1,0:T(8,128)(2,1)S(1)}, bf16[256,128]{1,0:T(8,128)(2,1)S(1)}, u32[]{:S(2)}, u32[]{:S(2)}) collective-permute-start(bf16[256,128]{1,0:T(8,128)(2,1)S(1)} %bitcast.61), channel_id=1, source_target_pairs={{0,6},{2,4},{4,2},{6,0},{1,7},{3,5},{5,3},{7,1},{8,14},{10,12},{12... | collective-permute-start | bytes 196616 | tf_op jit(solution)/shard_map/ppermute | solution.py:429
  62.8 1.6 %collective-permute-start.24 = (f32[7,64,128]{2,1,0:T(8,128)S(1)}, f32[7,64,128]{2,1,0:T(8,128)S(1)}, u32[]{:S(2)}, u32[]{:S(2)}) collective-permute-start(f32[7,64,128]{2,1,0:T(8,128)S(1)} %add_multiply_fusion.mine), channel_id=1, source_target_pairs={{0,1},{1,0},{2,3},{3,2},{4,5},{5,4},{6,7},{7,6},{8,9},{9,8},{10,11... | collective-permute-start | bytes 688136 | tf_op jit(solution)/shard_map/ppermute | solution.py:411

commit v4 on v3

--- a/solution.py
+++ b/solution.py
@@ -48,7 +48,7 @@
 
 def beside(place, below, first, second):
     use_first = jnp.where((place[0] == 1) == below, 1.0, 0.0)
-    use_second = (1.0 - use_first) * jnp.where(place[5] == 1, 1.0, 0.0)
+    use_second = (1.0 - use_first) * jnp.where(place[2] == 1, 1.0, 0.0)
     lanes = (1, first.shape[-1])
     return first[...] * jnp.full(lanes, use_first, F32).astype(BF) + second[...] * jnp.full(
         lanes, use_second, F32
@@ -172,25 +172,15 @@
             pre = acc[xp, t] + dot(w1b[2 * xp], two_rows(cells, 4 * t))
             above = pre > 0
             flags = jnp.where(above, 1.0, 0.0).astype(BF)
-            if t > 0:
-                mask[xp, 2 * t - 1] = flags[:, :half]
-            if 2 * t < rows2 - 2:
-                mask[xp, 2 * t] = flags[:, half:]
+            mask[xp, 2 * t] = flags[:, :half]
+            mask[xp, 2 * t + 1] = flags[:, half:]
             act = jnp.where(above, pre, 0.3 * pre)
             for b in range(4):
                 piece = act[b * c1 : (b + 1) * c1]
                 total = piece if total is None else total + piece
-        if t == 0:
-            total = total * jnp.where(at_low(total, half) & (place[1] == 0), 0.0, 1.0)
-        if t == rows2 // 2 - 1:
-            total = total * jnp.where(at_low(total, half) | (place[2] == 1), 1.0, 0.0)
         mean = (total * 0.125).astype(BF)
         pooled[2 * t] = mean[:, :half]
         pooled[2 * t + 1] = mean[:, half:]
-
-
-def at_low(value, half):
-    return lax.broadcasted_iota(jnp.int32, value.shape, 1) < half
 
 
 def with_shifts(store, plane, shifts):
@@ -233,83 +223,94 @@
             pieces[s, y + 1] = out[s * nf : (s + 1) * nf, width:]
 
 
-def own_body(co, pooled, w2r, wb, own_back, own_g2, own_b2, t_ref):
+def block_taps(block):
+    if block < 9:
+        return block * 3, block * 3 + 1
+    first = 2 * (block - 9)
+    return first * 3 + 2, (first + 1) * 3 + 2 if first < 8 else 27
+
+
+def fill_plane(t_ref, plane):
+    for s in range(plane.shape[0]):
+        nf = plane.shape[2]
+        t_ref[:, s * nf : (s + 1) * nf] = plane[s]
+
+
+def pair_rows(t_ref, t):
+    rows, chans, width = t_ref.shape
+    return jnp.concatenate(
+        [t_ref[2 * t + n : 2 * t + n + 3].reshape(3 * chans, width) for n in range(2)], axis=1
+    )
+
+
+def rows_wide(t_ref):
+    count = t_ref.shape[0] - 2
+    return jnp.concatenate(
+        [
+            jnp.concatenate([t_ref[y + ys] for y in range(count)], axis=1)
+            for ys in range(3)
+        ],
+        axis=0,
+    )
+
+
+def own_body(co, pooled, w2r, wb, wide, own_back, own_g2, own_b2, t_ref):
     count, rows, nf, width = co.shape
     pairs = w2r.shape[1]
     c1 = pooled.shape[1]
     c2 = count * nf
-    fill_planes(t_ref, co, shift_both(width))
+    fill_plane(t_ref, co)
     eye = identity(2 * c1)
     for p in range(pairs):
         block = jnp.concatenate([w2r[s, p] for s in range(count)], axis=0)
-        turned = dot_nt(eye, block)
+        turned = dot_nt(eye, block).astype(BF)
         for half, d in ((0, p), (1, p + pairs)):
             if d < 27:
                 i, j, k = d // 9, (d // 3) % 3, d % 3
-                at = ((2 - j) * 3 + (2 - k)) * c2
-                wb[2 - i, :, at : at + c2] = turned[half * c1 : (half + 1) * c1].astype(BF)
+                at = (2 - j) * c2
+                wb[2 - i, k * c1 : (k + 1) * c1, at : at + c2] = turned[
+                    half * c1 : (half + 1) * c1
+                ]
     for t in range((rows - 2) // 2):
         own_back[t] = dot(wb[1], pair_rows(t_ref, t))
-    rhs = pooled_wide(pooled)
-    for ys in range(3):
-        out = dot_nt(rows_wide(t_ref, ys, rows - 2), rhs)
-        for zs in range(3):
-            own_g2[(2 - ys) * 3 + (2 - zs)] = out[zs * c2 : (zs + 1) * c2]
+    cells2 = pooled.shape[0]
+    moved = dot(pooled[...].reshape(cells2 * c1, width), shift_both(width)).astype(BF)
+    for y in range(cells2):
+        lanes = slice(y * width, (y + 1) * width)
+        after = moved[y * c1 : (y + 1) * c1, width:]
+        wide[0:c1, lanes] = moved[y * c1 : (y + 1) * c1, :width]
+        wide[c1 : 2 * c1, lanes] = pooled[y]
+        wide[2 * c1 : 3 * c1, lanes] = after
+        wide[3 * c1 : 4 * c1, lanes] = after
+    own_g2[...] = dot_nt(rows_wide(t_ref), wide[...])
     sums = None
     for y in range(1, rows - 1):
-        v = t_ref[y, 1].astype(F32)
+        v = t_ref[y].astype(F32)
         sums = v if sums is None else sums + v
     own_b2[...] = jnp.broadcast_to(jnp.sum(sums, axis=1, keepdims=True), own_b2.shape)
 
 
-def fill_planes(t_ref, plane, shifts):
-    nf = plane.shape[2]
-    for s in range(plane.shape[0]):
-
-        def store(k, value, s=s):
-            t_ref[:, k, s * nf : (s + 1) * nf] = value
-
-        with_shifts(store, plane[s], shifts)
-
-
-def pair_rows(t_ref, t):
-    rows, slots, chans, width = t_ref.shape
-    return jnp.concatenate(
-        [t_ref[2 * t + n : 2 * t + n + 3].reshape(3 * slots * chans, width) for n in range(2)],
-        axis=1,
-    )
-
-
-def rows_wide(t_ref, ys, count):
-    rows, slots, chans, width = t_ref.shape
-    return jnp.concatenate(
-        [t_ref[y + ys].reshape(slots * chans, width) for y in range(count)], axis=1
-    )
-
-
-def pooled_wide(pooled):
-    return jnp.concatenate(
-        [
-            jnp.concatenate([pooled[y], pooled[y]], axis=0)
-            for y in range(1, pooled.shape[0] - 1)
-        ],
-        axis=1,
-    )
-
-
-def back_body(place, mask, pooled, ca, cb, wb, own_back, gp, g2, bias1, t0, t2):
+def back_body(place, mask, wide, ca, cb, wb, own_back, gp, g2, bias1, t0, t2):
     count, rows, nf, width = ca.shape
-    c1 = pooled.shape[1]
-    c2 = count * nf
-    shifts = shift_both(width)
-    fill_planes(t0, beside(place, True, ca, cb), shifts)
-    fill_planes(t2, beside(place, False, ca, cb), shifts)
+    c1 = wide.shape[0] // 4
+    fill_plane(t0, beside(place, True, ca, cb))
+    fill_plane(t2, beside(place, False, ca, cb))
     sums = jnp.zeros((8, 4 * c1), F32)
     ones = jnp.ones((8, 2 * width), BF)
-    n_pairs = (rows - 2) // 2
-    for t in range(n_pairs):
+    lane = lax.broadcasted_iota(jnp.int32, (c1, width), 1)
+    for t in range((rows - 2) // 2):
         acc = own_back[t] + dot(wb[0], pair_rows(t0, t)) + dot(wb[2], pair_rows(t2, t))
-        eighth = acc * 0.125
+        rows_back = []
+        for n in range(2):
+            part = acc[:, n * width : (n + 1) * width]
+            ahead = pltpu.roll(part[:c1], width - 1, 1)
+            behind = pltpu.roll(part[2 * c1 :], 1, 1)
+            rows_back.append(
+                part[c1 : 2 * c1]
+                + jnp.where(lane < width - 1, ahead, 0.0)
+                + jnp.where(lane > 0, behind, 0.0)
+            )
+        eighth = jnp.concatenate(rows_back, axis=1) * 0.125
         spread = jnp.concatenate([eighth] * 4, axis=0)
         for xp in range(2):
             flags = jnp.concatenate([mask[xp, 2 * t], mask[xp, 2 * t + 1]], axis=1)
@@ -317,12 +318,8 @@
             gp[xp, t] = grad
             sums = sums + dot_nt(ones, grad)
     bias1[...] = sums
-    rhs = pooled_wide(pooled)
-    for n, t_ref in enumerate((t0, t2)):
-        for ys in range(3):
-            out = dot_nt(rows_wide(t_ref, ys, rows - 2), rhs)
-            for zs in range(3):
-                g2[n, (2 - ys) * 3 + (2 - zs)] = out[zs * c2 : (zs + 1) * c2]
+    g2[0] = dot_nt(rows_wide(t0), wide[...])
+    g2[1] = dot_nt(rows_wide(t2), wide[...])
 
 
 def weights_body(place, cells, low, high, gp, g2, bias1, own_g2, own_b2, keep, send, red):
@@ -333,14 +330,17 @@
     pairs = 14
     sources = (low, cells.at[0], cells.at[1], high)
 
-    def part2(d):
-        if d == 27:
-            return own_b2[...]
-        return own_g2[d - 9] if 9 <= d < 18 else g2[1 - d // 18, d % 9]
+    def part2(ij):
+        x, ys = 2 - ij // 3, 2 - ij % 3
+        rows_of = slice(ys * c2, (ys + 1) * c2)
+        return own_g2[rows_of] if x == 1 else g2[x // 2, rows_of]
 
     low_wide = lax.broadcasted_iota(jnp.int32, (c2, 2 * c1), 1) < c1
-    for p in range(pairs):
-        red[p, :c2] = jnp.where(low_wide, part2(p), part2(p + pairs))
+    for ij in range(9):
+        red[ij, :c2] = part2(ij)[:, : 2 * c1]
+    for m in range(5):
+        other = part2(2 * m + 1)[:, 2 * c1 :] if m < 4 else own_b2[...]
+        red[9 + m, :c2] = jnp.where(low_wide, part2(2 * m)[:, 2 * c1 :], other)
     lane = lax.broadcasted_iota(jnp.int32, (cin, 2 * c1), 1)
     low_half = lane < c1
     lows, highs = {}, {}
@@ -348,7 +348,7 @@
         acc = None
         for xp in range(2):
             for t in range(n_pairs):
-                lhs = two_rows(sources[xp + i], 4 * t + 2)
+                lhs = two_rows(sources[xp + i], 4 * t)
                 part = dot_nt(lhs, gp[xp, t])
                 acc = part if acc is None else acc + part
         for j in range(3):
@@ -358,20 +358,18 @@
                 r1 = ((j + 1) * 4 + slot) * cin
                 slots.append(acc[r0 : r0 + cin, : 2 * c1] + acc[r1 : r1 + cin, 2 * c1 :])
             turned = [pltpu.roll(v, c1, 1) for v in slots]
-            for k in range(3):
-                d = (i * 3 + j) * 3 + k
-                if d < pairs:
-                    lows[d] = slots[k] + turned[k + 1]
-                else:
-                    highs[d - pairs] = slots[k + 1] + turned[k]
+            n = i * 3 + j
+            red[n, c2:] = jnp.where(low_half, slots[0], slots[2]) + turned[1]
+            lows[n] = slots[2] + turned[3]
+            highs[n] = slots[3] + turned[2]
     b1 = bias1[:, : 2 * c1] + bias1[:, 2 * c1 :]
     b1 = b1 + pltpu.roll(b1, c1, 1)
-    highs[pairs - 1] = jnp.concatenate([b1] * (cin // 8), axis=0)
-    for p in range(pairs):
-        red[p, c2:] = jnp.where(low_half, lows[p], highs[p])
+    highs[9] = jnp.concatenate([b1] * (cin // 8), axis=0)
+    for m in range(5):
+        red[9 + m, c2:] = jnp.where(low_half, lows[2 * m], highs[2 * m + 1])
     hp = pairs // 2
-    keep[...] = red[pl.ds(place[4] * hp, hp)]
-    send[...] = red[pl.ds((1 - place[4]) * hp, hp)]
+    keep[...] = red[pl.ds(place[1] * hp, hp)]
+    send[...] = red[pl.ds((1 - place[1]) * hp, hp)]
 
 
 def unpack_body(me, *refs):
@@ -387,13 +385,13 @@
 def finish_body(place, mine, other, g2, b2, g1, b1):
     hp, _, width = mine.shape
     nf, c1 = g2.shape[1], g2.shape[2]
-    first = place[4] == 0
+    first = place[1] == 0
     got, more = mine[...], other[...]
     halves = (jnp.where(first, got, more), jnp.where(first, more, got))
     for p in range(2 * hp):
         block = halves[p // hp][p % hp]
         turned = pltpu.roll(block, c1, 1)
-        for d, v in ((p, block), (p + 2 * hp, turned)):
+        for d, v in zip(block_taps(p), (block, turned)):
             low, high = v[:nf, :c1], v[nf:, :c1]
             if d < 27:
                 g2[d] = low
@@ -456,10 +454,10 @@
     place = jnp.stack(
         [
             jnp.asarray(v, jnp.int32)
-            for v in (odd_x, sy > 0, sy < n_sy - 1, sx, rep, (sx > 0) & (sx < n_sx - 1))
+            for v in (odd_x, rep, (sx > 0) & (sx < n_sx - 1))
         ]
     )
-    rim = 3
+    rim = 1
 
     w1 = first_kernel.transpose(2, 3, 4, 1, 0)
     w1q = jnp.concatenate(
@@ -508,7 +506,7 @@
     w2p, vr = lax.optimization_barrier((w2p, vr))
     wgot = [w2p] + [to_partner(w2p, "sy", s) for s in range(1, n_sy)]
 
-    pooled_rows = own2 + 2
+    pooled_rows = own2
     cell_shape = (rows + 2 * rim, 4 * cin, width // 2)
     cells, w1b, acc = call(
         conv1_own_body,
@@ -540,19 +538,31 @@
         smem_ins=1,
         flops=1 << 30,
     )
-    wgot, pooled = lax.optimization_barrier((wgot, pooled))
+    wgot, _ = lax.optimization_barrier((wgot, pooled))
     w2r = jnp.stack(wgot)
-    ua = swap_first(pooled, "sx")
-    ub = swap_second(pooled, "sx")
-
-    plane_shape = (own2 + 2, 3, c2, width2)
-    wb, own_back, own_g2, own_b2 = call(
+    pa = swap_first(jnp.where(odd_y == 1, pooled[0], pooled[own2 - 1]), "sy")
+    pb = swap_second(jnp.where(odd_y == 1, pooled[own2 - 1], pooled[0]), "sy")
+    pb = jnp.where((sy > 0) & (sy < n_sy - 1), pb, jnp.zeros_like(pb))
+    ur = jnp.concatenate(
+        [
+            jnp.where(odd_y == 1, pa, pb)[None],
+            pooled,
+            jnp.where(odd_y == 1, pb, pa)[None],
+        ],
+        axis=0,
+    )
+    ua = swap_first(ur, "sx")
+    ub = swap_second(ur, "sx")
+
+    plane_shape = (own2 + 2, c2, width2)
+    wb, wide, own_back, own_g2, own_b2 = call(
         own_body,
         "backward_own",
         [
-            jax.ShapeDtypeStruct((3, c1, 9 * c2), BF),
-            jax.ShapeDtypeStruct((own2 // 2, c1, 2 * width2), F32),
-            jax.ShapeDtypeStruct((9, c2, 2 * c1), F32),
+            jax.ShapeDtypeStruct((3, 3 * c1, 3 * c2), BF),
+            jax.ShapeDtypeStruct((4 * c1, own2 * width2), BF),
+            jax.ShapeDtypeStruct((own2 // 2, 3 * c1, 2 * width2), F32),
+            jax.ShapeDtypeStruct((3 * c2, 4 * c1), F32),
             jax.ShapeDtypeStruct((c2, 2 * c1), F32),
         ],
         [pltpu.VMEM(plane_shape, BF)],
@@ -566,15 +576,14 @@
         "backward",
         [
             jax.ShapeDtypeStruct((2, own2 // 2, 4 * c1, width), BF),
-            jax.ShapeDtypeStruct((2, 9, c2, 2 * c1), F32),
+            jax.ShapeDtypeStruct((2, 3 * c2, 4 * c1), F32),
             jax.ShapeDtypeStruct((8, 4 * c1), F32),
         ],
         [pltpu.VMEM(plane_shape, BF), pltpu.VMEM(plane_shape, BF)],
-        (place, mask, pooled, ca, cb, wb, own_back),
+        (place, mask, wide, ca, cb, wb, own_back),
         smem_ins=1,
         flops=2 << 30,
     )
-    gp, ua, ub = lax.optimization_barrier((gp, ua, ub))
     keep, send = call(
         weights_body,
         "first_weights",
@@ -585,6 +594,7 @@
         flops=3 << 30,
     )
 
+    send, ua, ub = lax.optimization_barrier((send, ua, ub))
     half = keep + swap_first(send, "rep")
     half, ua, ub = lax.optimization_barrier((half, ua, ub))
     half_bf = half.astype(BF)
@@ -600,16 +610,18 @@
         "conv2",
         jax.ShapeDtypeStruct((n_sy, own2, nf, width2), BF),
         [pltpu.VMEM((3, own2 + 2, 3, c1, width2), BF)],
-        (place, pooled, ua, ub, w2r),
+        (place, ur, ua, ub, w2r),
         smem_ins=1,
         flops=1 << 30,
     )
     own = jnp.concatenate([half[:, :nf], tail.astype(F32)], axis=1)
+    flat = pieces.reshape(n_sy, own2 * nf, width2)
+    beside_sy = to_partner(flat[1], "sy", 1)
+    got, beside_sy = lax.optimization_barrier((got, beside_sy))
     part = tree_sum([own] + got).astype(BF)
-    part, pieces = lax.optimization_barrier((part, pieces))
+    part, flat = lax.optimization_barrier((part, flat))
     parts = [part] + [to_partner(part, "sx", s) for s in range(1, n_sx)]
-    flat = pieces.reshape(n_sy, own2 * nf, width2)
-    out_got = [flat[0]] + [to_partner(flat[s], "sy", s) for s in range(1, n_sy)]
+    out_got = [flat[0], beside_sy] + [to_partner(flat[s], "sy", s) for s in range(2, n_sy)]
     bias_wide = jnp.broadcast_to(second_bias[:, None, None], (nf, 1, width2))
     second_out = call(
         unpack_body,

time: 66.2 us -> 64.3 us (0.971)
  Pallas kernels: 17.6 us -> 15.6 us
  starting transfers between devices: 31 us -> 32.7 us
  waiting for transfers between devices: 14.2 us -> 12.6 us
    pallas_call x10, Pallas kernels: 17.6 us -> 15.6 us  [call(): pl.pallas_call(body, name=name, out_shape=outs, in_specs=[sm] * smem_ins...]
    ppermute x15, waiting for transfers between devices: 9.1 us -> 7.45 us  [to_partner(): return lax.ppermute(value, axis, [(i, i ^ s) for i in range(count)])]
    ppermute x15, starting transfers between devices: 21.6 us -> 22.3 us  [to_partner(): return lax.ppermute(value, axis, [(i, i ^ s) for i in range(count)])]
    ppermute x6 -> x7, starting transfers between devices: 9.44 us -> 10.1 us  [swap_first(): return lax.ppermute(value, axis, [(i, i ^ 1) for i in range(count)])]
    ppermute x6 -> x7, waiting for transfers between devices: 5.12 us -> 5.14 us  [swap_first(): return lax.ppermute(value, axis, [(i, i ^ 1) for i in range(count)])]
  transfers between devices with their start and end apart: 25 -> 27, of which waited for: 9 -> 10; matrix products, arithmetic and copies ran while one was open for 1% -> 1% of each run, Pallas kernels for 19% -> 20%
where the time goes in v4:
time: 64.3 us; the launch traced here: 64.1 us
  starting transfers between devices  32.7 us (51%)
  Pallas kernels  15.6 us (24%)
  waiting for transfers between devices  12.6 us (20%)
  local copies, waits for them, and re-layouts  1.35 us (2%)
  between operations  1 us (2%)
  other arithmetic  0.86 us (1%)
    ppermute x15, starting transfers between devices, to_partner(): return lax.ppermute(value, axis, [(i, i ^ s) for i in range(count)])  22.3 us
    pallas_call x10, Pallas kernels, call(): pl.pallas_call(body, name=name, out_shape=outs, in_specs=[sm] * smem_ins...  15.6 us
    ppermute x7, starting transfers between devices, swap_first(): return lax.ppermute(value, axis, [(i, i ^ 1) for i in range(count)])  10.1 us
    ppermute x15, waiting for transfers between devices, to_partner(): return lax.ppermute(value, axis, [(i, i ^ s) for i in range(count)])  7.45 us
    ppermute x7, waiting for transfers between devices, swap_first(): return lax.ppermute(value, axis, [(i, i ^ 1) for i in range(count)])  5.14 us
  transfers between devices with their start and end apart: 27, of which 10 were waited for; matrix products, arithmetic and copies ran while one was open for 1% of the time, Pallas kernels for 20%

profile of v4, /device:TPU:0, one launch (start us, length us, event | category | flops | bytes accessed | tf_op | source)
XLA Modules:
  0.0 64.1 jit_solution(13929615155439844407)
XLA Ops:
  0.7 1.0 %copy-done = bf16[1,32,2,16,256]{4,3,2,1,0:T(8,128)(2,1)S(1)} copy-done((bf16[1,32,2,16,256]{4,3,2,1,0:T(8,128)(2,1)S(1)}, bf16[1,32,2,16,256]{4,3,2,1,0:T(8,128)(2,1)}, u32[]{:S(2)}) %copy-start) | copy-done | bytes 524312
  1.7 0.9 %volume_cells.1 = bf16[2,16,32,256]{3,2,1,0:T(8,128)(2,1)S(1)} custom-call(bf16[32,2,16,256]{3,2,1,0:T(8,128)(2,1)S(1)} %bitcast.59), custom_call_target="tpu_custom_call" | custom-call | flops 1073741824 | bytes 1048576 | tf_op jit(solution)/shard_map/volume_cells/pallas_call | solution.py:61
  2.7 3.0 %collective-permute-start = (bf16[2,1,32,256]{3,2,1,0:T(8,128)(2,1)S(1)}, bf16[2,1,32,256]{3,2,1,0:T(8,128)(2,1)S(1)}, u32[]{:S(2)}, u32[]{:S(2)}) collective-permute-start(bf16[2,1,32,256]{3,2,1,0:T(8,128)(2,1)S(1)} %get-tuple-element.120), channel_id=1, source_target_pairs={{0,2},{2,0},{4,6},{6,4},{1,3},{3,1},{5,7},{7,5},{8,10},{10,8},{12,... | collective-permute-start | bytes 98312 | tf_op jit(solution)/shard_map/ppermute | solution.py:409
  5.7 0.0 copy-start.3
  5.7 0.0 copy-start.4
  5.7 0.5 cotangent_cells.1
  6.3 3.0 %collective-permute-start.4 = (bf16[10,32,128]{2,1,0:T(8,128)(2,1)S(1)}, bf16[10,32,128]{2,1,0:T(8,128)(2,1)S(1)}, u32[]{:S(2)}, u32[]{:S(2)}) collective-permute-start(bf16[10,32,128]{2,1,0:T(8,128)(2,1)S(1)} %get-tuple-element.123), channel_id=1, source_target_pairs={{0,2},{2,0},{4,6},{6,4},{1,3},{3,1},{5,7},{7,5},{8,10},{10,8},{12,... | collective-permute-start | bytes 245768 | tf_op jit(solution)/shard_map/ppermute | solution.py:427
  9.3 1.5 %collective-permute-start.6 = (bf16[10,32,128]{2,1,0:T(8,128)(2,1)S(1)}, bf16[10,32,128]{2,1,0:T(8,128)(2,1)S(1)}, u32[]{:S(2)}, u32[]{:S(2)}) collective-permute-start(bf16[10,32,128]{2,1,0:T(8,128)(2,1)S(1)} %get-tuple-element.121), channel_id=1, source_target_pairs={{0,6},{2,4},{4,2},{6,0},{1,7},{3,5},{5,3},{7,1},{8,14},{10,12},{12... | collective-permute-start | bytes 245768 | tf_op jit(solution)/shard_map/ppermute | solution.py:427
  10.8 0.2 fusion.2.w1q
  11.0 0.1 pad_add_fusion.place
  11.1 0.1 broadcast_in_dim_tile.4.bias
  11.3 0.1 pad_maximum_fusion.vr
  11.4 1.6 %collective-permute-start.2 = (bf16[18,32,256]{2,1,0:T(8,128)(2,1)S(1)}, bf16[18,32,256]{2,1,0:T(8,128)(2,1)S(1)}, u32[]{:S(2)}, u32[]{:S(2)}) collective-permute-start(bf16[18,32,256]{2,1,0:T(8,128)(2,1)S(1)} %get-tuple-element.118), channel_id=1, source_target_pairs={{0,8},{8,0},{16,24},{24,16},{1,9},{9,1},{17,25},{25,17},{2,10},{10... | collective-permute-start | bytes 884744 | tf_op jit(solution)/shard_map/ppermute | solution.py:409
  13.1 0.0 collective-permute-start.3
  13.1 1.7 %conv1_own.1 = (bf16[2,18,128,128]{3,2,1,0:T(8,128)(2,1)S(1)}, bf16[3,256,512]{2,1,0:T(8,128)(2,1)S(1)}, f32[2,4,256,256]{3,2,1,0:T(8,128)S(1)}) custom-call(bf16[2,18,32,256]{3,2,1,0:T(8,128)(2,1)S(1)} %pad_maximum_fusion.vr, bf16[3,3,4,32,128]{4,3,2,1,0:T(8,128)(2,1)S(1)} %fusion.2.w1q, f32[256,1]{1,0:T(8,128)S(1)} %broadcast_in_dim_tile.4.bias), custom_call_target="tpu_custom_call" | custom-call | flops 2147483648 | bytes 1048576 | tf_op jit(solution)/shard_map/conv1_own/pallas_call | solution.py:61
  14.8 0.0 collective-permute-done.4
  14.8 2.0 %collective-permute-start.7 = (bf16[14,32,128]{2,1,0:T(8,128)(2,1)S(1)}, bf16[14,32,128]{2,1,0:T(8,128)(2,1)S(1)}, u32[]{:S(2)}, u32[]{:S(2)}) collective-permute-start(bf16[14,32,128]{2,1,0:T(8,128)(2,1)S(1)} %get-tuple-element.72), channel_id=1, source_target_pairs={{0,2},{2,0},{4,6},{6,4},{1,3},{3,1},{5,7},{7,5},{8,10},{10,8},{12,... | collective-permute-start | bytes 344072 | tf_op jit(solution)/shard_map/ppermute | solution.py:427
  16.8 0.0 collective-permute-done.5
  16.8 0.0 collective-permute-start.8
  16.8 0.0 collective-permute-done.6
  16.9 1.5 %collective-permute-start.9 = (bf16[14,32,128]{2,1,0:T(8,128)(2,1)S(1)}, bf16[14,32,128]{2,1,0:T(8,128)(2,1)S(1)}, u32[]{:S(2)}, u32[]{:S(2)}) collective-permute-start(bf16[14,32,128]{2,1,0:T(8,128)(2,1)S(1)} %get-tuple-element.72), channel_id=1, source_target_pairs={{0,6},{2,4},{4,2},{6,0},{1,7},{3,5},{5,3},{7,1},{8,14},{10,12},{12... | collective-permute-start | bytes 344072 | tf_op jit(solution)/shard_map/ppermute | solution.py:427
  18.4 0.7 %collective-permute-done.2.za = bf16[18,32,256]{2,1,0:T(8,128)(2,1)S(1)} collective-permute-done((bf16[18,32,256]{2,1,0:T(8,128)(2,1)S(1)}, bf16[18,32,256]{2,1,0:T(8,128)(2,1)S(1)}, u32[]{:S(2)}, u32[]{:S(2)}) %collective-permute-start.2) | collective-permute-done | bytes 294944 | tf_op jit(solution)/shard_map/ppermute | solution.py:409
  19.1 2.5 %collective-permute-start.10 = (bf16[4,10,32,128]{3,2,1,0:T(8,128)(2,1)S(1)}, bf16[4,10,32,128]{3,2,1,0:T(8,128)(2,1)S(1)}, u32[]{:S(2)}, u32[]{:S(2)}) collective-permute-start(bf16[4,10,32,128]{3,2,1,0:T(8,128)(2,1)S(1)} %pad_maximum_fusion.2.co), channel_id=1, source_target_pairs={{0,8},{8,0},{16,24},{24,16},{1,9},{9,1},{17,25},{25,17},{2,10},{10... | collective-permute-start | bytes 983048 | tf_op jit(solution)/shard_map/ppermute | solution.py:409
  21.7 0.0 collective-permute-done.3.zb
  21.7 0.0 collective-permute-start.11
  21.7 1.6 %conv1.1 = (bf16[18,128,128]{2,1,0:T(8,128)(2,1)S(1)}, bf16[18,128,128]{2,1,0:T(8,128)(2,1)S(1)}, bf16[2,8,256,128]{3,2,1,0:T(8,128)(2,1)S(1)}, bf16[8,64,128]{2,1,0:T(8,128)(2,1)S(1)}) custom-call(s32[3]{0:T(128)S(1)} %pad_add_fusion.place, bf16[18,32,256]{2,1,0:T(8,128)(2,1)S(1)} %collective-permute-done.2.za, ...), custom_call_target="tpu_custom_call" | custom-call | flops 1073741824 | bytes 1048576 | tf_op jit(solution)/shard_map/conv1/pallas_call | solution.py:61
  23.3 1.3 %collective-permute-done.8 = bf16[14,32,128]{2,1,0:T(8,128)(2,1)S(1)} collective-permute-done((bf16[14,32,128]{2,1,0:T(8,128)(2,1)S(1)}, bf16[14,32,128]{2,1,0:T(8,128)(2,1)S(1)}, u32[]{:S(2)}, u32[]{:S(2)}) %collective-permute-start.8) | collective-permute-done | bytes 114720 | tf_op jit(solution)/shard_map/ppermute | solution.py:427
  24.6 0.0 collective-permute-done.9
  24.6 0.8 %collective-permute-start.12 = (bf16[64,128]{1,0:T(8,128)(2,1)S(1)}, bf16[64,128]{1,0:T(8,128)(2,1)S(1)}, u32[]{:S(2)}, u32[]{:S(2)}) collective-permute-start(bf16[64,128]{1,0:T(8,128)(2,1)S(1)} %get-tuple-element.133), channel_id=1, source_target_pairs={{0,2},{2,0},{4,6},{6,4},{1,3},{3,1},{5,7},{7,5},{8,10},{10,8},{12,... | collective-permute-start | bytes 49160 | tf_op jit(solution)/shard_map/ppermute | solution.py:409
  25.4 0.2 collective-permute-start.13
  25.6 0.1 pad_maximum_fusion.1.w2r
  25.7 1.3 %backward_own.1 = (bf16[3,192,384]{2,1,0:T(8,128)(2,1)S(1)}, bf16[256,1024]{1,0:T(8,128)(2,1)S(1)}, f32[4,192,256]{2,1,0:T(8,128)S(1)}, f32[384,256]{1,0:T(8,128)S(1)}, f32[128,128]{1,0:T(8,128)S(1)}) custom-call(bf16[4,10,32,128]{3,2,1,0:T(8,128)(2,1)S(1)} %pad_maximum_fusion.2.co, bf16[8,64,128]{2,1,0:T(8,128)(2,1)S(1)} %get-tuple-element.70.pooled, ...), custom_call_target="tpu_custom_call" | custom-call | flops 2147483648 | bytes 1048576 | tf_op jit(solution)/shard_map/backward_own/pallas_call | solution.py:61
  27.0 1.4 %collective-permute-done.12 = bf16[64,128]{1,0:T(8,128)(2,1)S(1)} collective-permute-done((bf16[64,128]{1,0:T(8,128)(2,1)S(1)}, bf16[64,128]{1,0:T(8,128)(2,1)S(1)}, u32[]{:S(2)}, u32[]{:S(2)}) %collective-permute-start.12) | collective-permute-done | bytes 16416 | tf_op jit(solution)/shard_map/ppermute | solution.py:409
  28.3 0.0 collective-permute-done.13
  28.4 1.5 %collective-permute-start.14 = (bf16[10,64,128]{2,1,0:T(8,128)(2,1)S(1)}, bf16[10,64,128]{2,1,0:T(8,128)(2,1)S(1)}, u32[]{:S(2)}, u32[]{:S(2)}) collective-permute-start(bf16[10,64,128]{2,1,0:T(8,128)(2,1)S(1)} %pad_maximum_fusion.3.ur), channel_id=1, source_target_pairs={{0,8},{8,0},{16,24},{24,16},{1,9},{9,1},{17,25},{25,17},{2,10},{10... | collective-permute-start | bytes 491528 | tf_op jit(solution)/shard_map/ppermute | solution.py:409
  29.9 2.6 %backward.1 = (bf16[2,4,256,256]{3,2,1,0:T(8,128)(2,1)S(1)}, f32[2,384,256]{2,1,0:T(8,128)S(1)}, f32[8,256]{1,0:T(8,128)S(1)}) custom-call(s32[3]{0:T(128)S(1)} %pad_add_fusion.place, bf16[2,8,256,128]{3,2,1,0:T(8,128)(2,1)S(1)} %get-tuple-element.65.mask, bf16[256,1024]{1,0:T(8,128)(2,1)S(1)} %get-tuple-element.76.wide, ...), custom_call_target="tpu_custom_call" | custom-call | flops 2147483648 | bytes 1048576 | tf_op jit(solution)/shard_map/backward/pallas_call | solution.py:61
  32.5 2.6 %first_weights.1 = (f32[7,160,128]{2,1,0:T(8,128)S(1)}, f32[7,160,128]{2,1,0:T(8,128)S(1)}) custom-call(s32[3]{0:T(128)S(1)} %pad_add_fusion.place, bf16[2,18,128,128]{3,2,1,0:T(8,128)(2,1)S(1)} %get-tuple-element.58.cells, bf16[18,128,128]{2,1,0:T(8,128)(2,1)S(1)} %get-tuple-element.63.low, bf16[18,128,128]{2,1,0:T(8,128)(2,1)S(1)} %get-tuple-element.64.high, ...), custom_call_target="tpu_custom_call" | custom-call | flops 3221225472 | bytes 1048576 | tf_op jit(solution)/shard_map/first_weights/pallas_call | solution.py:61
  35.1 0.0 collective-permute-done.14.ua
  35.1 0.6 collective-permute-start.16
  35.7 1.6 %collective-permute-done.16 = f32[7,160,128]{2,1,0:T(8,128)S(1)} collective-permute-done((f32[7,160,128]{2,1,0:T(8,128)S(1)}, f32[7,160,128]{2,1,0:T(8,128)S(1)}, u32[]{:S(2)}, u32[]{:S(2)}) %collective-permute-start.16) | collective-permute-done | bytes 573472 | tf_op jit(solution)/shard_map/ppermute | solution.py:409
  37.3 0.1 add.34
  37.5 3.0 %collective-permute-start.17 = (bf16[7,64,128]{2,1,0:T(8,128)(2,1)S(1)}, bf16[7,64,128]{2,1,0:T(8,128)(2,1)S(1)}, u32[]{:S(2)}, u32[]{:S(2)}) collective-permute-start(bf16[7,64,128]{2,1,0:T(8,128)(2,1)S(1)} %get-tuple-element.137), channel_id=1, source_target_pairs={{0,2},{2,0},{4,6},{6,4},{1,3},{3,1},{5,7},{7,5},{8,10},{10,8},{12,... | collective-permute-start | bytes 344072 | tf_op jit(solution)/shard_map/ppermute | solution.py:427
  40.5 0.0 collective-permute-start.18
  40.5 1.5 %collective-permute-start.19 = (bf16[7,64,128]{2,1,0:T(8,128)(2,1)S(1)}, bf16[7,64,128]{2,1,0:T(8,128)(2,1)S(1)}, u32[]{:S(2)}, u32[]{:S(2)}) collective-permute-start(bf16[7,64,128]{2,1,0:T(8,128)(2,1)S(1)} %concatenate.28), channel_id=1, source_target_pairs={{0,6},{2,4},{4,2},{6,0},{1,7},{3,5},{5,3},{7,1},{8,14},{10,12},{12... | collective-permute-start | bytes 344072 | tf_op jit(solution)/shard_map/ppermute | solution.py:427
  42.0 1.5 %conv2.1 = bf16[4,8,32,128]{3,2,1,0:T(8,128)(2,1)S(1)} custom-call(s32[3]{0:T(128)S(1)} %pad_add_fusion.place, bf16[10,64,128]{2,1,0:T(8,128)(2,1)S(1)} %pad_maximum_fusion.3.ur, bf16[10,64,128]{2,1,0:T(8,128)(2,1)S(1)} %collective-permute-done.14.ua, bf16[10,64,128]{2,1,0:T(8,128)(2,1)S(1)} %collective-permute-done.15.ub, ...), custom_call_target="tpu_custom_call" | custom-call | flops 1073741824 | bytes 1048576 | tf_op jit(solution)/shard_map/conv2/pallas_call | solution.py:61
  43.5 0.0 copy-start.5
  43.6 2.0 %collective-permute-start.20 = (bf16[256,128]{1,0:T(8,128)(2,1)S(1)}, bf16[256,128]{1,0:T(8,128)(2,1)S(1)}, u32[]{:S(2)}, u32[]{:S(2)}) collective-permute-start(bf16[256,128]{1,0:T(8,128)(2,1)S(1)} %bitcast.70), channel_id=1, source_target_pairs={{0,2},{2,0},{4,6},{6,4},{1,3},{3,1},{5,7},{7,5},{8,10},{10,8},{12,... | collective-permute-start | bytes 196616 | tf_op jit(solution)/shard_map/ppermute | solution.py:427
  45.6 0.0 collective-permute-done.17
  45.6 2.2 %collective-permute-done.18 = bf16[7,64,128]{2,1,0:T(8,128)(2,1)S(1)} collective-permute-done((bf16[7,64,128]{2,1,0:T(8,128)(2,1)S(1)}, bf16[7,64,128]{2,1,0:T(8,128)(2,1)S(1)}, u32[]{:S(2)}, u32[]{:S(2)}) %collective-permute-start.18) | collective-permute-done | bytes 114720 | tf_op jit(solution)/shard_map/ppermute | solution.py:427
  47.9 0.3 collective-permute-done.19
  48.3 0.1 fusion.4
  48.3 2.0 %collective-permute-start.21 = (bf16[7,64,128]{2,1,0:T(8,128)(2,1)S(1)}, bf16[7,64,128]{2,1,0:T(8,128)(2,1)S(1)}, u32[]{:S(2)}, u32[]{:S(2)}) collective-permute-start(bf16[7,64,128]{2,1,0:T(8,128)(2,1)S(1)} %fusion.4), channel_id=1, source_target_pairs={{0,8},{8,0},{16,24},{24,16},{1,9},{9,1},{17,25},{25,17},{2,10},{10... | collective-permute-start | bytes 344072 | tf_op jit(solution)/shard_map/ppermute | solution.py:427
  50.3 2.5 %collective-permute-start.23 = (bf16[7,64,128]{2,1,0:T(8,128)(2,1)S(1)}, bf16[7,64,128]{2,1,0:T(8,128)(2,1)S(1)}, u32[]{:S(2)}, u32[]{:S(2)}) collective-permute-start(bf16[7,64,128]{2,1,0:T(8,128)(2,1)S(1)} %fusion.4), channel_id=1, source_target_pairs={{0,24},{8,16},{16,8},{24,0},{1,25},{9,17},{17,9},{25,1},{2,26},{10... | collective-permute-start | bytes 344072 | tf_op jit(solution)/shard_map/ppermute | solution.py:427
  52.8 1.5 %collective-permute-start.24 = (bf16[256,128]{1,0:T(8,128)(2,1)S(1)}, bf16[256,128]{1,0:T(8,128)(2,1)S(1)}, u32[]{:S(2)}, u32[]{:S(2)}) collective-permute-start(bf16[256,128]{1,0:T(8,128)(2,1)S(1)} %get-tuple-element.130), channel_id=1, source_target_pairs={{0,4},{2,6},{4,0},{6,2},{1,5},{3,7},{5,1},{7,3},{8,12},{10,14},{12... | collective-permute-start | bytes 196616 | tf_op jit(solution)/shard_map/ppermute | solution.py:427
  54.3 1.7 %collective-permute-start.25 = (bf16[256,128]{1,0:T(8,128)(2,1)S(1)}, bf16[256,128]{1,0:T(8,128)(2,1)S(1)}, u32[]{:S(2)}, u32[]{:S(2)}) collective-permute-start(bf16[256,128]{1,0:T(8,128)(2,1)S(1)} %get-tuple-element.129), channel_id=1, source_target_pairs={{0,6},{2,4},{4,2},{6,0},{1,7},{3,5},{5,3},{7,1},{8,14},{10,12},{12... | collective-permute-start | bytes 196616 | tf_op jit(solution)/shard_map/ppermute | solution.py:427
  56.0 1.4 %collective-permute-done.24.refs_2_ = bf16[256,128]{1,0:T(8,128)(2,1)S(1)} collective-permute-done((bf16[256,128]{1,0:T(8,128)(2,1)S(1)}, bf16[256,128]{1,0:T(8,128)(2,1)S(1)}, u32[]{:S(2)}, u32[]{:S(2)}) %collective-permute-start.24) | collective-permute-done | bytes 65568 | tf_op jit(solution)/shard_map/ppermute | solution.py:427
  57.4 2.0 %collective-permute-done.25.refs_3_ = bf16[256,128]{1,0:T(8,128)(2,1)S(1)} collective-permute-done((bf16[256,128]{1,0:T(8,128)(2,1)S(1)}, bf16[256,128]{1,0:T(8,128)(2,1)S(1)}, u32[]{:S(2)}, u32[]{:S(2)}) %collective-permute-start.25) | collective-permute-done | bytes 65568 | tf_op jit(solution)/shard_map/ppermute | solution.py:427
  59.5 0.1 broadcast_in_dim.25.refs_4_
  59.6 1.1 %unpack.1 = f32[32,32,128]{2,1,0:T(8,128)} custom-call(s32[1]{0:T(128)} %bitcast.3.me, bf16[256,128]{1,0:T(8,128)(2,1)S(1)} %get-tuple-element.131.refs_0_, bf16[256,128]{1,0:T(8,128)(2,1)S(1)} %collective-permute-done.20.refs_1_, bf16[256,128]{1,0:T(8,128)(2,1)S(1)} %collective-permute-done.24.refs_2_, ...), custom_call_target="tpu_custom_call" | custom-call | flops 268435456 | bytes 1048576 | tf_op jit(solution)/shard_map/unpack/pallas_call | solution.py:61
  60.7 0.1 collective-permute-done.22
  60.8 0.1 add_multiply_fusion.mine
  60.9 0.1 collective-permute-start.26
  61.0 1.5 %collective-permute-done.26.other = f32[7,64,128]{2,1,0:T(8,128)S(1)} collective-permute-done((f32[7,64,128]{2,1,0:T(8,128)S(1)}, f32[7,64,128]{2,1,0:T(8,128)S(1)}, u32[]{:S(2)}, u32[]{:S(2)}) %collective-permute-start.26) | collective-permute-done | bytes 229408 | tf_op jit(solution)/shard_map/ppermute | solution.py:409
  62.4 1.7 %finish.1 = (f32[27,32,64]{2,1,0:T(8,128)}, f32[1,32]{1,0:T(1,128)}, f32[27,32,64]{2,1,0:T(8,128)}, f32[1,64]{1,0:T(1,128)}) custom-call(s32[3]{0:T(128)S(1)} %pad_add_fusion.place, f32[7,64,128]{2,1,0:T(8,128)S(1)} %add_multiply_fusion.mine, f32[7,64,128]{2,1,0:T(8,128)S(1)} %collective-permute-done.26.other), custom_call_target="tpu_custom_call" | custom-call | flops 1048576 | bytes 1048576 | tf_op jit(solution)/shard_map/finish/pallas_call | solution.py:61
  (40 shorter events, 0.4 us)
Async XLA Ops:
  0.6 1.0 %copy-start = (bf16[1,32,2,16,256]{4,3,2,1,0:T(8,128)(2,1)S(1)}, bf16[1,32,2,16,256]{4,3,2,1,0:T(8,128)(2,1)}, u32[]{:S(2)}) copy-start(bf16[1,32,2,16,256]{4,3,2,1,0:T(8,128)(2,1)} %param.6) | copy-start | bytes 1572868
  1.7 4.0 %copy-start.1 = (bf16[1,32,1,32,128]{4,3,2,1,0:T(8,128)(2,1)S(1)}, bf16[1,32,1,32,128]{4,3,2,1,0:T(8,128)(2,1)}, u32[]{:S(2)}) copy-start(bf16[1,32,1,32,128]{4,3,2,1,0:T(8,128)(2,1)} %param.11) | copy-start | bytes 786436
  1.7 4.0 %copy-start.2 = (bf16[32,64,3,3,3]{1,0,4,3,2:T(8,128)(2,1)S(1)}, bf16[32,64,3,3,3]{1,0,4,3,2:T(8,128)(2,1)}, u32[]{:S(2)}) copy-start(bf16[32,64,3,3,3]{1,0,4,3,2:T(8,128)(2,1)} %param.9) | copy-start | bytes 331780
  2.7 8.6 %collective-permute-start = (bf16[2,1,32,256]{3,2,1,0:T(8,128)(2,1)S(1)}, bf16[2,1,32,256]{3,2,1,0:T(8,128)(2,1)S(1)}, u32[]{:S(2)}, u32[]{:S(2)}) collective-permute-start(bf16[2,1,32,256]{3,2,1,0:T(8,128)(2,1)S(1)} %get-tuple-element.120), channel_id=1, source_target_pairs={{0,2},{2,0},{4,6},{6,4},{1,3},{3,1},{5,7},{7,5},{8,10},{10,8},{12,... | collective-permute-start | bytes 98312 | tf_op jit(solution)/shard_map/ppermute | solution.py:409
  5.7 5.6 %collective-permute-start.1 = (bf16[2,1,32,256]{3,2,1,0:T(8,128)(2,1)S(1)}, bf16[2,1,32,256]{3,2,1,0:T(8,128)(2,1)S(1)}, u32[]{:S(2)}, u32[]{:S(2)}) collective-permute-start(bf16[2,1,32,256]{3,2,1,0:T(8,128)(2,1)S(1)} %get-tuple-element.119), channel_id=1, source_target_pairs={{0,1},{1,0},{2,4},{3,5},{4,2},{5,3},{6,7},{7,6},{8,9},{9,8},{10,12... | collective-permute-start | bytes 98312 | tf_op jit(solution)/shard_map/ppermute | solution.py:422
  5.7 5.2 %copy-start.3 = (bf16[64,32,3,3,3]{0,1,4,3,2:T(8,128)(2,1)S(1)}, bf16[64,32,3,3,3]{0,1,4,3,2:T(8,128)(2,1)}, u32[]{:S(2)}) copy-start(bf16[64,32,3,3,3]{0,1,4,3,2:T(8,128)(2,1)} %param.7) | copy-start | bytes 331780
  5.7 5.4 %copy-start.4 = (f32[64]{0:T(128)S(1)}, f32[64]{0:T(128)}, u32[]{:S(2)}) copy-start(f32[64]{0:T(128)} %param.8) | copy-start | bytes 772
  6.3 8.6 %collective-permute-start.4 = (bf16[10,32,128]{2,1,0:T(8,128)(2,1)S(1)}, bf16[10,32,128]{2,1,0:T(8,128)(2,1)S(1)}, u32[]{:S(2)}, u32[]{:S(2)}) collective-permute-start(bf16[10,32,128]{2,1,0:T(8,128)(2,1)S(1)} %get-tuple-element.123), channel_id=1, source_target_pairs={{0,2},{2,0},{4,6},{6,4},{1,3},{3,1},{5,7},{7,5},{8,10},{10,8},{12,... | collective-permute-start | bytes 245768 | tf_op jit(solution)/shard_map/ppermute | solution.py:427
  9.3 7.5 %collective-permute-start.5 = (bf16[10,32,128]{2,1,0:T(8,128)(2,1)S(1)}, bf16[10,32,128]{2,1,0:T(8,128)(2,1)S(1)}, u32[]{:S(2)}, u32[]{:S(2)}) collective-permute-start(bf16[10,32,128]{2,1,0:T(8,128)(2,1)S(1)} %get-tuple-element.122), channel_id=1, source_target_pairs={{0,4},{2,6},{4,0},{6,2},{1,5},{3,7},{5,1},{7,3},{8,12},{10,14},{12... | collective-permute-start | bytes 245768 | tf_op jit(solution)/shard_map/ppermute | solution.py:427
  9.3 7.5 %collective-permute-start.6 = (bf16[10,32,128]{2,1,0:T(8,128)(2,1)S(1)}, bf16[10,32,128]{2,1,0:T(8,128)(2,1)S(1)}, u32[]{:S(2)}, u32[]{:S(2)}) collective-permute-start(bf16[10,32,128]{2,1,0:T(8,128)(2,1)S(1)} %get-tuple-element.121), channel_id=1, source_target_pairs={{0,6},{2,4},{4,2},{6,0},{1,7},{3,5},{5,3},{7,1},{8,14},{10,12},{12... | collective-permute-start | bytes 245768 | tf_op jit(solution)/shard_map/ppermute | solution.py:427
  11.4 7.7 %collective-permute-start.2 = (bf16[18,32,256]{2,1,0:T(8,128)(2,1)S(1)}, bf16[18,32,256]{2,1,0:T(8,128)(2,1)S(1)}, u32[]{:S(2)}, u32[]{:S(2)}) collective-permute-start(bf16[18,32,256]{2,1,0:T(8,128)(2,1)S(1)} %get-tuple-element.118), channel_id=1, source_target_pairs={{0,8},{8,0},{16,24},{24,16},{1,9},{9,1},{17,25},{25,17},{2,10},{10... | collective-permute-start | bytes 884744 | tf_op jit(solution)/shard_map/ppermute | solution.py:409
  13.1 8.6 %collective-permute-start.3 = (bf16[18,32,256]{2,1,0:T(8,128)(2,1)S(1)}, bf16[18,32,256]{2,1,0:T(8,128)(2,1)S(1)}, u32[]{:S(2)}, u32[]{:S(2)}) collective-permute-start(bf16[18,32,256]{2,1,0:T(8,128)(2,1)S(1)} %get-tuple-element.117), channel_id=1, source_target_pairs={{0,1},{1,0},{8,16},{9,17},{16,8},{17,9},{24,25},{25,24},{2,3},{3,2... | collective-permute-start | bytes 884744 | tf_op jit(solution)/shard_map/ppermute | solution.py:422
  14.8 8.5 %collective-permute-start.7 = (bf16[14,32,128]{2,1,0:T(8,128)(2,1)S(1)}, bf16[14,32,128]{2,1,0:T(8,128)(2,1)S(1)}, u32[]{:S(2)}, u32[]{:S(2)}) collective-permute-start(bf16[14,32,128]{2,1,0:T(8,128)(2,1)S(1)} %get-tuple-element.72), channel_id=1, source_target_pairs={{0,2},{2,0},{4,6},{6,4},{1,3},{3,1},{5,7},{7,5},{8,10},{10,8},{12,... | collective-permute-start | bytes 344072 | tf_op jit(solution)/shard_map/ppermute | solution.py:427
  16.8 7.7 %collective-permute-start.8 = (bf16[14,32,128]{2,1,0:T(8,128)(2,1)S(1)}, bf16[14,32,128]{2,1,0:T(8,128)(2,1)S(1)}, u32[]{:S(2)}, u32[]{:S(2)}) collective-permute-start(bf16[14,32,128]{2,1,0:T(8,128)(2,1)S(1)} %get-tuple-element.72), channel_id=1, source_target_pairs={{0,4},{2,6},{4,0},{6,2},{1,5},{3,7},{5,1},{7,3},{8,12},{10,14},{12... | collective-permute-start | bytes 344072 | tf_op jit(solution)/shard_map/ppermute | solution.py:427
  16.9 7.7 %collective-permute-start.9 = (bf16[14,32,128]{2,1,0:T(8,128)(2,1)S(1)}, bf16[14,32,128]{2,1,0:T(8,128)(2,1)S(1)}, u32[]{:S(2)}, u32[]{:S(2)}) collective-permute-start(bf16[14,32,128]{2,1,0:T(8,128)(2,1)S(1)} %get-tuple-element.72), channel_id=1, source_target_pairs={{0,6},{2,4},{4,2},{6,0},{1,7},{3,5},{5,3},{7,1},{8,14},{10,12},{12... | collective-permute-start | bytes 344072 | tf_op jit(solution)/shard_map/ppermute | solution.py:427
  19.1 10.7 %collective-permute-start.10 = (bf16[4,10,32,128]{3,2,1,0:T(8,128)(2,1)S(1)}, bf16[4,10,32,128]{3,2,1,0:T(8,128)(2,1)S(1)}, u32[]{:S(2)}, u32[]{:S(2)}) collective-permute-start(bf16[4,10,32,128]{3,2,1,0:T(8,128)(2,1)S(1)} %pad_maximum_fusion.2.co), channel_id=1, source_target_pairs={{0,8},{8,0},{16,24},{24,16},{1,9},{9,1},{17,25},{25,17},{2,10},{10... | collective-permute-start | bytes 983048 | tf_op jit(solution)/shard_map/ppermute | solution.py:409
  21.7 8.2 %collective-permute-start.11 = (bf16[4,10,32,128]{3,2,1,0:T(8,128)(2,1)S(1)}, bf16[4,10,32,128]{3,2,1,0:T(8,128)(2,1)S(1)}, u32[]{:S(2)}, u32[]{:S(2)}) collective-permute-start(bf16[4,10,32,128]{3,2,1,0:T(8,128)(2,1)S(1)} %pad_maximum_fusion.2.co), channel_id=1, source_target_pairs={{0,1},{1,0},{8,16},{9,17},{16,8},{17,9},{24,25},{25,24},{2,3},{3,2... | collective-permute-start | bytes 983048 | tf_op jit(solution)/shard_map/ppermute | solution.py:422
  24.6 3.7 %collective-permute-start.12 = (bf16[64,128]{1,0:T(8,128)(2,1)S(1)}, bf16[64,128]{1,0:T(8,128)(2,1)S(1)}, u32[]{:S(2)}, u32[]{:S(2)}) collective-permute-start(bf16[64,128]{1,0:T(8,128)(2,1)S(1)} %get-tuple-element.133), channel_id=1, source_target_pairs={{0,2},{2,0},{4,6},{6,4},{1,3},{3,1},{5,7},{7,5},{8,10},{10,8},{12,... | collective-permute-start | bytes 49160 | tf_op jit(solution)/shard_map/ppermute | solution.py:409
  25.4 3.0 %collective-permute-start.13 = (bf16[64,128]{1,0:T(8,128)(2,1)S(1)}, bf16[64,128]{1,0:T(8,128)(2,1)S(1)}, u32[]{:S(2)}, u32[]{:S(2)}) collective-permute-start(bf16[64,128]{1,0:T(8,128)(2,1)S(1)} %get-tuple-element.132), channel_id=1, source_target_pairs={{0,1},{1,0},{2,4},{3,5},{4,2},{5,3},{6,7},{7,6},{8,9},{9,8},{10,12... | collective-permute-start | bytes 49160 | tf_op jit(solution)/shard_map/ppermute | solution.py:422
  28.4 6.7 %collective-permute-start.14 = (bf16[10,64,128]{2,1,0:T(8,128)(2,1)S(1)}, bf16[10,64,128]{2,1,0:T(8,128)(2,1)S(1)}, u32[]{:S(2)}, u32[]{:S(2)}) collective-permute-start(bf16[10,64,128]{2,1,0:T(8,128)(2,1)S(1)} %pad_maximum_fusion.3.ur), channel_id=1, source_target_pairs={{0,8},{8,0},{16,24},{24,16},{1,9},{9,1},{17,25},{25,17},{2,10},{10... | collective-permute-start | bytes 491528 | tf_op jit(solution)/shard_map/ppermute | solution.py:409
  29.9 5.2 %collective-permute-start.15 = (bf16[10,64,128]{2,1,0:T(8,128)(2,1)S(1)}, bf16[10,64,128]{2,1,0:T(8,128)(2,1)S(1)}, u32[]{:S(2)}, u32[]{:S(2)}) collective-permute-start(bf16[10,64,128]{2,1,0:T(8,128)(2,1)S(1)} %pad_maximum_fusion.3.ur), channel_id=1, source_target_pairs={{0,1},{1,0},{8,16},{9,17},{16,8},{17,9},{24,25},{25,24},{2,3},{3,2... | collective-permute-start | bytes 491528 | tf_op jit(solution)/shard_map/ppermute | solution.py:422
  35.1 2.2 %collective-permute-start.16 = (f32[7,160,128]{2,1,0:T(8,128)S(1)}, f32[7,160,128]{2,1,0:T(8,128)S(1)}, u32[]{:S(2)}, u32[]{:S(2)}) collective-permute-start(f32[7,160,128]{2,1,0:T(8,128)S(1)} %get-tuple-element.86), channel_id=1, source_target_pairs={{0,1},{1,0},{2,3},{3,2},{4,5},{5,4},{6,7},{7,6},{8,9},{9,8},{10,11... | collective-permute-start | bytes 1720328 | tf_op jit(solution)/shard_map/ppermute | solution.py:409
  37.5 8.1 %collective-permute-start.17 = (bf16[7,64,128]{2,1,0:T(8,128)(2,1)S(1)}, bf16[7,64,128]{2,1,0:T(8,128)(2,1)S(1)}, u32[]{:S(2)}, u32[]{:S(2)}) collective-permute-start(bf16[7,64,128]{2,1,0:T(8,128)(2,1)S(1)} %get-tuple-element.137), channel_id=1, source_target_pairs={{0,2},{2,0},{4,6},{6,4},{1,3},{3,1},{5,7},{7,5},{8,10},{10,8},{12,... | collective-permute-start | bytes 344072 | tf_op jit(solution)/shard_map/ppermute | solution.py:427
  40.5 7.4 %collective-permute-start.18 = (bf16[7,64,128]{2,1,0:T(8,128)(2,1)S(1)}, bf16[7,64,128]{2,1,0:T(8,128)(2,1)S(1)}, u32[]{:S(2)}, u32[]{:S(2)}) collective-permute-start(bf16[7,64,128]{2,1,0:T(8,128)(2,1)S(1)} %get-tuple-element.136), channel_id=1, source_target_pairs={{0,4},{2,6},{4,0},{6,2},{1,5},{3,7},{5,1},{7,3},{8,12},{10,14},{12... | collective-permute-start | bytes 344072 | tf_op jit(solution)/shard_map/ppermute | solution.py:427
  40.5 7.7 %collective-permute-start.19 = (bf16[7,64,128]{2,1,0:T(8,128)(2,1)S(1)}, bf16[7,64,128]{2,1,0:T(8,128)(2,1)S(1)}, u32[]{:S(2)}, u32[]{:S(2)}) collective-permute-start(bf16[7,64,128]{2,1,0:T(8,128)(2,1)S(1)} %concatenate.28), channel_id=1, source_target_pairs={{0,6},{2,4},{4,2},{6,0},{1,7},{3,5},{5,3},{7,1},{8,14},{10,12},{12... | collective-permute-start | bytes 344072 | tf_op jit(solution)/shard_map/ppermute | solution.py:427
  43.5 15.9 %copy-start.5 = (f32[32]{0:T(128)S(1)}, f32[32]{0:T(128)}, u32[]{:S(2)}) copy-start(f32[32]{0:T(128)} %param.10) | copy-start | bytes 388
  43.6 4.7 %collective-permute-start.20 = (bf16[256,128]{1,0:T(8,128)(2,1)S(1)}, bf16[256,128]{1,0:T(8,128)(2,1)S(1)}, u32[]{:S(2)}, u32[]{:S(2)}) collective-permute-start(bf16[256,128]{1,0:T(8,128)(2,1)S(1)} %bitcast.70), channel_id=1, source_target_pairs={{0,2},{2,0},{4,6},{6,4},{1,3},{3,1},{5,7},{7,5},{8,10},{10,8},{12,... | collective-permute-start | bytes 196616 | tf_op jit(solution)/shard_map/ppermute | solution.py:427
  48.3 12.4 %collective-permute-start.21 = (bf16[7,64,128]{2,1,0:T(8,128)(2,1)S(1)}, bf16[7,64,128]{2,1,0:T(8,128)(2,1)S(1)}, u32[]{:S(2)}, u32[]{:S(2)}) collective-permute-start(bf16[7,64,128]{2,1,0:T(8,128)(2,1)S(1)} %fusion.4), channel_id=1, source_target_pairs={{0,8},{8,0},{16,24},{24,16},{1,9},{9,1},{17,25},{25,17},{2,10},{10... | collective-permute-start | bytes 344072 | tf_op jit(solution)/shard_map/ppermute | solution.py:427
  50.3 10.5 %collective-permute-start.22 = (bf16[7,64,128]{2,1,0:T(8,128)(2,1)S(1)}, bf16[7,64,128]{2,1,0:T(8,128)(2,1)S(1)}, u32[]{:S(2)}, u32[]{:S(2)}) collective-permute-start(bf16[7,64,128]{2,1,0:T(8,128)(2,1)S(1)} %fusion.4), channel_id=1, source_target_pairs={{0,16},{8,24},{16,0},{24,8},{1,17},{9,25},{17,1},{25,9},{2,18},{10... | collective-permute-start | bytes 344072 | tf_op jit(solution)/shard_map/ppermute | solution.py:427
  50.3 10.5 %collective-permute-start.23 = (bf16[7,64,128]{2,1,0:T(8,128)(2,1)S(1)}, bf16[7,64,128]{2,1,0:T(8,128)(2,1)S(1)}, u32[]{:S(2)}, u32[]{:S(2)}) collective-permute-start(bf16[7,64,128]{2,1,0:T(8,128)(2,1)S(1)} %fusion.4), channel_id=1, source_target_pairs={{0,24},{8,16},{16,8},{24,0},{1,25},{9,17},{17,9},{25,1},{2,26},{10... | collective-permute-start | bytes 344072 | tf_op jit(solution)/shard_map/ppermute | solution.py:427
  52.8 4.6 %collective-permute-start.24 = (bf16[256,128]{1,0:T(8,128)(2,1)S(1)}, bf16[256,128]{1,0:T(8,128)(2,1)S(1)}, u32[]{:S(2)}, u32[]{:S(2)}) collective-permute-start(bf16[256,128]{1,0:T(8,128)(2,1)S(1)} %get-tuple-element.130), channel_id=1, source_target_pairs={{0,4},{2,6},{4,0},{6,2},{1,5},{3,7},{5,1},{7,3},{8,12},{10,14},{12... | collective-permute-start | bytes 196616 | tf_op jit(solution)/shard_map/ppermute | solution.py:427
  54.3 5.2 %collective-permute-start.25 = (bf16[256,128]{1,0:T(8,128)(2,1)S(1)}, bf16[256,128]{1,0:T(8,128)(2,1)S(1)}, u32[]{:S(2)}, u32[]{:S(2)}) collective-permute-start(bf16[256,128]{1,0:T(8,128)(2,1)S(1)} %get-tuple-element.129), channel_id=1, source_target_pairs={{0,6},{2,4},{4,2},{6,0},{1,7},{3,5},{5,3},{7,1},{8,14},{10,12},{12... | collective-permute-start | bytes 196616 | tf_op jit(solution)/shard_map/ppermute | solution.py:427
  60.9 1.6 %collective-permute-start.26 = (f32[7,64,128]{2,1,0:T(8,128)S(1)}, f32[7,64,128]{2,1,0:T(8,128)S(1)}, u32[]{:S(2)}, u32[]{:S(2)}) collective-permute-start(f32[7,64,128]{2,1,0:T(8,128)S(1)} %add_multiply_fusion.mine), channel_id=1, source_target_pairs={{0,1},{1,0},{2,3},{3,2},{4,5},{5,4},{6,7},{7,6},{8,9},{9,8},{10,11... | collective-permute-start | bytes 688136 | tf_op jit(solution)/shard_map/ppermute | solution.py:409

commit v5 on v4

--- a/solution.py
+++ b/solution.py
@@ -369,7 +369,7 @@
         red[9 + m, c2:] = jnp.where(low_half, lows[2 * m], highs[2 * m + 1])
     hp = pairs // 2
     keep[...] = red[pl.ds(place[1] * hp, hp)]
-    send[...] = red[pl.ds((1 - place[1]) * hp, hp)]
+    send[...] = red[pl.ds((1 - place[1]) * hp, hp)].astype(BF)
 
 
 def unpack_body(me, *refs):
@@ -477,6 +477,7 @@
         (source,),
         flops=1 << 30,
     )
+    cotan, _ = lax.optimization_barrier((cotan, vt))
     cp, w2p = call(
         prep_body,
         "cotangent_cells",
@@ -502,9 +503,13 @@
     za = swap_first(jnp.where(odd_x == 1, vr[0], vr[planes - 1]), "sx")
     zb = swap_second(jnp.where(odd_x == 1, vr[planes - 1], vr[0]), "sx")
 
-    cgot = [cp[0]] + [to_partner(cp[s], "sy", s) for s in range(1, n_sy)]
-    w2p, vr = lax.optimization_barrier((w2p, vr))
-    wgot = [w2p] + [to_partner(w2p, "sy", s) for s in range(1, n_sy)]
+    w2_half = lax.dynamic_slice_in_dim(w2p, rep * (pairs // 2), pairs // 2, axis=0)
+    both = [
+        to_partner(jnp.concatenate([cp[s], w2_half], axis=0), "sy", s) for s in range(1, n_sy)
+    ]
+    cgot = [cp[0]] + [b[: own2 + 2] for b in both]
+    w2_mine = jnp.stack([b[own2 + 2 :] for b in both])
+    w2_other = swap_first(w2_mine, "rep")
 
     pooled_rows = own2
     cell_shape = (rows + 2 * rim, 4 * cin, width // 2)
@@ -538,8 +543,12 @@
         smem_ins=1,
         flops=1 << 30,
     )
-    wgot, _ = lax.optimization_barrier((wgot, pooled))
-    w2r = jnp.stack(wgot)
+    w2_other, _ = lax.optimization_barrier((w2_other, pooled))
+    w2_first = jnp.where(rep == 0, w2_mine, w2_other)
+    w2_second = jnp.where(rep == 0, w2_other, w2_mine)
+    w2r = jnp.concatenate(
+        [w2p[None], jnp.concatenate([w2_first, w2_second], axis=1)], axis=0
+    )
     pa = swap_first(jnp.where(odd_y == 1, pooled[0], pooled[own2 - 1]), "sy")
     pb = swap_second(jnp.where(odd_y == 1, pooled[own2 - 1], pooled[0]), "sy")
     pb = jnp.where((sy > 0) & (sy < n_sy - 1), pb, jnp.zeros_like(pb))
@@ -587,7 +596,7 @@
     keep, send = call(
         weights_body,
         "first_weights",
-        [half_shape, half_shape],
+        [half_shape, jax.ShapeDtypeStruct(half_shape.shape, BF)],
         [pltpu.VMEM((pairs, c2 + cin, 2 * c1), F32)],
         (place, cells, low, high, gp, back_g2, bias1, own_g2, own_b2),
         smem_ins=1,
@@ -595,7 +604,7 @@
     )
 
     send, ua, ub = lax.optimization_barrier((send, ua, ub))
-    half = keep + swap_first(send, "rep")
+    half = keep + swap_first(send, "rep").astype(F32)
     half, ua, ub = lax.optimization_barrier((half, ua, ub))
     half_bf = half.astype(BF)
     tail = half_bf[:, c2:]

time: 64.3 us -> 63.1 us (0.981)
  starting transfers between devices: 32.7 us -> 30.9 us
    ppermute x15 -> x12, starting transfers between devices: 22.3 us -> 18.4 us  [to_partner(): return lax.ppermute(value, axis, [(i, i ^ s) for i in range(count)])]
    ppermute x7 -> x8, starting transfers between devices: 10.1 us -> 12.4 us  [swap_first(): return lax.ppermute(value, axis, [(i, i ^ 1) for i in range(count)])]
    ppermute x15 -> x12, waiting for transfers between devices: 7.45 us -> 8.68 us  [to_partner(): return lax.ppermute(value, axis, [(i, i ^ s) for i in range(count)])]
    ppermute x7 -> x8, waiting for transfers between devices: 5.14 us -> 4.3 us  [swap_first(): return lax.ppermute(value, axis, [(i, i ^ 1) for i in range(count)])]
  transfers between devices with their start and end apart: 27 -> 25, of which waited for: 10 -> 9; matrix products, arithmetic and copies ran while one was open for 1% -> 2% of each run, Pallas kernels for 20% -> 21%
where the time goes in v5:
time: 63.1 us; the launch traced here: 62.9 us
  starting transfers between devices  30.9 us (49%)
  Pallas kernels  15.6 us (25%)
  waiting for transfers between devices  13 us (21%)
  local copies, waits for them, and re-layouts  1.4 us (2%)
  between operations  1.08 us (2%)
  other arithmetic  0.95 us (2%)
    ppermute x12, starting transfers between devices, to_partner(): return lax.ppermute(value, axis, [(i, i ^ s) for i in range(count)])  18.4 us
    pallas_call x10, Pallas kernels, call(): pl.pallas_call(body, name=name, out_shape=outs, in_specs=[sm] * smem_ins...  15.6 us
    ppermute x8, starting transfers between devices, swap_first(): return lax.ppermute(value, axis, [(i, i ^ 1) for i in range(count)])  12.4 us
    ppermute x12, waiting for transfers between devices, to_partner(): return lax.ppermute(value, axis, [(i, i ^ s) for i in range(count)])  8.68 us
    ppermute x8, waiting for transfers between devices, swap_first(): return lax.ppermute(value, axis, [(i, i ^ 1) for i in range(count)])  4.3 us
  transfers between devices with their start and end apart: 25, of which 9 were waited for; matrix products, arithmetic and copies ran while one was open for 2% of the time, Pallas kernels for 21%

profile of v5, /device:TPU:0, one launch (start us, length us, event | category | flops | bytes accessed | tf_op | source)
XLA Modules:
  0.0 62.9 jit_solution(16095526756575761695)
XLA Ops:
  0.7 1.0 %copy-done = bf16[1,32,2,16,256]{4,3,2,1,0:T(8,128)(2,1)S(1)} copy-done((bf16[1,32,2,16,256]{4,3,2,1,0:T(8,128)(2,1)S(1)}, bf16[1,32,2,16,256]{4,3,2,1,0:T(8,128)(2,1)}, u32[]{:S(2)}) %copy-start) | copy-done | bytes 524312
  1.7 0.9 %volume_cells.1 = bf16[2,16,32,256]{3,2,1,0:T(8,128)(2,1)S(1)} custom-call(bf16[32,2,16,256]{3,2,1,0:T(8,128)(2,1)S(1)} %bitcast.62), custom_call_target="tpu_custom_call" | custom-call | flops 1073741824 | bytes 1048576 | tf_op jit(solution)/shard_map/volume_cells/pallas_call | solution.py:61
  2.7 3.0 %collective-permute-start = (bf16[2,1,32,256]{3,2,1,0:T(8,128)(2,1)S(1)}, bf16[2,1,32,256]{3,2,1,0:T(8,128)(2,1)S(1)}, u32[]{:S(2)}, u32[]{:S(2)}) collective-permute-start(bf16[2,1,32,256]{3,2,1,0:T(8,128)(2,1)S(1)} %get-tuple-element.112), channel_id=1, source_target_pairs={{0,2},{2,0},{4,6},{6,4},{1,3},{3,1},{5,7},{7,5},{8,10},{10,8},{12,... | collective-permute-start | bytes 98312 | tf_op jit(solution)/shard_map/ppermute | solution.py:409
  5.7 0.0 copy-start.3
  5.7 0.0 copy-start.4
  5.7 0.5 cotangent_cells.1
  6.3 3.0 %collective-permute-start.4 = (bf16[17,32,128]{2,1,0:T(8,128)(2,1)S(1)}, bf16[17,32,128]{2,1,0:T(8,128)(2,1)S(1)}, u32[]{:S(2)}, u32[]{:S(2)}) collective-permute-start(bf16[17,32,128]{2,1,0:T(8,128)(2,1)S(1)} %get-tuple-element.134), channel_id=1, source_target_pairs={{0,2},{2,0},{4,6},{6,4},{1,3},{3,1},{5,7},{7,5},{8,10},{10,8},{12,... | collective-permute-start | bytes 417800 | tf_op jit(solution)/shard_map/ppermute | solution.py:427
  9.4 1.5 %collective-permute-start.6 = (bf16[17,32,128]{2,1,0:T(8,128)(2,1)S(1)}, bf16[17,32,128]{2,1,0:T(8,128)(2,1)S(1)}, u32[]{:S(2)}, u32[]{:S(2)}) collective-permute-start(bf16[17,32,128]{2,1,0:T(8,128)(2,1)S(1)} %get-tuple-element.132), channel_id=1, source_target_pairs={{0,6},{2,4},{4,2},{6,0},{1,7},{3,5},{5,3},{7,1},{8,14},{10,12},{12... | collective-permute-start | bytes 417800 | tf_op jit(solution)/shard_map/ppermute | solution.py:427
  10.9 0.2 fusion.2.w1q
  11.1 0.1 pad_add_fusion.place
  11.2 0.1 broadcast_in_dim_tile.4.bias
  11.3 0.0 collective-permute-done.1
  11.4 0.1 pad_maximum_fusion.vr
  11.5 1.6 %collective-permute-start.2 = (bf16[18,32,256]{2,1,0:T(8,128)(2,1)S(1)}, bf16[18,32,256]{2,1,0:T(8,128)(2,1)S(1)}, u32[]{:S(2)}, u32[]{:S(2)}) collective-permute-start(bf16[18,32,256]{2,1,0:T(8,128)(2,1)S(1)} %get-tuple-element.110), channel_id=1, source_target_pairs={{0,8},{8,0},{16,24},{24,16},{1,9},{9,1},{17,25},{25,17},{2,10},{10... | collective-permute-start | bytes 884744 | tf_op jit(solution)/shard_map/ppermute | solution.py:409
  13.1 0.0 collective-permute-start.3
  13.1 1.7 %conv1_own.1 = (bf16[2,18,128,128]{3,2,1,0:T(8,128)(2,1)S(1)}, bf16[3,256,512]{2,1,0:T(8,128)(2,1)S(1)}, f32[2,4,256,256]{3,2,1,0:T(8,128)S(1)}) custom-call(bf16[2,18,32,256]{3,2,1,0:T(8,128)(2,1)S(1)} %pad_maximum_fusion.vr, bf16[3,3,4,32,128]{4,3,2,1,0:T(8,128)(2,1)S(1)} %fusion.2.w1q, f32[256,1]{1,0:T(8,128)S(1)} %broadcast_in_dim_tile.4.bias), custom_call_target="tpu_custom_call" | custom-call | flops 2147483648 | bytes 1048576 | tf_op jit(solution)/shard_map/conv1_own/pallas_call | solution.py:61
  14.9 0.0 collective-permute-done.4
  14.9 2.0 %collective-permute-done.5 = bf16[17,32,128]{2,1,0:T(8,128)(2,1)S(1)} collective-permute-done((bf16[17,32,128]{2,1,0:T(8,128)(2,1)S(1)}, bf16[17,32,128]{2,1,0:T(8,128)(2,1)S(1)}, u32[]{:S(2)}, u32[]{:S(2)}) %collective-permute-start.5) | collective-permute-done | bytes 139296 | tf_op jit(solution)/shard_map/ppermute | solution.py:427
  17.0 1.6 %collective-permute-start.8 = (bf16[4,10,32,128]{3,2,1,0:T(8,128)(2,1)S(1)}, bf16[4,10,32,128]{3,2,1,0:T(8,128)(2,1)S(1)}, u32[]{:S(2)}, u32[]{:S(2)}) collective-permute-start(bf16[4,10,32,128]{3,2,1,0:T(8,128)(2,1)S(1)} %pad_maximum_fusion.1.co), channel_id=1, source_target_pairs={{0,8},{8,0},{16,24},{24,16},{1,9},{9,1},{17,25},{25,17},{2,10},{10... | collective-permute-start | bytes 983048 | tf_op jit(solution)/shard_map/ppermute | solution.py:409
  18.7 0.6 collective-permute-start.7
  19.3 0.9 %collective-permute-done.2.za = bf16[18,32,256]{2,1,0:T(8,128)(2,1)S(1)} collective-permute-done((bf16[18,32,256]{2,1,0:T(8,128)(2,1)S(1)}, bf16[18,32,256]{2,1,0:T(8,128)(2,1)S(1)}, u32[]{:S(2)}, u32[]{:S(2)}) %collective-permute-start.2) | collective-permute-done | bytes 294944 | tf_op jit(solution)/shard_map/ppermute | solution.py:409
  20.1 0.0 collective-permute-done.3.zb
  20.1 1.6 %conv1.1 = (bf16[18,128,128]{2,1,0:T(8,128)(2,1)S(1)}, bf16[18,128,128]{2,1,0:T(8,128)(2,1)S(1)}, bf16[2,8,256,128]{3,2,1,0:T(8,128)(2,1)S(1)}, bf16[8,64,128]{2,1,0:T(8,128)(2,1)S(1)}) custom-call(s32[3]{0:T(128)S(1)} %pad_add_fusion.place, bf16[18,32,256]{2,1,0:T(8,128)(2,1)S(1)} %collective-permute-done.2.za, ...), custom_call_target="tpu_custom_call" | custom-call | flops 1073741824 | bytes 1048576 | tf_op jit(solution)/shard_map/conv1/pallas_call | solution.py:61
  21.8 0.0 collective-permute-done.7
  21.8 1.6 %collective-permute-start.10 = (bf16[64,128]{1,0:T(8,128)(2,1)S(1)}, bf16[64,128]{1,0:T(8,128)(2,1)S(1)}, u32[]{:S(2)}, u32[]{:S(2)}) collective-permute-start(bf16[64,128]{1,0:T(8,128)(2,1)S(1)} %get-tuple-element.127), channel_id=1, source_target_pairs={{0,2},{2,0},{4,6},{6,4},{1,3},{3,1},{5,7},{7,5},{8,10},{10,8},{12,... | collective-permute-start | bytes 49160 | tf_op jit(solution)/shard_map/ppermute | solution.py:409
  23.4 0.0 collective-permute-start.11
  23.4 0.1 maximum_maximum_fusion.w2r
  23.5 1.3 %backward_own.1 = (bf16[3,192,384]{2,1,0:T(8,128)(2,1)S(1)}, bf16[256,1024]{1,0:T(8,128)(2,1)S(1)}, f32[4,192,256]{2,1,0:T(8,128)S(1)}, f32[384,256]{1,0:T(8,128)S(1)}, f32[128,128]{1,0:T(8,128)S(1)}) custom-call(bf16[4,10,32,128]{3,2,1,0:T(8,128)(2,1)S(1)} %pad_maximum_fusion.1.co, bf16[8,64,128]{2,1,0:T(8,128)(2,1)S(1)} %get-tuple-element.66.pooled, ...), custom_call_target="tpu_custom_call" | custom-call | flops 2147483648 | bytes 1048576 | tf_op jit(solution)/shard_map/backward_own/pallas_call | solution.py:61
  24.8 0.8 %collective-permute-done.10 = bf16[64,128]{1,0:T(8,128)(2,1)S(1)} collective-permute-done((bf16[64,128]{1,0:T(8,128)(2,1)S(1)}, bf16[64,128]{1,0:T(8,128)(2,1)S(1)}, u32[]{:S(2)}, u32[]{:S(2)}) %collective-permute-start.10) | collective-permute-done | bytes 16416 | tf_op jit(solution)/shard_map/ppermute | solution.py:409
  25.6 0.0 collective-permute-done.11
  25.6 3.3 %collective-permute-start.12 = (bf16[10,64,128]{2,1,0:T(8,128)(2,1)S(1)}, bf16[10,64,128]{2,1,0:T(8,128)(2,1)S(1)}, u32[]{:S(2)}, u32[]{:S(2)}) collective-permute-start(bf16[10,64,128]{2,1,0:T(8,128)(2,1)S(1)} %pad_maximum_fusion.6.ur), channel_id=1, source_target_pairs={{0,8},{8,0},{16,24},{24,16},{1,9},{9,1},{17,25},{25,17},{2,10},{10... | collective-permute-start | bytes 491528 | tf_op jit(solution)/shard_map/ppermute | solution.py:409
  29.0 2.6 %backward.1 = (bf16[2,4,256,256]{3,2,1,0:T(8,128)(2,1)S(1)}, f32[2,384,256]{2,1,0:T(8,128)S(1)}, f32[8,256]{1,0:T(8,128)S(1)}) custom-call(s32[3]{0:T(128)S(1)} %pad_add_fusion.place, bf16[2,8,256,128]{3,2,1,0:T(8,128)(2,1)S(1)} %get-tuple-element.61.mask, bf16[256,1024]{1,0:T(8,128)(2,1)S(1)} %get-tuple-element.68.wide, ...), custom_call_target="tpu_custom_call" | custom-call | flops 2147483648 | bytes 1048576 | tf_op jit(solution)/shard_map/backward/pallas_call | solution.py:61
  31.6 2.6 %first_weights.1 = (f32[7,160,128]{2,1,0:T(8,128)S(1)}, bf16[7,160,128]{2,1,0:T(8,128)(2,1)S(1)}) custom-call(s32[3]{0:T(128)S(1)} %pad_add_fusion.place, bf16[2,18,128,128]{3,2,1,0:T(8,128)(2,1)S(1)} %get-tuple-element.52.cells, bf16[18,128,128]{2,1,0:T(8,128)(2,1)S(1)} %get-tuple-element.59.low, bf16[18,128,128]{2,1,0:T(8,128)(2,1)S(1)} %get-tuple-element.60.high, ...), custom_call_target="tpu_custom_call" | custom-call | flops 3221225472 | bytes 1048576 | tf_op jit(solution)/shard_map/first_weights/pallas_call | solution.py:61
  34.2 0.0 collective-permute-done.12.ua
  34.2 0.0 collective-permute-done.13.ub
  34.2 0.6 collective-permute-start.14
  34.7 1.2 %collective-permute-done.14 = bf16[7,160,128]{2,1,0:T(8,128)(2,1)S(1)} collective-permute-done((bf16[7,160,128]{2,1,0:T(8,128)(2,1)S(1)}, bf16[7,160,128]{2,1,0:T(8,128)(2,1)S(1)}, u32[]{:S(2)}, u32[]{:S(2)}) %collective-permute-start.14) | collective-permute-done | bytes 286752 | tf_op jit(solution)/shard_map/ppermute | solution.py:409
  35.9 0.1 convert_add_fusion
  36.1 3.0 %collective-permute-start.15 = (bf16[7,64,128]{2,1,0:T(8,128)(2,1)S(1)}, bf16[7,64,128]{2,1,0:T(8,128)(2,1)S(1)}, u32[]{:S(2)}, u32[]{:S(2)}) collective-permute-start(bf16[7,64,128]{2,1,0:T(8,128)(2,1)S(1)} %get-tuple-element.131), channel_id=1, source_target_pairs={{0,2},{2,0},{4,6},{6,4},{1,3},{3,1},{5,7},{7,5},{8,10},{10,8},{12,... | collective-permute-start | bytes 344072 | tf_op jit(solution)/shard_map/ppermute | solution.py:427
  39.1 0.2 collective-permute-start.16
  39.3 1.4 %collective-permute-start.17 = (bf16[7,64,128]{2,1,0:T(8,128)(2,1)S(1)}, bf16[7,64,128]{2,1,0:T(8,128)(2,1)S(1)}, u32[]{:S(2)}, u32[]{:S(2)}) collective-permute-start(bf16[7,64,128]{2,1,0:T(8,128)(2,1)S(1)} %concatenate.48), channel_id=1, source_target_pairs={{0,6},{2,4},{4,2},{6,0},{1,7},{3,5},{5,3},{7,1},{8,14},{10,12},{12... | collective-permute-start | bytes 344072 | tf_op jit(solution)/shard_map/ppermute | solution.py:427
  40.7 1.5 %conv2.1 = bf16[4,8,32,128]{3,2,1,0:T(8,128)(2,1)S(1)} custom-call(s32[3]{0:T(128)S(1)} %pad_add_fusion.place, bf16[10,64,128]{2,1,0:T(8,128)(2,1)S(1)} %pad_maximum_fusion.6.ur, bf16[10,64,128]{2,1,0:T(8,128)(2,1)S(1)} %collective-permute-done.12.ua, bf16[10,64,128]{2,1,0:T(8,128)(2,1)S(1)} %collective-permute-done.13.ub, ...), custom_call_target="tpu_custom_call" | custom-call | flops 1073741824 | bytes 1048576 | tf_op jit(solution)/shard_map/conv2/pallas_call | solution.py:61
  42.3 0.0 copy-start.5
  42.3 2.0 %collective-permute-start.18 = (bf16[256,128]{1,0:T(8,128)(2,1)S(1)}, bf16[256,128]{1,0:T(8,128)(2,1)S(1)}, u32[]{:S(2)}, u32[]{:S(2)}) collective-permute-start(bf16[256,128]{1,0:T(8,128)(2,1)S(1)} %bitcast.70), channel_id=1, source_target_pairs={{0,2},{2,0},{4,6},{6,4},{1,3},{3,1},{5,7},{7,5},{8,10},{10,8},{12,... | collective-permute-start | bytes 196616 | tf_op jit(solution)/shard_map/ppermute | solution.py:427
  44.3 2.0 %collective-permute-done.16 = bf16[7,64,128]{2,1,0:T(8,128)(2,1)S(1)} collective-permute-done((bf16[7,64,128]{2,1,0:T(8,128)(2,1)S(1)}, bf16[7,64,128]{2,1,0:T(8,128)(2,1)S(1)}, u32[]{:S(2)}, u32[]{:S(2)}) %collective-permute-start.16) | collective-permute-done | bytes 114720 | tf_op jit(solution)/shard_map/ppermute | solution.py:427
  46.3 0.8 %collective-permute-done.17 = bf16[7,64,128]{2,1,0:T(8,128)(2,1)S(1)} collective-permute-done((bf16[7,64,128]{2,1,0:T(8,128)(2,1)S(1)}, bf16[7,64,128]{2,1,0:T(8,128)(2,1)S(1)}, u32[]{:S(2)}, u32[]{:S(2)}) %collective-permute-start.17) | collective-permute-done | bytes 114720 | tf_op jit(solution)/shard_map/ppermute | solution.py:427
  47.2 0.0 collective-permute-done.18.refs_1_
  47.2 0.1 fusion.4
  47.2 1.8 %collective-permute-start.19 = (bf16[7,64,128]{2,1,0:T(8,128)(2,1)S(1)}, bf16[7,64,128]{2,1,0:T(8,128)(2,1)S(1)}, u32[]{:S(2)}, u32[]{:S(2)}) collective-permute-start(bf16[7,64,128]{2,1,0:T(8,128)(2,1)S(1)} %fusion.4), channel_id=1, source_target_pairs={{0,8},{8,0},{16,24},{24,16},{1,9},{9,1},{17,25},{25,17},{2,10},{10... | collective-permute-start | bytes 344072 | tf_op jit(solution)/shard_map/ppermute | solution.py:427
  49.0 1.5 %collective-permute-start.20 = (bf16[7,64,128]{2,1,0:T(8,128)(2,1)S(1)}, bf16[7,64,128]{2,1,0:T(8,128)(2,1)S(1)}, u32[]{:S(2)}, u32[]{:S(2)}) collective-permute-start(bf16[7,64,128]{2,1,0:T(8,128)(2,1)S(1)} %fusion.4), channel_id=1, source_target_pairs={{0,16},{8,24},{16,0},{24,8},{1,17},{9,25},{17,1},{25,9},{2,18},{10... | collective-permute-start | bytes 344072 | tf_op jit(solution)/shard_map/ppermute | solution.py:427
  50.5 1.2 %collective-permute-start.21 = (bf16[7,64,128]{2,1,0:T(8,128)(2,1)S(1)}, bf16[7,64,128]{2,1,0:T(8,128)(2,1)S(1)}, u32[]{:S(2)}, u32[]{:S(2)}) collective-permute-start(bf16[7,64,128]{2,1,0:T(8,128)(2,1)S(1)} %fusion.4), channel_id=1, source_target_pairs={{0,24},{8,16},{16,8},{24,0},{1,25},{9,17},{17,9},{25,1},{2,26},{10... | collective-permute-start | bytes 344072 | tf_op jit(solution)/shard_map/ppermute | solution.py:427
  51.7 1.5 %collective-permute-start.22 = (bf16[256,128]{1,0:T(8,128)(2,1)S(1)}, bf16[256,128]{1,0:T(8,128)(2,1)S(1)}, u32[]{:S(2)}, u32[]{:S(2)}) collective-permute-start(bf16[256,128]{1,0:T(8,128)(2,1)S(1)} %get-tuple-element.124), channel_id=1, source_target_pairs={{0,4},{2,6},{4,0},{6,2},{1,5},{3,7},{5,1},{7,3},{8,12},{10,14},{12... | collective-permute-start | bytes 196616 | tf_op jit(solution)/shard_map/ppermute | solution.py:427
  53.2 1.4 %collective-permute-start.23 = (bf16[256,128]{1,0:T(8,128)(2,1)S(1)}, bf16[256,128]{1,0:T(8,128)(2,1)S(1)}, u32[]{:S(2)}, u32[]{:S(2)}) collective-permute-start(bf16[256,128]{1,0:T(8,128)(2,1)S(1)} %get-tuple-element.123), channel_id=1, source_target_pairs={{0,6},{2,4},{4,2},{6,0},{1,7},{3,5},{5,3},{7,1},{8,14},{10,12},{12... | collective-permute-start | bytes 196616 | tf_op jit(solution)/shard_map/ppermute | solution.py:427
  54.6 1.7 %collective-permute-done.22.refs_2_ = bf16[256,128]{1,0:T(8,128)(2,1)S(1)} collective-permute-done((bf16[256,128]{1,0:T(8,128)(2,1)S(1)}, bf16[256,128]{1,0:T(8,128)(2,1)S(1)}, u32[]{:S(2)}, u32[]{:S(2)}) %collective-permute-start.22) | collective-permute-done | bytes 65568 | tf_op jit(solution)/shard_map/ppermute | solution.py:427
  56.3 2.1 %collective-permute-done.23.refs_3_ = bf16[256,128]{1,0:T(8,128)(2,1)S(1)} collective-permute-done((bf16[256,128]{1,0:T(8,128)(2,1)S(1)}, bf16[256,128]{1,0:T(8,128)(2,1)S(1)}, u32[]{:S(2)}, u32[]{:S(2)}) %collective-permute-start.23) | collective-permute-done | bytes 65568 | tf_op jit(solution)/shard_map/ppermute | solution.py:427
  58.4 0.1 broadcast_in_dim.29.refs_4_
  58.5 1.1 %unpack.1 = f32[32,32,128]{2,1,0:T(8,128)} custom-call(s32[1]{0:T(128)} %bitcast.7.me, bf16[256,128]{1,0:T(8,128)(2,1)S(1)} %get-tuple-element.125.refs_0_, bf16[256,128]{1,0:T(8,128)(2,1)S(1)} %collective-permute-done.18.refs_1_, bf16[256,128]{1,0:T(8,128)(2,1)S(1)} %collective-permute-done.22.refs_2_, ...), custom_call_target="tpu_custom_call" | custom-call | flops 268435456 | bytes 1048576 | tf_op jit(solution)/shard_map/unpack/pallas_call | solution.py:61
  59.6 0.0 collective-permute-done.19
  59.6 0.0 collective-permute-done.20
  59.6 0.0 collective-permute-done.21
  59.6 0.1 add_multiply_fusion.mine
  59.7 0.1 collective-permute-start.24
  59.8 1.5 %collective-permute-done.24.other = f32[7,64,128]{2,1,0:T(8,128)S(1)} collective-permute-done((f32[7,64,128]{2,1,0:T(8,128)S(1)}, f32[7,64,128]{2,1,0:T(8,128)S(1)}, u32[]{:S(2)}, u32[]{:S(2)}) %collective-permute-start.24) | collective-permute-done | bytes 229408 | tf_op jit(solution)/shard_map/ppermute | solution.py:409
  61.3 1.7 %finish.1 = (f32[27,32,64]{2,1,0:T(8,128)}, f32[1,32]{1,0:T(1,128)}, f32[27,32,64]{2,1,0:T(8,128)}, f32[1,64]{1,0:T(1,128)}) custom-call(s32[3]{0:T(128)S(1)} %pad_add_fusion.place, f32[7,64,128]{2,1,0:T(8,128)S(1)} %add_multiply_fusion.mine, f32[7,64,128]{2,1,0:T(8,128)S(1)} %collective-permute-done.24.other), custom_call_target="tpu_custom_call" | custom-call | flops 1048576 | bytes 1048576 | tf_op jit(solution)/shard_map/finish/pallas_call | solution.py:61
  (46 shorter events, 0.5 us)
Async XLA Ops:
  0.6 1.0 %copy-start = (bf16[1,32,2,16,256]{4,3,2,1,0:T(8,128)(2,1)S(1)}, bf16[1,32,2,16,256]{4,3,2,1,0:T(8,128)(2,1)}, u32[]{:S(2)}) copy-start(bf16[1,32,2,16,256]{4,3,2,1,0:T(8,128)(2,1)} %param.6) | copy-start | bytes 1572868
  1.7 4.0 %copy-start.1 = (bf16[1,32,1,32,128]{4,3,2,1,0:T(8,128)(2,1)S(1)}, bf16[1,32,1,32,128]{4,3,2,1,0:T(8,128)(2,1)}, u32[]{:S(2)}) copy-start(bf16[1,32,1,32,128]{4,3,2,1,0:T(8,128)(2,1)} %param.11) | copy-start | bytes 786436
  1.7 4.0 %copy-start.2 = (bf16[32,64,3,3,3]{1,0,4,3,2:T(8,128)(2,1)S(1)}, bf16[32,64,3,3,3]{1,0,4,3,2:T(8,128)(2,1)}, u32[]{:S(2)}) copy-start(bf16[32,64,3,3,3]{1,0,4,3,2:T(8,128)(2,1)} %param.9) | copy-start | bytes 331780
  2.7 8.7 %collective-permute-start = (bf16[2,1,32,256]{3,2,1,0:T(8,128)(2,1)S(1)}, bf16[2,1,32,256]{3,2,1,0:T(8,128)(2,1)S(1)}, u32[]{:S(2)}, u32[]{:S(2)}) collective-permute-start(bf16[2,1,32,256]{3,2,1,0:T(8,128)(2,1)S(1)} %get-tuple-element.112), channel_id=1, source_target_pairs={{0,2},{2,0},{4,6},{6,4},{1,3},{3,1},{5,7},{7,5},{8,10},{10,8},{12,... | collective-permute-start | bytes 98312 | tf_op jit(solution)/shard_map/ppermute | solution.py:409
  5.7 5.7 %collective-permute-start.1 = (bf16[2,1,32,256]{3,2,1,0:T(8,128)(2,1)S(1)}, bf16[2,1,32,256]{3,2,1,0:T(8,128)(2,1)S(1)}, u32[]{:S(2)}, u32[]{:S(2)}) collective-permute-start(bf16[2,1,32,256]{3,2,1,0:T(8,128)(2,1)S(1)} %get-tuple-element.111), channel_id=1, source_target_pairs={{0,1},{1,0},{2,4},{3,5},{4,2},{5,3},{6,7},{7,6},{8,9},{9,8},{10,12... | collective-permute-start | bytes 98312 | tf_op jit(solution)/shard_map/ppermute | solution.py:422
  5.7 5.2 %copy-start.3 = (bf16[64,32,3,3,3]{0,1,4,3,2:T(8,128)(2,1)S(1)}, bf16[64,32,3,3,3]{0,1,4,3,2:T(8,128)(2,1)}, u32[]{:S(2)}) copy-start(bf16[64,32,3,3,3]{0,1,4,3,2:T(8,128)(2,1)} %param.7) | copy-start | bytes 331780
  5.7 5.5 %copy-start.4 = (f32[64]{0:T(128)S(1)}, f32[64]{0:T(128)}, u32[]{:S(2)}) copy-start(f32[64]{0:T(128)} %param.8) | copy-start | bytes 772
  6.3 8.5 %collective-permute-start.4 = (bf16[17,32,128]{2,1,0:T(8,128)(2,1)S(1)}, bf16[17,32,128]{2,1,0:T(8,128)(2,1)S(1)}, u32[]{:S(2)}, u32[]{:S(2)}) collective-permute-start(bf16[17,32,128]{2,1,0:T(8,128)(2,1)S(1)} %get-tuple-element.134), channel_id=1, source_target_pairs={{0,2},{2,0},{4,6},{6,4},{1,3},{3,1},{5,7},{7,5},{8,10},{10,8},{12,... | collective-permute-start | bytes 417800 | tf_op jit(solution)/shard_map/ppermute | solution.py:427
  9.4 7.6 %collective-permute-start.5 = (bf16[17,32,128]{2,1,0:T(8,128)(2,1)S(1)}, bf16[17,32,128]{2,1,0:T(8,128)(2,1)S(1)}, u32[]{:S(2)}, u32[]{:S(2)}) collective-permute-start(bf16[17,32,128]{2,1,0:T(8,128)(2,1)S(1)} %get-tuple-element.133), channel_id=1, source_target_pairs={{0,4},{2,6},{4,0},{6,2},{1,5},{3,7},{5,1},{7,3},{8,12},{10,14},{12... | collective-permute-start | bytes 417800 | tf_op jit(solution)/shard_map/ppermute | solution.py:427
  9.4 7.6 %collective-permute-start.6 = (bf16[17,32,128]{2,1,0:T(8,128)(2,1)S(1)}, bf16[17,32,128]{2,1,0:T(8,128)(2,1)S(1)}, u32[]{:S(2)}, u32[]{:S(2)}) collective-permute-start(bf16[17,32,128]{2,1,0:T(8,128)(2,1)S(1)} %get-tuple-element.132), channel_id=1, source_target_pairs={{0,6},{2,4},{4,2},{6,0},{1,7},{3,5},{5,3},{7,1},{8,14},{10,12},{12... | collective-permute-start | bytes 417800 | tf_op jit(solution)/shard_map/ppermute | solution.py:427
  11.5 8.6 %collective-permute-start.2 = (bf16[18,32,256]{2,1,0:T(8,128)(2,1)S(1)}, bf16[18,32,256]{2,1,0:T(8,128)(2,1)S(1)}, u32[]{:S(2)}, u32[]{:S(2)}) collective-permute-start(bf16[18,32,256]{2,1,0:T(8,128)(2,1)S(1)} %get-tuple-element.110), channel_id=1, source_target_pairs={{0,8},{8,0},{16,24},{24,16},{1,9},{9,1},{17,25},{25,17},{2,10},{10... | collective-permute-start | bytes 884744 | tf_op jit(solution)/shard_map/ppermute | solution.py:409
  13.1 7.0 %collective-permute-start.3 = (bf16[18,32,256]{2,1,0:T(8,128)(2,1)S(1)}, bf16[18,32,256]{2,1,0:T(8,128)(2,1)S(1)}, u32[]{:S(2)}, u32[]{:S(2)}) collective-permute-start(bf16[18,32,256]{2,1,0:T(8,128)(2,1)S(1)} %get-tuple-element.109), channel_id=1, source_target_pairs={{0,1},{1,0},{8,16},{9,17},{16,8},{17,9},{24,25},{25,24},{2,3},{3,2... | collective-permute-start | bytes 884744 | tf_op jit(solution)/shard_map/ppermute | solution.py:422
  17.0 12.0 %collective-permute-start.8 = (bf16[4,10,32,128]{3,2,1,0:T(8,128)(2,1)S(1)}, bf16[4,10,32,128]{3,2,1,0:T(8,128)(2,1)S(1)}, u32[]{:S(2)}, u32[]{:S(2)}) collective-permute-start(bf16[4,10,32,128]{3,2,1,0:T(8,128)(2,1)S(1)} %pad_maximum_fusion.1.co), channel_id=1, source_target_pairs={{0,8},{8,0},{16,24},{24,16},{1,9},{9,1},{17,25},{25,17},{2,10},{10... | collective-permute-start | bytes 983048 | tf_op jit(solution)/shard_map/ppermute | solution.py:409
  18.6 10.3 %collective-permute-start.9 = (bf16[4,10,32,128]{3,2,1,0:T(8,128)(2,1)S(1)}, bf16[4,10,32,128]{3,2,1,0:T(8,128)(2,1)S(1)}, u32[]{:S(2)}, u32[]{:S(2)}) collective-permute-start(bf16[4,10,32,128]{3,2,1,0:T(8,128)(2,1)S(1)} %pad_maximum_fusion.1.co), channel_id=1, source_target_pairs={{0,1},{1,0},{8,16},{9,17},{16,8},{17,9},{24,25},{25,24},{2,3},{3,2... | collective-permute-start | bytes 983048 | tf_op jit(solution)/shard_map/ppermute | solution.py:422
  18.7 3.1 %collective-permute-start.7 = (bf16[3,7,32,128]{3,2,1,0:T(8,128)(2,1)S(1)}, bf16[3,7,32,128]{3,2,1,0:T(8,128)(2,1)S(1)}, u32[]{:S(2)}, u32[]{:S(2)}) collective-permute-start(bf16[3,7,32,128]{3,2,1,0:T(8,128)(2,1)S(1)} %pad_maximum_fusion.5), channel_id=1, source_target_pairs={{0,1},{1,0},{2,3},{3,2},{4,5},{5,4},{6,7},{7,6},{8,9},{9,8},{10,11... | collective-permute-start | bytes 516104 | tf_op jit(solution)/shard_map/ppermute | solution.py:409
  21.8 3.8 %collective-permute-start.10 = (bf16[64,128]{1,0:T(8,128)(2,1)S(1)}, bf16[64,128]{1,0:T(8,128)(2,1)S(1)}, u32[]{:S(2)}, u32[]{:S(2)}) collective-permute-start(bf16[64,128]{1,0:T(8,128)(2,1)S(1)} %get-tuple-element.127), channel_id=1, source_target_pairs={{0,2},{2,0},{4,6},{6,4},{1,3},{3,1},{5,7},{7,5},{8,10},{10,8},{12,... | collective-permute-start | bytes 49160 | tf_op jit(solution)/shard_map/ppermute | solution.py:409
  23.4 2.2 %collective-permute-start.11 = (bf16[64,128]{1,0:T(8,128)(2,1)S(1)}, bf16[64,128]{1,0:T(8,128)(2,1)S(1)}, u32[]{:S(2)}, u32[]{:S(2)}) collective-permute-start(bf16[64,128]{1,0:T(8,128)(2,1)S(1)} %get-tuple-element.126), channel_id=1, source_target_pairs={{0,1},{1,0},{2,4},{3,5},{4,2},{5,3},{6,7},{7,6},{8,9},{9,8},{10,12... | collective-permute-start | bytes 49160 | tf_op jit(solution)/shard_map/ppermute | solution.py:422
  25.6 8.5 %collective-permute-start.12 = (bf16[10,64,128]{2,1,0:T(8,128)(2,1)S(1)}, bf16[10,64,128]{2,1,0:T(8,128)(2,1)S(1)}, u32[]{:S(2)}, u32[]{:S(2)}) collective-permute-start(bf16[10,64,128]{2,1,0:T(8,128)(2,1)S(1)} %pad_maximum_fusion.6.ur), channel_id=1, source_target_pairs={{0,8},{8,0},{16,24},{24,16},{1,9},{9,1},{17,25},{25,17},{2,10},{10... | collective-permute-start | bytes 491528 | tf_op jit(solution)/shard_map/ppermute | solution.py:409
  29.0 5.2 %collective-permute-start.13 = (bf16[10,64,128]{2,1,0:T(8,128)(2,1)S(1)}, bf16[10,64,128]{2,1,0:T(8,128)(2,1)S(1)}, u32[]{:S(2)}, u32[]{:S(2)}) collective-permute-start(bf16[10,64,128]{2,1,0:T(8,128)(2,1)S(1)} %pad_maximum_fusion.6.ur), channel_id=1, source_target_pairs={{0,1},{1,0},{8,16},{9,17},{16,8},{17,9},{24,25},{25,24},{2,3},{3,2... | collective-permute-start | bytes 491528 | tf_op jit(solution)/shard_map/ppermute | solution.py:422
  34.2 1.8 %collective-permute-start.14 = (bf16[7,160,128]{2,1,0:T(8,128)(2,1)S(1)}, bf16[7,160,128]{2,1,0:T(8,128)(2,1)S(1)}, u32[]{:S(2)}, u32[]{:S(2)}) collective-permute-start(bf16[7,160,128]{2,1,0:T(8,128)(2,1)S(1)} %get-tuple-element.78), channel_id=1, source_target_pairs={{0,1},{1,0},{2,3},{3,2},{4,5},{5,4},{6,7},{7,6},{8,9},{9,8},{10,11... | collective-permute-start | bytes 860168 | tf_op jit(solution)/shard_map/ppermute | solution.py:409
  36.1 8.1 %collective-permute-start.15 = (bf16[7,64,128]{2,1,0:T(8,128)(2,1)S(1)}, bf16[7,64,128]{2,1,0:T(8,128)(2,1)S(1)}, u32[]{:S(2)}, u32[]{:S(2)}) collective-permute-start(bf16[7,64,128]{2,1,0:T(8,128)(2,1)S(1)} %get-tuple-element.131), channel_id=1, source_target_pairs={{0,2},{2,0},{4,6},{6,4},{1,3},{3,1},{5,7},{7,5},{8,10},{10,8},{12,... | collective-permute-start | bytes 344072 | tf_op jit(solution)/shard_map/ppermute | solution.py:427
  39.1 7.2 %collective-permute-start.16 = (bf16[7,64,128]{2,1,0:T(8,128)(2,1)S(1)}, bf16[7,64,128]{2,1,0:T(8,128)(2,1)S(1)}, u32[]{:S(2)}, u32[]{:S(2)}) collective-permute-start(bf16[7,64,128]{2,1,0:T(8,128)(2,1)S(1)} %get-tuple-element.130), channel_id=1, source_target_pairs={{0,4},{2,6},{4,0},{6,2},{1,5},{3,7},{5,1},{7,3},{8,12},{10,14},{12... | collective-permute-start | bytes 344072 | tf_op jit(solution)/shard_map/ppermute | solution.py:427
  39.3 7.8 %collective-permute-start.17 = (bf16[7,64,128]{2,1,0:T(8,128)(2,1)S(1)}, bf16[7,64,128]{2,1,0:T(8,128)(2,1)S(1)}, u32[]{:S(2)}, u32[]{:S(2)}) collective-permute-start(bf16[7,64,128]{2,1,0:T(8,128)(2,1)S(1)} %concatenate.48), channel_id=1, source_target_pairs={{0,6},{2,4},{4,2},{6,0},{1,7},{3,5},{5,3},{7,1},{8,14},{10,12},{12... | collective-permute-start | bytes 344072 | tf_op jit(solution)/shard_map/ppermute | solution.py:427
  42.3 16.1 %copy-start.5 = (f32[32]{0:T(128)S(1)}, f32[32]{0:T(128)}, u32[]{:S(2)}) copy-start(f32[32]{0:T(128)} %param.10) | copy-start | bytes 388
  42.3 4.9 %collective-permute-start.18 = (bf16[256,128]{1,0:T(8,128)(2,1)S(1)}, bf16[256,128]{1,0:T(8,128)(2,1)S(1)}, u32[]{:S(2)}, u32[]{:S(2)}) collective-permute-start(bf16[256,128]{1,0:T(8,128)(2,1)S(1)} %bitcast.70), channel_id=1, source_target_pairs={{0,2},{2,0},{4,6},{6,4},{1,3},{3,1},{5,7},{7,5},{8,10},{10,8},{12,... | collective-permute-start | bytes 196616 | tf_op jit(solution)/shard_map/ppermute | solution.py:427
  47.2 12.4 %collective-permute-start.19 = (bf16[7,64,128]{2,1,0:T(8,128)(2,1)S(1)}, bf16[7,64,128]{2,1,0:T(8,128)(2,1)S(1)}, u32[]{:S(2)}, u32[]{:S(2)}) collective-permute-start(bf16[7,64,128]{2,1,0:T(8,128)(2,1)S(1)} %fusion.4), channel_id=1, source_target_pairs={{0,8},{8,0},{16,24},{24,16},{1,9},{9,1},{17,25},{25,17},{2,10},{10... | collective-permute-start | bytes 344072 | tf_op jit(solution)/shard_map/ppermute | solution.py:427
  49.0 10.6 %collective-permute-start.20 = (bf16[7,64,128]{2,1,0:T(8,128)(2,1)S(1)}, bf16[7,64,128]{2,1,0:T(8,128)(2,1)S(1)}, u32[]{:S(2)}, u32[]{:S(2)}) collective-permute-start(bf16[7,64,128]{2,1,0:T(8,128)(2,1)S(1)} %fusion.4), channel_id=1, source_target_pairs={{0,16},{8,24},{16,0},{24,8},{1,17},{9,25},{17,1},{25,9},{2,18},{10... | collective-permute-start | bytes 344072 | tf_op jit(solution)/shard_map/ppermute | solution.py:427
  50.5 9.1 %collective-permute-start.21 = (bf16[7,64,128]{2,1,0:T(8,128)(2,1)S(1)}, bf16[7,64,128]{2,1,0:T(8,128)(2,1)S(1)}, u32[]{:S(2)}, u32[]{:S(2)}) collective-permute-start(bf16[7,64,128]{2,1,0:T(8,128)(2,1)S(1)} %fusion.4), channel_id=1, source_target_pairs={{0,24},{8,16},{16,8},{24,0},{1,25},{9,17},{17,9},{25,1},{2,26},{10... | collective-permute-start | bytes 344072 | tf_op jit(solution)/shard_map/ppermute | solution.py:427
  51.7 4.5 %collective-permute-start.22 = (bf16[256,128]{1,0:T(8,128)(2,1)S(1)}, bf16[256,128]{1,0:T(8,128)(2,1)S(1)}, u32[]{:S(2)}, u32[]{:S(2)}) collective-permute-start(bf16[256,128]{1,0:T(8,128)(2,1)S(1)} %get-tuple-element.124), channel_id=1, source_target_pairs={{0,4},{2,6},{4,0},{6,2},{1,5},{3,7},{5,1},{7,3},{8,12},{10,14},{12... | collective-permute-start | bytes 196616 | tf_op jit(solution)/shard_map/ppermute | solution.py:427
  53.2 5.2 %collective-permute-start.23 = (bf16[256,128]{1,0:T(8,128)(2,1)S(1)}, bf16[256,128]{1,0:T(8,128)(2,1)S(1)}, u32[]{:S(2)}, u32[]{:S(2)}) collective-permute-start(bf16[256,128]{1,0:T(8,128)(2,1)S(1)} %get-tuple-element.123), channel_id=1, source_target_pairs={{0,6},{2,4},{4,2},{6,0},{1,7},{3,5},{5,3},{7,1},{8,14},{10,12},{12... | collective-permute-start | bytes 196616 | tf_op jit(solution)/shard_map/ppermute | solution.py:427
  59.7 1.6 %collective-permute-start.24 = (f32[7,64,128]{2,1,0:T(8,128)S(1)}, f32[7,64,128]{2,1,0:T(8,128)S(1)}, u32[]{:S(2)}, u32[]{:S(2)}) collective-permute-start(f32[7,64,128]{2,1,0:T(8,128)S(1)} %add_multiply_fusion.mine), channel_id=1, source_target_pairs={{0,1},{1,0},{2,3},{3,2},{4,5},{5,4},{6,7},{7,6},{8,9},{9,8},{10,11... | collective-permute-start | bytes 688136 | tf_op jit(solution)/shard_map/ppermute | solution.py:409

commit v6 on v5

--- a/solution.py
+++ b/solution.py
@@ -631,6 +631,7 @@
     part, flat = lax.optimization_barrier((part, flat))
     parts = [part] + [to_partner(part, "sx", s) for s in range(1, n_sx)]
     out_got = [flat[0], beside_sy] + [to_partner(flat[s], "sy", s) for s in range(2, n_sy)]
+    parts, out_got = lax.optimization_barrier((parts, out_got))
     bias_wide = jnp.broadcast_to(second_bias[:, None, None], (nf, 1, width2))
     second_out = call(
         unpack_body,
@@ -641,9 +642,9 @@
         smem_ins=1,
         flops=1 << 28,
     )
-    parts, second_out = lax.optimization_barrier((parts, second_out))
     total = tree_sum(parts) * scale
     other = swap_first(total, "rep")
+    other, second_out = lax.optimization_barrier((other, second_out))
     g2, t2, g1, t1 = call(
         finish_body,
         "finish",

time: 63.1 us -> 63.1 us (level)
    ppermute x8, waiting for transfers between devices: 4.3 us -> 3.09 us  [swap_first(): return lax.ppermute(value, axis, [(i, i ^ 1) for i in range(count)])]
    ppermute x12, waiting for transfers between devices: 8.68 us -> 9.89 us  [to_partner(): return lax.ppermute(value, axis, [(i, i ^ s) for i in range(count)])]
  transfers between devices with their start and end apart: 25 -> 25, of which waited for: 9 -> 10; matrix products, arithmetic and copies ran while one was open for 2% -> 2% of each run, Pallas kernels for 21% -> 21%
where the time goes in v6:
time: 63.1 us; the launch traced here: 62.9 us
  starting transfers between devices  30.9 us (49%)
  Pallas kernels  15.6 us (25%)
  waiting for transfers between devices  13 us (21%)
  local copies, waits for them, and re-layouts  1.4 us (2%)
  between operations  1.08 us (2%)
  other arithmetic  0.95 us (2%)
    ppermute x12, starting transfers between devices, to_partner(): return lax.ppermute(value, axis, [(i, i ^ s) for i in range(count)])  18.4 us
    pallas_call x10, Pallas kernels, call(): pl.pallas_call(body, name=name, out_shape=outs, in_specs=[sm] * smem_ins...  15.6 us
    ppermute x8, starting transfers between devices, swap_first(): return lax.ppermute(value, axis, [(i, i ^ 1) for i in range(count)])  12.4 us
    ppermute x12, waiting for transfers between devices, to_partner(): return lax.ppermute(value, axis, [(i, i ^ s) for i in range(count)])  9.89 us
    ppermute x8, waiting for transfers between devices, swap_first(): return lax.ppermute(value, axis, [(i, i ^ 1) for i in range(count)])  3.09 us
  transfers between devices with their start and end apart: 25, of which 10 were waited for; matrix products, arithmetic and copies ran while one was open for 2% of the time, Pallas kernels for 21%

profile of v6, /device:TPU:0, one launch (start us, length us, event | category | flops | bytes accessed | tf_op | source)
XLA Modules:
  0.0 62.9 jit_solution(2847185303457943246)
XLA Ops:
  0.7 1.0 %copy-done = bf16[1,32,2,16,256]{4,3,2,1,0:T(8,128)(2,1)S(1)} copy-done((bf16[1,32,2,16,256]{4,3,2,1,0:T(8,128)(2,1)S(1)}, bf16[1,32,2,16,256]{4,3,2,1,0:T(8,128)(2,1)}, u32[]{:S(2)}) %copy-start) | copy-done | bytes 524312
  1.7 0.9 %volume_cells.1 = bf16[2,16,32,256]{3,2,1,0:T(8,128)(2,1)S(1)} custom-call(bf16[32,2,16,256]{3,2,1,0:T(8,128)(2,1)S(1)} %bitcast.62), custom_call_target="tpu_custom_call" | custom-call | flops 1073741824 | bytes 1048576 | tf_op jit(solution)/shard_map/volume_cells/pallas_call | solution.py:61
  2.7 3.0 %collective-permute-start = (bf16[2,1,32,256]{3,2,1,0:T(8,128)(2,1)S(1)}, bf16[2,1,32,256]{3,2,1,0:T(8,128)(2,1)S(1)}, u32[]{:S(2)}, u32[]{:S(2)}) collective-permute-start(bf16[2,1,32,256]{3,2,1,0:T(8,128)(2,1)S(1)} %get-tuple-element.122), channel_id=1, source_target_pairs={{0,2},{2,0},{4,6},{6,4},{1,3},{3,1},{5,7},{7,5},{8,10},{10,8},{12,... | collective-permute-start | bytes 98312 | tf_op jit(solution)/shard_map/ppermute | solution.py:409
  5.7 0.0 copy-start.3
  5.7 0.0 copy-start.4
  5.7 0.5 cotangent_cells.1
  6.3 3.0 %collective-permute-start.4 = (bf16[17,32,128]{2,1,0:T(8,128)(2,1)S(1)}, bf16[17,32,128]{2,1,0:T(8,128)(2,1)S(1)}, u32[]{:S(2)}, u32[]{:S(2)}) collective-permute-start(bf16[17,32,128]{2,1,0:T(8,128)(2,1)S(1)} %get-tuple-element.144), channel_id=1, source_target_pairs={{0,2},{2,0},{4,6},{6,4},{1,3},{3,1},{5,7},{7,5},{8,10},{10,8},{12,... | collective-permute-start | bytes 417800 | tf_op jit(solution)/shard_map/ppermute | solution.py:427
  9.4 1.5 %collective-permute-start.6 = (bf16[17,32,128]{2,1,0:T(8,128)(2,1)S(1)}, bf16[17,32,128]{2,1,0:T(8,128)(2,1)S(1)}, u32[]{:S(2)}, u32[]{:S(2)}) collective-permute-start(bf16[17,32,128]{2,1,0:T(8,128)(2,1)S(1)} %get-tuple-element.142), channel_id=1, source_target_pairs={{0,6},{2,4},{4,2},{6,0},{1,7},{3,5},{5,3},{7,1},{8,14},{10,12},{12... | collective-permute-start | bytes 417800 | tf_op jit(solution)/shard_map/ppermute | solution.py:427
  10.9 0.2 fusion.2.w1q
  11.1 0.1 pad_add_fusion.place
  11.2 0.1 broadcast_in_dim_tile.4.bias
  11.3 0.0 collective-permute-done.1
  11.4 0.1 pad_maximum_fusion.vr
  11.5 1.6 %collective-permute-start.2 = (bf16[18,32,256]{2,1,0:T(8,128)(2,1)S(1)}, bf16[18,32,256]{2,1,0:T(8,128)(2,1)S(1)}, u32[]{:S(2)}, u32[]{:S(2)}) collective-permute-start(bf16[18,32,256]{2,1,0:T(8,128)(2,1)S(1)} %get-tuple-element.120), channel_id=1, source_target_pairs={{0,8},{8,0},{16,24},{24,16},{1,9},{9,1},{17,25},{25,17},{2,10},{10... | collective-permute-start | bytes 884744 | tf_op jit(solution)/shard_map/ppermute | solution.py:409
  13.1 0.0 collective-permute-start.3
  13.1 1.7 %conv1_own.1 = (bf16[2,18,128,128]{3,2,1,0:T(8,128)(2,1)S(1)}, bf16[3,256,512]{2,1,0:T(8,128)(2,1)S(1)}, f32[2,4,256,256]{3,2,1,0:T(8,128)S(1)}) custom-call(bf16[2,18,32,256]{3,2,1,0:T(8,128)(2,1)S(1)} %pad_maximum_fusion.vr, bf16[3,3,4,32,128]{4,3,2,1,0:T(8,128)(2,1)S(1)} %fusion.2.w1q, f32[256,1]{1,0:T(8,128)S(1)} %broadcast_in_dim_tile.4.bias), custom_call_target="tpu_custom_call" | custom-call | flops 2147483648 | bytes 1048576 | tf_op jit(solution)/shard_map/conv1_own/pallas_call | solution.py:61
  14.9 0.0 collective-permute-done.4
  14.9 2.0 %collective-permute-done.5 = bf16[17,32,128]{2,1,0:T(8,128)(2,1)S(1)} collective-permute-done((bf16[17,32,128]{2,1,0:T(8,128)(2,1)S(1)}, bf16[17,32,128]{2,1,0:T(8,128)(2,1)S(1)}, u32[]{:S(2)}, u32[]{:S(2)}) %collective-permute-start.5) | collective-permute-done | bytes 139296 | tf_op jit(solution)/shard_map/ppermute | solution.py:427
  17.0 1.6 %collective-permute-start.8 = (bf16[4,10,32,128]{3,2,1,0:T(8,128)(2,1)S(1)}, bf16[4,10,32,128]{3,2,1,0:T(8,128)(2,1)S(1)}, u32[]{:S(2)}, u32[]{:S(2)}) collective-permute-start(bf16[4,10,32,128]{3,2,1,0:T(8,128)(2,1)S(1)} %pad_maximum_fusion.1.co), channel_id=1, source_target_pairs={{0,8},{8,0},{16,24},{24,16},{1,9},{9,1},{17,25},{25,17},{2,10},{10... | collective-permute-start | bytes 983048 | tf_op jit(solution)/shard_map/ppermute | solution.py:409
  18.7 0.6 collective-permute-start.7
  19.3 0.9 %collective-permute-done.2.za = bf16[18,32,256]{2,1,0:T(8,128)(2,1)S(1)} collective-permute-done((bf16[18,32,256]{2,1,0:T(8,128)(2,1)S(1)}, bf16[18,32,256]{2,1,0:T(8,128)(2,1)S(1)}, u32[]{:S(2)}, u32[]{:S(2)}) %collective-permute-start.2) | collective-permute-done | bytes 294944 | tf_op jit(solution)/shard_map/ppermute | solution.py:409
  20.1 0.0 collective-permute-done.3.zb
  20.1 1.6 %conv1.1 = (bf16[18,128,128]{2,1,0:T(8,128)(2,1)S(1)}, bf16[18,128,128]{2,1,0:T(8,128)(2,1)S(1)}, bf16[2,8,256,128]{3,2,1,0:T(8,128)(2,1)S(1)}, bf16[8,64,128]{2,1,0:T(8,128)(2,1)S(1)}) custom-call(s32[3]{0:T(128)S(1)} %pad_add_fusion.place, bf16[18,32,256]{2,1,0:T(8,128)(2,1)S(1)} %collective-permute-done.2.za, ...), custom_call_target="tpu_custom_call" | custom-call | flops 1073741824 | bytes 1048576 | tf_op jit(solution)/shard_map/conv1/pallas_call | solution.py:61
  21.8 0.0 collective-permute-done.7
  21.8 1.6 %collective-permute-start.10 = (bf16[64,128]{1,0:T(8,128)(2,1)S(1)}, bf16[64,128]{1,0:T(8,128)(2,1)S(1)}, u32[]{:S(2)}, u32[]{:S(2)}) collective-permute-start(bf16[64,128]{1,0:T(8,128)(2,1)S(1)} %get-tuple-element.137), channel_id=1, source_target_pairs={{0,2},{2,0},{4,6},{6,4},{1,3},{3,1},{5,7},{7,5},{8,10},{10,8},{12,... | collective-permute-start | bytes 49160 | tf_op jit(solution)/shard_map/ppermute | solution.py:409
  23.4 0.0 collective-permute-start.11
  23.4 0.1 maximum_maximum_fusion.w2r
  23.5 1.3 %backward_own.1 = (bf16[3,192,384]{2,1,0:T(8,128)(2,1)S(1)}, bf16[256,1024]{1,0:T(8,128)(2,1)S(1)}, f32[4,192,256]{2,1,0:T(8,128)S(1)}, f32[384,256]{1,0:T(8,128)S(1)}, f32[128,128]{1,0:T(8,128)S(1)}) custom-call(bf16[4,10,32,128]{3,2,1,0:T(8,128)(2,1)S(1)} %pad_maximum_fusion.1.co, bf16[8,64,128]{2,1,0:T(8,128)(2,1)S(1)} %get-tuple-element.71.pooled, ...), custom_call_target="tpu_custom_call" | custom-call | flops 2147483648 | bytes 1048576 | tf_op jit(solution)/shard_map/backward_own/pallas_call | solution.py:61
  24.8 0.8 %collective-permute-done.10 = bf16[64,128]{1,0:T(8,128)(2,1)S(1)} collective-permute-done((bf16[64,128]{1,0:T(8,128)(2,1)S(1)}, bf16[64,128]{1,0:T(8,128)(2,1)S(1)}, u32[]{:S(2)}, u32[]{:S(2)}) %collective-permute-start.10) | collective-permute-done | bytes 16416 | tf_op jit(solution)/shard_map/ppermute | solution.py:409
  25.6 0.0 collective-permute-done.11
  25.6 3.3 %collective-permute-start.12 = (bf16[10,64,128]{2,1,0:T(8,128)(2,1)S(1)}, bf16[10,64,128]{2,1,0:T(8,128)(2,1)S(1)}, u32[]{:S(2)}, u32[]{:S(2)}) collective-permute-start(bf16[10,64,128]{2,1,0:T(8,128)(2,1)S(1)} %pad_maximum_fusion.6.ur), channel_id=1, source_target_pairs={{0,8},{8,0},{16,24},{24,16},{1,9},{9,1},{17,25},{25,17},{2,10},{10... | collective-permute-start | bytes 491528 | tf_op jit(solution)/shard_map/ppermute | solution.py:409
  29.0 2.6 %backward.1 = (bf16[2,4,256,256]{3,2,1,0:T(8,128)(2,1)S(1)}, f32[2,384,256]{2,1,0:T(8,128)S(1)}, f32[8,256]{1,0:T(8,128)S(1)}) custom-call(s32[3]{0:T(128)S(1)} %pad_add_fusion.place, bf16[2,8,256,128]{3,2,1,0:T(8,128)(2,1)S(1)} %get-tuple-element.66.mask, bf16[256,1024]{1,0:T(8,128)(2,1)S(1)} %get-tuple-element.73.wide, ...), custom_call_target="tpu_custom_call" | custom-call | flops 2147483648 | bytes 1048576 | tf_op jit(solution)/shard_map/backward/pallas_call | solution.py:61
  31.6 2.6 %first_weights.1 = (f32[7,160,128]{2,1,0:T(8,128)S(1)}, bf16[7,160,128]{2,1,0:T(8,128)(2,1)S(1)}) custom-call(s32[3]{0:T(128)S(1)} %pad_add_fusion.place, bf16[2,18,128,128]{3,2,1,0:T(8,128)(2,1)S(1)} %get-tuple-element.57.cells, bf16[18,128,128]{2,1,0:T(8,128)(2,1)S(1)} %get-tuple-element.64.low, bf16[18,128,128]{2,1,0:T(8,128)(2,1)S(1)} %get-tuple-element.65.high, ...), custom_call_target="tpu_custom_call" | custom-call | flops 3221225472 | bytes 1048576 | tf_op jit(solution)/shard_map/first_weights/pallas_call | solution.py:61
  34.2 0.0 collective-permute-done.12.ua
  34.2 0.0 collective-permute-done.13.ub
  34.2 0.6 collective-permute-start.14
  34.7 1.2 %collective-permute-done.14 = bf16[7,160,128]{2,1,0:T(8,128)(2,1)S(1)} collective-permute-done((bf16[7,160,128]{2,1,0:T(8,128)(2,1)S(1)}, bf16[7,160,128]{2,1,0:T(8,128)(2,1)S(1)}, u32[]{:S(2)}, u32[]{:S(2)}) %collective-permute-start.14) | collective-permute-done | bytes 286752 | tf_op jit(solution)/shard_map/ppermute | solution.py:409
  35.9 0.1 convert_add_fusion
  36.1 3.0 %collective-permute-start.15 = (bf16[7,64,128]{2,1,0:T(8,128)(2,1)S(1)}, bf16[7,64,128]{2,1,0:T(8,128)(2,1)S(1)}, u32[]{:S(2)}, u32[]{:S(2)}) collective-permute-start(bf16[7,64,128]{2,1,0:T(8,128)(2,1)S(1)} %get-tuple-element.141), channel_id=1, source_target_pairs={{0,2},{2,0},{4,6},{6,4},{1,3},{3,1},{5,7},{7,5},{8,10},{10,8},{12,... | collective-permute-start | bytes 344072 | tf_op jit(solution)/shard_map/ppermute | solution.py:427
  39.1 0.2 collective-permute-start.16
  39.3 1.4 %collective-permute-start.17 = (bf16[7,64,128]{2,1,0:T(8,128)(2,1)S(1)}, bf16[7,64,128]{2,1,0:T(8,128)(2,1)S(1)}, u32[]{:S(2)}, u32[]{:S(2)}) collective-permute-start(bf16[7,64,128]{2,1,0:T(8,128)(2,1)S(1)} %concatenate.48), channel_id=1, source_target_pairs={{0,6},{2,4},{4,2},{6,0},{1,7},{3,5},{5,3},{7,1},{8,14},{10,12},{12... | collective-permute-start | bytes 344072 | tf_op jit(solution)/shard_map/ppermute | solution.py:427
  40.7 1.5 %conv2.1 = bf16[4,8,32,128]{3,2,1,0:T(8,128)(2,1)S(1)} custom-call(s32[3]{0:T(128)S(1)} %pad_add_fusion.place, bf16[10,64,128]{2,1,0:T(8,128)(2,1)S(1)} %pad_maximum_fusion.6.ur, bf16[10,64,128]{2,1,0:T(8,128)(2,1)S(1)} %collective-permute-done.12.ua, bf16[10,64,128]{2,1,0:T(8,128)(2,1)S(1)} %collective-permute-done.13.ub, ...), custom_call_target="tpu_custom_call" | custom-call | flops 1073741824 | bytes 1048576 | tf_op jit(solution)/shard_map/conv2/pallas_call | solution.py:61
  42.3 0.0 copy-start.5
  42.3 2.0 %collective-permute-start.18 = (bf16[256,128]{1,0:T(8,128)(2,1)S(1)}, bf16[256,128]{1,0:T(8,128)(2,1)S(1)}, u32[]{:S(2)}, u32[]{:S(2)}) collective-permute-start(bf16[256,128]{1,0:T(8,128)(2,1)S(1)} %bitcast.70), channel_id=1, source_target_pairs={{0,2},{2,0},{4,6},{6,4},{1,3},{3,1},{5,7},{7,5},{8,10},{10,8},{12,... | collective-permute-start | bytes 196616 | tf_op jit(solution)/shard_map/ppermute | solution.py:427
  44.3 2.0 %collective-permute-done.16 = bf16[7,64,128]{2,1,0:T(8,128)(2,1)S(1)} collective-permute-done((bf16[7,64,128]{2,1,0:T(8,128)(2,1)S(1)}, bf16[7,64,128]{2,1,0:T(8,128)(2,1)S(1)}, u32[]{:S(2)}, u32[]{:S(2)}) %collective-permute-start.16) | collective-permute-done | bytes 114720 | tf_op jit(solution)/shard_map/ppermute | solution.py:427
  46.3 0.8 %collective-permute-done.17 = bf16[7,64,128]{2,1,0:T(8,128)(2,1)S(1)} collective-permute-done((bf16[7,64,128]{2,1,0:T(8,128)(2,1)S(1)}, bf16[7,64,128]{2,1,0:T(8,128)(2,1)S(1)}, u32[]{:S(2)}, u32[]{:S(2)}) %collective-permute-start.17) | collective-permute-done | bytes 114720 | tf_op jit(solution)/shard_map/ppermute | solution.py:427
  47.2 0.0 collective-permute-done.18.refs_1_
  47.2 0.1 fusion.4
  47.2 1.8 %collective-permute-start.19 = (bf16[7,64,128]{2,1,0:T(8,128)(2,1)S(1)}, bf16[7,64,128]{2,1,0:T(8,128)(2,1)S(1)}, u32[]{:S(2)}, u32[]{:S(2)}) collective-permute-start(bf16[7,64,128]{2,1,0:T(8,128)(2,1)S(1)} %fusion.4), channel_id=1, source_target_pairs={{0,8},{8,0},{16,24},{24,16},{1,9},{9,1},{17,25},{25,17},{2,10},{10... | collective-permute-start | bytes 344072 | tf_op jit(solution)/shard_map/ppermute | solution.py:427
  49.0 1.5 %collective-permute-start.20 = (bf16[7,64,128]{2,1,0:T(8,128)(2,1)S(1)}, bf16[7,64,128]{2,1,0:T(8,128)(2,1)S(1)}, u32[]{:S(2)}, u32[]{:S(2)}) collective-permute-start(bf16[7,64,128]{2,1,0:T(8,128)(2,1)S(1)} %fusion.4), channel_id=1, source_target_pairs={{0,16},{8,24},{16,0},{24,8},{1,17},{9,25},{17,1},{25,9},{2,18},{10... | collective-permute-start | bytes 344072 | tf_op jit(solution)/shard_map/ppermute | solution.py:427
  50.5 1.2 %collective-permute-start.21 = (bf16[7,64,128]{2,1,0:T(8,128)(2,1)S(1)}, bf16[7,64,128]{2,1,0:T(8,128)(2,1)S(1)}, u32[]{:S(2)}, u32[]{:S(2)}) collective-permute-start(bf16[7,64,128]{2,1,0:T(8,128)(2,1)S(1)} %fusion.4), channel_id=1, source_target_pairs={{0,24},{8,16},{16,8},{24,0},{1,25},{9,17},{17,9},{25,1},{2,26},{10... | collective-permute-start | bytes 344072 | tf_op jit(solution)/shard_map/ppermute | solution.py:427
  51.7 1.5 %collective-permute-start.22 = (bf16[256,128]{1,0:T(8,128)(2,1)S(1)}, bf16[256,128]{1,0:T(8,128)(2,1)S(1)}, u32[]{:S(2)}, u32[]{:S(2)}) collective-permute-start(bf16[256,128]{1,0:T(8,128)(2,1)S(1)} %get-tuple-element.134), channel_id=1, source_target_pairs={{0,4},{2,6},{4,0},{6,2},{1,5},{3,7},{5,1},{7,3},{8,12},{10,14},{12... | collective-permute-start | bytes 196616 | tf_op jit(solution)/shard_map/ppermute | solution.py:427
  53.2 1.4 %collective-permute-start.23 = (bf16[256,128]{1,0:T(8,128)(2,1)S(1)}, bf16[256,128]{1,0:T(8,128)(2,1)S(1)}, u32[]{:S(2)}, u32[]{:S(2)}) collective-permute-start(bf16[256,128]{1,0:T(8,128)(2,1)S(1)} %get-tuple-element.133), channel_id=1, source_target_pairs={{0,6},{2,4},{4,2},{6,0},{1,7},{3,5},{5,3},{7,1},{8,14},{10,12},{12... | collective-permute-start | bytes 196616 | tf_op jit(solution)/shard_map/ppermute | solution.py:427
  54.6 1.7 %collective-permute-done.22.refs_2_ = bf16[256,128]{1,0:T(8,128)(2,1)S(1)} collective-permute-done((bf16[256,128]{1,0:T(8,128)(2,1)S(1)}, bf16[256,128]{1,0:T(8,128)(2,1)S(1)}, u32[]{:S(2)}, u32[]{:S(2)}) %collective-permute-start.22) | collective-permute-done | bytes 65568 | tf_op jit(solution)/shard_map/ppermute | solution.py:427
  56.3 2.1 %collective-permute-done.23.refs_3_ = bf16[256,128]{1,0:T(8,128)(2,1)S(1)} collective-permute-done((bf16[256,128]{1,0:T(8,128)(2,1)S(1)}, bf16[256,128]{1,0:T(8,128)(2,1)S(1)}, u32[]{:S(2)}, u32[]{:S(2)}) %collective-permute-start.23) | collective-permute-done | bytes 65568 | tf_op jit(solution)/shard_map/ppermute | solution.py:427
  58.4 0.0 collective-permute-done.19
  58.4 1.2 %collective-permute-done.20 = bf16[7,64,128]{2,1,0:T(8,128)(2,1)S(1)} collective-permute-done((bf16[7,64,128]{2,1,0:T(8,128)(2,1)S(1)}, bf16[7,64,128]{2,1,0:T(8,128)(2,1)S(1)}, u32[]{:S(2)}, u32[]{:S(2)}) %collective-permute-start.20) | collective-permute-done | bytes 114720 | tf_op jit(solution)/shard_map/ppermute | solution.py:427
  59.6 0.0 collective-permute-done.21
  59.6 0.1 add_multiply_fusion.mine
  59.7 0.1 collective-permute-start.24
  59.8 0.1 broadcast_in_dim.29.refs_4_
  59.9 1.1 %unpack.1 = f32[32,32,128]{2,1,0:T(8,128)} custom-call(s32[1]{0:T(128)} %bitcast.7.me, bf16[256,128]{1,0:T(8,128)(2,1)S(1)} %get-tuple-element.99.refs_0_, bf16[256,128]{1,0:T(8,128)(2,1)S(1)} %collective-permute-done.18.refs_1_, bf16[256,128]{1,0:T(8,128)(2,1)S(1)} %collective-permute-done.22.refs_2_, bf16[256,128]{1,0:T(8,128)(2,1)S(1)} %collective-permute-done.23.refs_3_, ...), custom_call_target="tpu_custom_call" | custom-call | flops 268435456 | bytes 1048576 | tf_op jit(solution)/shard_map/unpack/pallas_call | solution.py:61
  61.0 0.3 collective-permute-done.24.other
  61.3 1.7 %finish.1 = (f32[27,32,64]{2,1,0:T(8,128)}, f32[1,32]{1,0:T(1,128)}, f32[27,32,64]{2,1,0:T(8,128)}, f32[1,64]{1,0:T(1,128)}) custom-call(s32[3]{0:T(128)S(1)} %pad_add_fusion.place, f32[7,64,128]{2,1,0:T(8,128)S(1)} %add_multiply_fusion.mine, f32[7,64,128]{2,1,0:T(8,128)S(1)} %collective-permute-done.24.other), custom_call_target="tpu_custom_call" | custom-call | flops 1048576 | bytes 1048576 | tf_op jit(solution)/shard_map/finish/pallas_call | solution.py:61
  (46 shorter events, 0.5 us)
Async XLA Ops:
  0.6 1.0 %copy-start = (bf16[1,32,2,16,256]{4,3,2,1,0:T(8,128)(2,1)S(1)}, bf16[1,32,2,16,256]{4,3,2,1,0:T(8,128)(2,1)}, u32[]{:S(2)}) copy-start(bf16[1,32,2,16,256]{4,3,2,1,0:T(8,128)(2,1)} %param.6) | copy-start | bytes 1572868
  1.7 4.0 %copy-start.1 = (bf16[1,32,1,32,128]{4,3,2,1,0:T(8,128)(2,1)S(1)}, bf16[1,32,1,32,128]{4,3,2,1,0:T(8,128)(2,1)}, u32[]{:S(2)}) copy-start(bf16[1,32,1,32,128]{4,3,2,1,0:T(8,128)(2,1)} %param.11) | copy-start | bytes 786436
  1.7 4.0 %copy-start.2 = (bf16[32,64,3,3,3]{1,0,4,3,2:T(8,128)(2,1)S(1)}, bf16[32,64,3,3,3]{1,0,4,3,2:T(8,128)(2,1)}, u32[]{:S(2)}) copy-start(bf16[32,64,3,3,3]{1,0,4,3,2:T(8,128)(2,1)} %param.9) | copy-start | bytes 331780
  2.7 8.7 %collective-permute-start = (bf16[2,1,32,256]{3,2,1,0:T(8,128)(2,1)S(1)}, bf16[2,1,32,256]{3,2,1,0:T(8,128)(2,1)S(1)}, u32[]{:S(2)}, u32[]{:S(2)}) collective-permute-start(bf16[2,1,32,256]{3,2,1,0:T(8,128)(2,1)S(1)} %get-tuple-element.122), channel_id=1, source_target_pairs={{0,2},{2,0},{4,6},{6,4},{1,3},{3,1},{5,7},{7,5},{8,10},{10,8},{12,... | collective-permute-start | bytes 98312 | tf_op jit(solution)/shard_map/ppermute | solution.py:409
  5.7 5.7 %collective-permute-start.1 = (bf16[2,1,32,256]{3,2,1,0:T(8,128)(2,1)S(1)}, bf16[2,1,32,256]{3,2,1,0:T(8,128)(2,1)S(1)}, u32[]{:S(2)}, u32[]{:S(2)}) collective-permute-start(bf16[2,1,32,256]{3,2,1,0:T(8,128)(2,1)S(1)} %get-tuple-element.121), channel_id=1, source_target_pairs={{0,1},{1,0},{2,4},{3,5},{4,2},{5,3},{6,7},{7,6},{8,9},{9,8},{10,12... | collective-permute-start | bytes 98312 | tf_op jit(solution)/shard_map/ppermute | solution.py:422
  5.7 5.2 %copy-start.3 = (bf16[64,32,3,3,3]{0,1,4,3,2:T(8,128)(2,1)S(1)}, bf16[64,32,3,3,3]{0,1,4,3,2:T(8,128)(2,1)}, u32[]{:S(2)}) copy-start(bf16[64,32,3,3,3]{0,1,4,3,2:T(8,128)(2,1)} %param.7) | copy-start | bytes 331780
  5.7 5.5 %copy-start.4 = (f32[64]{0:T(128)S(1)}, f32[64]{0:T(128)}, u32[]{:S(2)}) copy-start(f32[64]{0:T(128)} %param.8) | copy-start | bytes 772
  6.3 8.5 %collective-permute-start.4 = (bf16[17,32,128]{2,1,0:T(8,128)(2,1)S(1)}, bf16[17,32,128]{2,1,0:T(8,128)(2,1)S(1)}, u32[]{:S(2)}, u32[]{:S(2)}) collective-permute-start(bf16[17,32,128]{2,1,0:T(8,128)(2,1)S(1)} %get-tuple-element.144), channel_id=1, source_target_pairs={{0,2},{2,0},{4,6},{6,4},{1,3},{3,1},{5,7},{7,5},{8,10},{10,8},{12,... | collective-permute-start | bytes 417800 | tf_op jit(solution)/shard_map/ppermute | solution.py:427
  9.4 7.6 %collective-permute-start.5 = (bf16[17,32,128]{2,1,0:T(8,128)(2,1)S(1)}, bf16[17,32,128]{2,1,0:T(8,128)(2,1)S(1)}, u32[]{:S(2)}, u32[]{:S(2)}) collective-permute-start(bf16[17,32,128]{2,1,0:T(8,128)(2,1)S(1)} %get-tuple-element.143), channel_id=1, source_target_pairs={{0,4},{2,6},{4,0},{6,2},{1,5},{3,7},{5,1},{7,3},{8,12},{10,14},{12... | collective-permute-start | bytes 417800 | tf_op jit(solution)/shard_map/ppermute | solution.py:427
  9.4 7.6 %collective-permute-start.6 = (bf16[17,32,128]{2,1,0:T(8,128)(2,1)S(1)}, bf16[17,32,128]{2,1,0:T(8,128)(2,1)S(1)}, u32[]{:S(2)}, u32[]{:S(2)}) collective-permute-start(bf16[17,32,128]{2,1,0:T(8,128)(2,1)S(1)} %get-tuple-element.142), channel_id=1, source_target_pairs={{0,6},{2,4},{4,2},{6,0},{1,7},{3,5},{5,3},{7,1},{8,14},{10,12},{12... | collective-permute-start | bytes 417800 | tf_op jit(solution)/shard_map/ppermute | solution.py:427
  11.5 8.6 %collective-permute-start.2 = (bf16[18,32,256]{2,1,0:T(8,128)(2,1)S(1)}, bf16[18,32,256]{2,1,0:T(8,128)(2,1)S(1)}, u32[]{:S(2)}, u32[]{:S(2)}) collective-permute-start(bf16[18,32,256]{2,1,0:T(8,128)(2,1)S(1)} %get-tuple-element.120), channel_id=1, source_target_pairs={{0,8},{8,0},{16,24},{24,16},{1,9},{9,1},{17,25},{25,17},{2,10},{10... | collective-permute-start | bytes 884744 | tf_op jit(solution)/shard_map/ppermute | solution.py:409
  13.1 7.0 %collective-permute-start.3 = (bf16[18,32,256]{2,1,0:T(8,128)(2,1)S(1)}, bf16[18,32,256]{2,1,0:T(8,128)(2,1)S(1)}, u32[]{:S(2)}, u32[]{:S(2)}) collective-permute-start(bf16[18,32,256]{2,1,0:T(8,128)(2,1)S(1)} %get-tuple-element.119), channel_id=1, source_target_pairs={{0,1},{1,0},{8,16},{9,17},{16,8},{17,9},{24,25},{25,24},{2,3},{3,2... | collective-permute-start | bytes 884744 | tf_op jit(solution)/shard_map/ppermute | solution.py:422
  17.0 12.0 %collective-permute-start.8 = (bf16[4,10,32,128]{3,2,1,0:T(8,128)(2,1)S(1)}, bf16[4,10,32,128]{3,2,1,0:T(8,128)(2,1)S(1)}, u32[]{:S(2)}, u32[]{:S(2)}) collective-permute-start(bf16[4,10,32,128]{3,2,1,0:T(8,128)(2,1)S(1)} %pad_maximum_fusion.1.co), channel_id=1, source_target_pairs={{0,8},{8,0},{16,24},{24,16},{1,9},{9,1},{17,25},{25,17},{2,10},{10... | collective-permute-start | bytes 983048 | tf_op jit(solution)/shard_map/ppermute | solution.py:409
  18.6 10.3 %collective-permute-start.9 = (bf16[4,10,32,128]{3,2,1,0:T(8,128)(2,1)S(1)}, bf16[4,10,32,128]{3,2,1,0:T(8,128)(2,1)S(1)}, u32[]{:S(2)}, u32[]{:S(2)}) collective-permute-start(bf16[4,10,32,128]{3,2,1,0:T(8,128)(2,1)S(1)} %pad_maximum_fusion.1.co), channel_id=1, source_target_pairs={{0,1},{1,0},{8,16},{9,17},{16,8},{17,9},{24,25},{25,24},{2,3},{3,2... | collective-permute-start | bytes 983048 | tf_op jit(solution)/shard_map/ppermute | solution.py:422
  18.7 3.1 %collective-permute-start.7 = (bf16[3,7,32,128]{3,2,1,0:T(8,128)(2,1)S(1)}, bf16[3,7,32,128]{3,2,1,0:T(8,128)(2,1)S(1)}, u32[]{:S(2)}, u32[]{:S(2)}) collective-permute-start(bf16[3,7,32,128]{3,2,1,0:T(8,128)(2,1)S(1)} %pad_maximum_fusion.5), channel_id=1, source_target_pairs={{0,1},{1,0},{2,3},{3,2},{4,5},{5,4},{6,7},{7,6},{8,9},{9,8},{10,11... | collective-permute-start | bytes 516104 | tf_op jit(solution)/shard_map/ppermute | solution.py:409
  21.8 3.8 %collective-permute-start.10 = (bf16[64,128]{1,0:T(8,128)(2,1)S(1)}, bf16[64,128]{1,0:T(8,128)(2,1)S(1)}, u32[]{:S(2)}, u32[]{:S(2)}) collective-permute-start(bf16[64,128]{1,0:T(8,128)(2,1)S(1)} %get-tuple-element.137), channel_id=1, source_target_pairs={{0,2},{2,0},{4,6},{6,4},{1,3},{3,1},{5,7},{7,5},{8,10},{10,8},{12,... | collective-permute-start | bytes 49160 | tf_op jit(solution)/shard_map/ppermute | solution.py:409
  23.4 2.2 %collective-permute-start.11 = (bf16[64,128]{1,0:T(8,128)(2,1)S(1)}, bf16[64,128]{1,0:T(8,128)(2,1)S(1)}, u32[]{:S(2)}, u32[]{:S(2)}) collective-permute-start(bf16[64,128]{1,0:T(8,128)(2,1)S(1)} %get-tuple-element.136), channel_id=1, source_target_pairs={{0,1},{1,0},{2,4},{3,5},{4,2},{5,3},{6,7},{7,6},{8,9},{9,8},{10,12... | collective-permute-start | bytes 49160 | tf_op jit(solution)/shard_map/ppermute | solution.py:422
  25.6 8.5 %collective-permute-start.12 = (bf16[10,64,128]{2,1,0:T(8,128)(2,1)S(1)}, bf16[10,64,128]{2,1,0:T(8,128)(2,1)S(1)}, u32[]{:S(2)}, u32[]{:S(2)}) collective-permute-start(bf16[10,64,128]{2,1,0:T(8,128)(2,1)S(1)} %pad_maximum_fusion.6.ur), channel_id=1, source_target_pairs={{0,8},{8,0},{16,24},{24,16},{1,9},{9,1},{17,25},{25,17},{2,10},{10... | collective-permute-start | bytes 491528 | tf_op jit(solution)/shard_map/ppermute | solution.py:409
  29.0 5.2 %collective-permute-start.13 = (bf16[10,64,128]{2,1,0:T(8,128)(2,1)S(1)}, bf16[10,64,128]{2,1,0:T(8,128)(2,1)S(1)}, u32[]{:S(2)}, u32[]{:S(2)}) collective-permute-start(bf16[10,64,128]{2,1,0:T(8,128)(2,1)S(1)} %pad_maximum_fusion.6.ur), channel_id=1, source_target_pairs={{0,1},{1,0},{8,16},{9,17},{16,8},{17,9},{24,25},{25,24},{2,3},{3,2... | collective-permute-start | bytes 491528 | tf_op jit(solution)/shard_map/ppermute | solution.py:422
  34.2 1.8 %collective-permute-start.14 = (bf16[7,160,128]{2,1,0:T(8,128)(2,1)S(1)}, bf16[7,160,128]{2,1,0:T(8,128)(2,1)S(1)}, u32[]{:S(2)}, u32[]{:S(2)}) collective-permute-start(bf16[7,160,128]{2,1,0:T(8,128)(2,1)S(1)} %get-tuple-element.83), channel_id=1, source_target_pairs={{0,1},{1,0},{2,3},{3,2},{4,5},{5,4},{6,7},{7,6},{8,9},{9,8},{10,11... | collective-permute-start | bytes 860168 | tf_op jit(solution)/shard_map/ppermute | solution.py:409
  36.1 8.1 %collective-permute-start.15 = (bf16[7,64,128]{2,1,0:T(8,128)(2,1)S(1)}, bf16[7,64,128]{2,1,0:T(8,128)(2,1)S(1)}, u32[]{:S(2)}, u32[]{:S(2)}) collective-permute-start(bf16[7,64,128]{2,1,0:T(8,128)(2,1)S(1)} %get-tuple-element.141), channel_id=1, source_target_pairs={{0,2},{2,0},{4,6},{6,4},{1,3},{3,1},{5,7},{7,5},{8,10},{10,8},{12,... | collective-permute-start | bytes 344072 | tf_op jit(solution)/shard_map/ppermute | solution.py:427
  39.1 7.2 %collective-permute-start.16 = (bf16[7,64,128]{2,1,0:T(8,128)(2,1)S(1)}, bf16[7,64,128]{2,1,0:T(8,128)(2,1)S(1)}, u32[]{:S(2)}, u32[]{:S(2)}) collective-permute-start(bf16[7,64,128]{2,1,0:T(8,128)(2,1)S(1)} %get-tuple-element.140), channel_id=1, source_target_pairs={{0,4},{2,6},{4,0},{6,2},{1,5},{3,7},{5,1},{7,3},{8,12},{10,14},{12... | collective-permute-start | bytes 344072 | tf_op jit(solution)/shard_map/ppermute | solution.py:427
  39.3 7.8 %collective-permute-start.17 = (bf16[7,64,128]{2,1,0:T(8,128)(2,1)S(1)}, bf16[7,64,128]{2,1,0:T(8,128)(2,1)S(1)}, u32[]{:S(2)}, u32[]{:S(2)}) collective-permute-start(bf16[7,64,128]{2,1,0:T(8,128)(2,1)S(1)} %concatenate.48), channel_id=1, source_target_pairs={{0,6},{2,4},{4,2},{6,0},{1,7},{3,5},{5,3},{7,1},{8,14},{10,12},{12... | collective-permute-start | bytes 344072 | tf_op jit(solution)/shard_map/ppermute | solution.py:427
  42.3 17.5 %copy-start.5 = (f32[32]{0:T(128)S(1)}, f32[32]{0:T(128)}, u32[]{:S(2)}) copy-start(f32[32]{0:T(128)} %param.10) | copy-start | bytes 388
  42.3 4.9 %collective-permute-start.18 = (bf16[256,128]{1,0:T(8,128)(2,1)S(1)}, bf16[256,128]{1,0:T(8,128)(2,1)S(1)}, u32[]{:S(2)}, u32[]{:S(2)}) collective-permute-start(bf16[256,128]{1,0:T(8,128)(2,1)S(1)} %bitcast.70), channel_id=1, source_target_pairs={{0,2},{2,0},{4,6},{6,4},{1,3},{3,1},{5,7},{7,5},{8,10},{10,8},{12,... | collective-permute-start | bytes 196616 | tf_op jit(solution)/shard_map/ppermute | solution.py:427
  47.2 11.2 %collective-permute-start.19 = (bf16[7,64,128]{2,1,0:T(8,128)(2,1)S(1)}, bf16[7,64,128]{2,1,0:T(8,128)(2,1)S(1)}, u32[]{:S(2)}, u32[]{:S(2)}) collective-permute-start(bf16[7,64,128]{2,1,0:T(8,128)(2,1)S(1)} %fusion.4), channel_id=1, source_target_pairs={{0,8},{8,0},{16,24},{24,16},{1,9},{9,1},{17,25},{25,17},{2,10},{10... | collective-permute-start | bytes 344072 | tf_op jit(solution)/shard_map/ppermute | solution.py:427
  49.0 10.6 %collective-permute-start.20 = (bf16[7,64,128]{2,1,0:T(8,128)(2,1)S(1)}, bf16[7,64,128]{2,1,0:T(8,128)(2,1)S(1)}, u32[]{:S(2)}, u32[]{:S(2)}) collective-permute-start(bf16[7,64,128]{2,1,0:T(8,128)(2,1)S(1)} %fusion.4), channel_id=1, source_target_pairs={{0,16},{8,24},{16,0},{24,8},{1,17},{9,25},{17,1},{25,9},{2,18},{10... | collective-permute-start | bytes 344072 | tf_op jit(solution)/shard_map/ppermute | solution.py:427
  50.5 9.1 %collective-permute-start.21 = (bf16[7,64,128]{2,1,0:T(8,128)(2,1)S(1)}, bf16[7,64,128]{2,1,0:T(8,128)(2,1)S(1)}, u32[]{:S(2)}, u32[]{:S(2)}) collective-permute-start(bf16[7,64,128]{2,1,0:T(8,128)(2,1)S(1)} %fusion.4), channel_id=1, source_target_pairs={{0,24},{8,16},{16,8},{24,0},{1,25},{9,17},{17,9},{25,1},{2,26},{10... | collective-permute-start | bytes 344072 | tf_op jit(solution)/shard_map/ppermute | solution.py:427
  51.7 4.5 %collective-permute-start.22 = (bf16[256,128]{1,0:T(8,128)(2,1)S(1)}, bf16[256,128]{1,0:T(8,128)(2,1)S(1)}, u32[]{:S(2)}, u32[]{:S(2)}) collective-permute-start(bf16[256,128]{1,0:T(8,128)(2,1)S(1)} %get-tuple-element.134), channel_id=1, source_target_pairs={{0,4},{2,6},{4,0},{6,2},{1,5},{3,7},{5,1},{7,3},{8,12},{10,14},{12... | collective-permute-start | bytes 196616 | tf_op jit(solution)/shard_map/ppermute | solution.py:427
  53.2 5.2 %collective-permute-start.23 = (bf16[256,128]{1,0:T(8,128)(2,1)S(1)}, bf16[256,128]{1,0:T(8,128)(2,1)S(1)}, u32[]{:S(2)}, u32[]{:S(2)}) collective-permute-start(bf16[256,128]{1,0:T(8,128)(2,1)S(1)} %get-tuple-element.133), channel_id=1, source_target_pairs={{0,6},{2,4},{4,2},{6,0},{1,7},{3,5},{5,3},{7,1},{8,14},{10,12},{12... | collective-permute-start | bytes 196616 | tf_op jit(solution)/shard_map/ppermute | solution.py:427
  59.7 1.6 %collective-permute-start.24 = (f32[7,64,128]{2,1,0:T(8,128)S(1)}, f32[7,64,128]{2,1,0:T(8,128)S(1)}, u32[]{:S(2)}, u32[]{:S(2)}) collective-permute-start(f32[7,64,128]{2,1,0:T(8,128)S(1)} %add_multiply_fusion.mine), channel_id=1, source_target_pairs={{0,1},{1,0},{2,3},{3,2},{4,5},{5,4},{6,7},{7,6},{8,9},{9,8},{10,11... | collective-permute-start | bytes 688136 | tf_op jit(solution)/shard_map/ppermute | solution.py:409
